TPU v7x, 512 devices: a whole 4x4x16 slice. The times are simulated.
512 devices in a mesh: img: 32 (over z, y_hi), txt: 16 (over y_lo, x, core).
Axes of the slice: x: 4, y: 4 (y_hi: 2, y_lo: 2; y = y_hi * 2 + y_lo), z: 16, core: 2. Of those that a mesh axis runs over, the one named last changes fastest.
Arguments:
- picture_tiles: bfloat16 [16384, 32, 1152], P(('img', 'txt')), may hold values from -19 to 19
- query_key_product: bfloat16 [1152, 16], replicated, may hold values from -0.1355288 to 0.1355288
- pooling_exit_matrix: bfloat16 [1152, 1152], P(None, 'txt'), may hold values from -0.179722974 to 0.179722974
- caption_embedding: bfloat16 [16384, 1152], P(('txt', 'img')), may hold values from -11 to 11
- caption_head_matrix: bfloat16 [1152, 1152], P(None, 'txt'), may hold values from -0.179722974 to 0.179722974
- matching_caption_index: int32 [16384], P(('img', 'txt')), may hold values from 0 to 16383, as said below
- natural_inverse_coolness: float32 [1], replicated, may hold values from 2 to 2.5
- score_offset: float32 [1], replicated, may hold values from -6 to -2
- objective_adjoint: float32 [1], replicated, may hold values from 20 to 60
Outputs:
- d_patches: bfloat16 [16384, 32, 1152], P(('img', 'txt'))
- d_text: bfloat16 [16384, 1152], P(('txt', 'img'))
Inputs may be any that keep to these rules, and one draw needn't show every extreme that they name: `matching_caption_index`: each text is the matching text of exactly one image.
All inputs are finite; a program needn't handle non-finite values.
Results may differ from a plain program's by a relative error of at most 0.024.
Values may be sent and summed in bfloat16 or wider, within the bound.
No kernel may reach another device: no remote copies, remote signals or barrier semaphores. Data moves between devices by JAX's collectives and lax.ppermute only.
A program may use at most 64 MiB of HBM per device.

v0:
```python
import jax
import jax.numpy as jnp
from jax import lax
from jax.sharding import PartitionSpec as P

EPSILON = 1e-06


def inverse_norm(pre_rows):
    return lax.rsqrt(jnp.sum(pre_rows * pre_rows, axis=-1, keepdims=True) + EPSILON)


def norm_backward(pre_rows, inverse, upstream):
    along = jnp.sum(pre_rows * upstream, axis=-1, keepdims=True)
    return (inverse * upstream - inverse**3 * pre_rows * along).astype(jnp.bfloat16)


def scale_match_couples(couple_scores, match_polarity, score_coolness, incoming_adjoint):
    score_derivative = (
        -incoming_adjoint * match_polarity * jax.nn.sigmoid(-match_polarity * couple_scores)
    )
    return (score_coolness * score_derivative).astype(jnp.bfloat16)


def shards(
    picture_tiles,
    query_key_product,
    pooling_exit_matrix,
    caption_embedding,
    caption_head_matrix,
    matching_caption_index,
    natural_inverse_coolness,
    score_offset,
    objective_adjoint,
):
    images, patch_count, model_width = picture_tiles.shape
    head_count = query_key_product.shape[1]
    head_width = model_width // head_count
    scores = jnp.einsum(
        "bpd,dh->bhp", picture_tiles, query_key_product, preferred_element_type=jnp.float32
    )
    attend = jax.nn.softmax(scores, axis=-1)
    attend_low = attend.astype(jnp.bfloat16)
    per_head = picture_tiles.reshape(images, patch_count, head_count, head_width)
    pooled = jnp.einsum("bhp,bphc->bhc", attend_low, per_head, preferred_element_type=jnp.float32)
    pooled = pooled.reshape(images, model_width).astype(jnp.bfloat16)
    full_out, full_text = (
        lax.all_gather(pooling_exit_matrix, "txt", axis=1, tiled=True),
        lax.all_gather(caption_head_matrix, "txt", axis=1, tiled=True),
    )
    image_pre = jnp.dot(pooled, full_out, preferred_element_type=jnp.float32)
    text_pre = jnp.dot(caption_embedding, full_text, preferred_element_type=jnp.float32)
    image_inv = inverse_norm(image_pre)
    text_inv = inverse_norm(text_pre)
    image_unit = (image_pre * image_inv).astype(jnp.bfloat16)
    text_unit = (text_pre * text_inv).astype(jnp.bfloat16)
    image_rows, positives = (
        lax.all_gather(image_unit, "txt", axis=0, tiled=True),
        lax.all_gather(matching_caption_index, "txt", axis=0, tiled=True),
    )
    score_coolness = jnp.exp(natural_inverse_coolness[0])
    offset = score_offset[0]
    incoming_adjoint = objective_adjoint[0]
    text_rows = lax.all_gather(text_unit, "img", axis=0, tiled=True)
    text_count = text_rows.shape[0]
    columns = lax.axis_index("txt") * text_count + lax.iota(jnp.int32, text_count)
    couple_scores = (
        score_coolness
        * lax.dot_general(
            image_rows, text_rows, (((1,), (1,)), ((), ())), preferred_element_type=jnp.float32
        )
        + offset
    )
    match_polarity = jnp.where(positives[:, None] == columns[None, :], 1.0, -1.0).astype(
        jnp.float32
    )
    scaled_couples = scale_match_couples(
        couple_scores, match_polarity, score_coolness, incoming_adjoint
    )
    text_grad = lax.psum_scatter(
        lax.dot_general(
            scaled_couples, image_rows, (((0,), (0,)), ((), ())), preferred_element_type=jnp.float32
        ).astype(jnp.bfloat16),
        "img",
        scatter_dimension=0,
        tiled=True,
    ).astype(jnp.float32)
    image_grad = lax.psum_scatter(
        jnp.dot(scaled_couples, text_rows, preferred_element_type=jnp.float32).astype(jnp.bfloat16),
        "txt",
        scatter_dimension=0,
        tiled=True,
    ).astype(jnp.float32)
    image_dpre = norm_backward(image_pre, image_inv, image_grad)
    text_dpre = norm_backward(text_pre, text_inv, text_grad)
    dpooled = jnp.dot(image_dpre, full_out.T, preferred_element_type=jnp.float32)
    text_back = jnp.dot(text_dpre, full_text.T, preferred_element_type=jnp.float32)
    d_text = text_back.astype(jnp.bfloat16)
    dpooled_low = dpooled.astype(jnp.bfloat16).reshape(images, head_count, head_width)
    dattend = jnp.einsum("bhc,bphc->bhp", dpooled_low, per_head, preferred_element_type=jnp.float32)
    dscores = attend * (dattend - jnp.sum(attend * dattend, axis=-1, keepdims=True))
    dscores_low = dscores.astype(jnp.bfloat16)
    direct = jnp.einsum(
        "bhp,bhc->bphc", attend_low, dpooled_low, preferred_element_type=jnp.float32
    )
    through = jnp.einsum(
        "bhp,dh->bpd", dscores_low, query_key_product, preferred_element_type=jnp.float32
    )
    d_patches = (direct.reshape(images, patch_count, model_width) + through).astype(jnp.bfloat16)
    return (d_patches, d_text)


def solution(mesh):
    return jax.shard_map(
        shards,
        mesh=mesh,
        in_specs=(
            P(("img", "txt"), None, None),
            P(),
            P(None, "txt"),
            P(("txt", "img"), None),
            P(None, "txt"),
            P(("img", "txt")),
            P(),
            P(),
            P(),
        ),
        out_specs=(P(("img", "txt"), None, None), P(("txt", "img"), None)),
        check_vma=False,
    )
```

profile of v0, /device:TPU:6, one launch (start us, length us, event | category | flops | bytes accessed | tf_op | source)
XLA Modules:
  0.0 1056.6 jit_solution(4419882422208231097)
XLA Ops:
  7.2 0.0 all-gather.5.cloned.1.call-start
  7.2 0.7 all-gather.5.cloned.1.call-update
  7.9 0.0 all-gather.9.cloned.1.call-start
  8.0 0.7 all-gather.9.cloned.1.call-update
  8.7 0.0 all-gather.7.cloned.1.call-start
  8.7 9.8 reshape.51
  18.5 1.8 convolution_bitcast_fusion
  20.3 5.3 fusion.34
  25.6 0.6 copy-done.6
  26.2 0.1 convert_bitcast_fusion
  26.4 3.4 fusion.4
  29.8 0.2 convert_element_type.50
  30.0 26.6 %all-gather.5.cloned.1.call-done = bf16[1152,1152]{0,1:T(8,128)(2,1)} async-done(((bf16[1152,72]{0,1:T(8,128)(2,1)}), bf16[1152,1152]{0,1:T(8,128)(2,1)}) %all-gather.5.cloned.1.call-update) | async-done | bytes 2654224 | tf_op jit(solution)/shard_map/all_gather | solution.py:48
  56.6 2.8 multiply_reduce_fusion.2
  59.3 0.5 multiply_multiply_fusion.1
  59.9 0.7 multiply_convert_fusion.2
  60.6 0.0 all-gather.7.cloned.1.call-update
  60.6 0.0 all-gather.11.cloned.1.call-start
  60.7 40.7 %all-gather.9.cloned.1.call-done = bf16[1152,1152]{0,1:T(8,128)(2,1)} async-done(((bf16[1152,72]{0,1:T(8,128)(2,1)}), bf16[1152,1152]{0,1:T(8,128)(2,1)}) %all-gather.9.cloned.1.call-update) | async-done | bytes 2654224 | tf_op jit(solution)/shard_map/all_gather | solution.py:49
  101.4 2.8 multiply_reduce_fusion.1
  104.1 0.6 multiply_multiply_fusion
  104.7 0.7 multiply_convert_fusion.1
  105.4 0.0 all-gather.11.cloned.1.call-update
  105.5 0.0 reduce-scatter.3.cloned.1.call-start
  107.5 1.3 dynamic-slice
  109.4 0.2 dynamic-update-slice
  109.6 10.6 %all-reduce = s32[512]{0:T(512)S(1)} all-reduce(s32[512]{0:T(512)S(1)} %dynamic-update-slice), channel_id=1, replica_groups=mesh['img'=32,'txt'=16] {'txt'}, use_global_device_ids=true, to_apply=%add | all-reduce | flops 512 | bytes 4096
  120.2 24.2 %all-gather.7.cloned.1.call-done = bf16[512,1152]{1,0:T(8,128)(2,1)} async-done(((bf16[32,1152]{1,0:T(8,128)(2,1)}), bf16[512,1152]{1,0:T(8,128)(2,1)}) %all-gather.7.cloned.1.call-update) | async-done | bytes 1179664 | tf_op jit(solution)/shard_map/all_gather | solution.py:58
  144.4 156.7 %all-gather.11.cloned.1.call-done = bf16[1024,1152]{1,0:T(8,128)(2,1)} async-done(((bf16[32,1152]{1,0:T(8,128)(2,1)}), bf16[1024,1152]{1,0:T(8,128)(2,1)}) %all-gather.11.cloned.1.call-update) | async-done | bytes 2359312 | tf_op jit(solution)/shard_map/all_gather | solution.py:64
  301.1 4.3 fusion.8
  305.4 1.0 copy-done.15
  306.4 2.5 convolution_convert_fusion.1
  309.0 0.2 reduce-scatter.5.cloned.1.call-start
  309.2 4.7 convolution_convert_fusion
  313.9 55.2 %reduce-scatter.3.cloned.1.call-done = bf16[32,1152]{1,0:T(8,128)(2,1)} async-done(((bf16[512,1152]{1,0:T(8,128)(2,1)}), bf16[32,1152]{1,0:T(8,128)(2,1)}) %reduce-scatter.3.cloned.1.call-update) | async-done | bytes 73744 | tf_op jit(solution)/shard_map/reduce_scatter | solution.py:88
  369.1 1.0 fusion.19
  370.1 2.1 convolution_convert_fusion.3
  372.3 1.1 reshape.52
  373.4 1.3 reshape.65
  374.7 4.5 fusion.2
  379.2 0.9 multiply_reduce_fusion
  380.1 0.2 copy.11
  380.3 4.6 multiply_bitcast_fusion
  384.9 8.5 reshape.53
  393.4 5.7 fusion.1
  399.0 647.6 %reduce-scatter.5.cloned.1.call-done = bf16[32,1152]{1,0:T(8,128)(2,1)} async-done(((bf16[1024,1152]{1,0:T(8,128)(2,1)}), bf16[32,1152]{1,0:T(8,128)(2,1)}) %reduce-scatter.5.cloned.1.call-update) | async-done | bytes 73744 | tf_op jit(solution)/shard_map/reduce_scatter | solution.py:80
  1046.6 1.0 fusion.22
  1047.6 2.1 convolution_convert_fusion.2
  (36 shorter events, 0.1 us)
Async XLA Ops:
  7.2 94.2 %copy-start = (bf16[32,1152]{1,0:T(8,128)(2,1)S(1)}, bf16[32,1152]{1,0:T(8,128)(2,1)}, u32[]{:S(2)}) copy-start(bf16[32,1152]{1,0:T(8,128)(2,1)} %param.12) | copy-start | bytes 221188
  7.2 49.4 %all-gather.5.cloned.1.call-start = ((), (), s32[]{:S(2)}) async-start(), calls=%async_computation.2 | async-start | bytes 2820096 | tf_op jit(solution)/shard_map/all_gather | solution.py:48
  7.9 93.5 %all-gather.9.cloned.1.call-start = ((), (), s32[]{:S(2)}) async-start(), calls=%async_computation.4 | async-start | bytes 2820096 | tf_op jit(solution)/shard_map/all_gather | solution.py:49
  8.7 9.8 copy-start.3
  8.7 9.8 copy-start.9
  8.7 135.7 %all-gather.7.cloned.1.call-start = ((), (), s32[]{:S(2)}) async-start(), calls=%async_computation.3 | async-start | bytes 1253376 | tf_op jit(solution)/shard_map/all_gather | solution.py:58
  25.6 0.6 copy-start.6
  59.3 50.0 %copy-start.14 = (s32[32]{0:T(128)S(1)}, s32[32]{0:T(128)}, u32[]{:S(2)}) copy-start(s32[32]{0:T(128)} %param.14) | copy-start | bytes 388
  60.6 240.5 %all-gather.11.cloned.1.call-start = ((), (), s32[]{:S(2)}) async-start(), calls=%async_computation.5 | async-start | bytes 2433024 | tf_op jit(solution)/shard_map/all_gather | solution.py:64
  105.5 263.6 %reduce-scatter.3.cloned.1.call-start = ((), (), s32[]{:S(2)}) async-start(), calls=%async_computation.6 | async-start | bytes 1253376 | tf_op jit(solution)/shard_map/reduce_scatter | solution.py:88
  301.1 5.3 copy-start.13
  305.4 1.0 copy-start.15
  309.0 737.7 %reduce-scatter.5.cloned.1.call-start = ((), (), s32[]{:S(2)}) async-start(), calls=%async_computation.7 | async-start | bytes 2433024 | tf_op jit(solution)/shard_map/reduce_scatter | solution.py:80
  309.2 60.9 %copy-start.2 = (bf16[1152,1152]{0,1:T(8,128)(2,1)S(1)}, bf16[1152,1152]{0,1:T(8,128)(2,1)}, u32[]{:S(2)}) copy-start(bf16[1152,1152]{0,1:T(8,128)(2,1)} %all-gather.5.cloned.1.call-done) | copy-start | bytes 7962628
  374.7 4.5 copy-start.7
  379.2 0.9 copy-start.4
  384.8 8.5 copy-start.5
  384.8 8.5 copy-start.8
  384.9 8.5 copy-start.10
  384.9 8.5 copy-start.11
  393.4 654.3 %copy-start.1 = (bf16[1152,1152]{0,1:T(8,128)(2,1)S(1)}, bf16[1152,1152]{0,1:T(8,128)(2,1)}, u32[]{:S(2)}) copy-start(bf16[1152,1152]{0,1:T(8,128)(2,1)} %all-gather.9.cloned.1.call-done) | copy-start | bytes 7962628
  393.4 654.3 %copy-start.12 = (f32[32]{0:T(128)S(1)}, f32[32]{0:T(128)}, u32[]{:S(2)}) copy-start(f32[32]{0:T(128)} %get-tuple-element.4) | copy-start | bytes 388
Sparse Core Ops, SparseCore 0:
  10.2 46.3 all-gather.4
  58.7 42.6 all-gather.8
  104.1 40.2 all-gather.6
  147.9 153.1 all-gather.10
  309.1 59.9 reduce-scatter.2
  373.4 673.1 reduce-scatter.4
where the time goes:
time: 1060 us
  waiting for transfers between devices  952 us (90%)
  matrix products  36.6 us (3%)
  local copies, waits for them, and re-layouts  24.2 us (2%)
  between operations  16.9 us (2%)
  other arithmetic  15.5 us (1%)
  blocking collectives  10.6 us (1%)
    reduce_scatter x1, waiting for transfers between devices, shards(): lax.psum_scatter(lax.dot_general(scaled_couples, image_rows, (((0,), (0,)...  648 us
    all_gather x1, waiting for transfers between devices, shards(): text_rows = lax.all_gather(text_unit, 'img', axis=0, tiled=True)  157 us
    reduce_scatter x1, waiting for transfers between devices, shards(): lax.psum_scatter(jnp.dot(scaled_couples, text_rows, preferred_element_typ...  55.2 us
    all_gather x1, waiting for transfers between devices, shards(): lax.all_gather(caption_head_matrix, 'txt', axis=1, tiled=True)  40.7 us
    all_gather x1, waiting for transfers between devices, shards(): lax.all_gather(pooling_exit_matrix, 'txt', axis=1, tiled=True)  26.6 us
    all_gather x1, waiting for transfers between devices, shards(): lax.all_gather(image_unit, 'txt', axis=0, tiled=True)  24.2 us
  transfers between devices with their start and end apart: 6, of which 6 were waited for; matrix products, arithmetic and copies ran while one was open for 6% of the time, Pallas kernels for 0%

commit v1 on v0

v1 whole, which is shorter than its diff:
```python
import jax
import jax.numpy as jnp
from jax import lax
from jax.experimental import pallas as pl
from jax.experimental.pallas import tpu as pltpu
from jax.sharding import Mesh, PartitionSpec as P

EPSILON = 1e-06
INTERPRET = False
BF, F32 = jnp.bfloat16, jnp.float32
NZ, NYH, NYL, NX, NC = 16, 2, 2, 4, 2
Y = ("y_hi", "y_lo")
XY = ("y_hi", "y_lo", "x")
VMEM = pltpu.VMEM
SMEM = pltpu.SMEM
NEAR = (0, 3, -3, 6, -6)
TEXT_OFFSETS = NEAR + tuple(o + 1 for o in NEAR) + tuple(o - 1 for o in NEAR) + (8,)


def take_from(values, axis, distance, size):
    return lax.ppermute(values, axis, [((i + distance) % size, i) for i in range(size)])


def swap_cores(values):
    return lax.ppermute(values, "core", [(0, 1), (1, 0)])


def nt_dot(a, b):
    return lax.dot_general(a, b, (((1,), (1,)), ((), ())), preferred_element_type=F32)


def tn_dot(a, b):
    return lax.dot_general(a, b, (((0,), (0,)), ((), ())), preferred_element_type=F32)


def nn_dot(a, b):
    return jnp.dot(a, b, preferred_element_type=F32)


def call(kernel, out_shape, *, flops=0, transcendentals=0, moved=0, **kw):
    return pl.pallas_call(
        kernel,
        out_shape=out_shape,
        compiler_params=pltpu.CompilerParams(vmem_limit_bytes=40 * 1024 * 1024),
        cost_estimate=pl.CostEstimate(
            flops=flops, transcendentals=transcendentals, bytes_accessed=moved
        ),
        interpret=INTERPRET,
        **kw,
    )


def attention_forward(tiles, query_key, spread, patches):
    rows, width = tiles.shape
    heads = query_key.shape[1]
    images = rows // patches
    step = min(8, images)

    def kernel(tile_ref, qk_ref, spread_ref, attend_ref, pooled_ref):
        tile = tile_ref[...]
        scores = nn_dot(tile, qk_ref[...]).reshape(step, patches, heads)
        top = jnp.max(scores, axis=1, keepdims=True)
        raised = jnp.exp(scores - top)
        attend = raised / jnp.sum(raised, axis=1, keepdims=True)
        attend = attend.reshape(step * patches, heads)
        attend_ref[...] = attend
        wide = nn_dot(attend.astype(BF), spread_ref[...])
        mixed = (wide * tile.astype(F32)).reshape(step, patches, width)
        pooled_ref[...] = jnp.sum(mixed, axis=1)

    return call(
        kernel,
        (
            jax.ShapeDtypeStruct((rows, heads), F32),
            jax.ShapeDtypeStruct((images, width), F32),
        ),
        grid=(images // step,),
        in_specs=[
            pl.BlockSpec((step * patches, width), lambda i: (i, 0)),
            pl.BlockSpec((width, heads), lambda i: (0, 0)),
            pl.BlockSpec((heads, width), lambda i: (0, 0)),
        ],
        out_specs=[
            pl.BlockSpec((step * patches, heads), lambda i: (i, 0)),
            pl.BlockSpec((step, width), lambda i: (i, 0)),
        ],
        flops=4 * rows * width * 128,
        moved=rows * width * 2,
    )(tiles, query_key, spread)


def attention_backward(tiles, attend, dpooled, query_key_t, spread, gather, patches):
    rows, width = tiles.shape
    heads = attend.shape[1]
    images = rows // patches
    step = min(8, images)

    def kernel(tile_ref, attend_ref, dpooled_ref, qkt_ref, spread_ref, gather_ref, out_ref):
        block = step * patches
        upstream = dpooled_ref[...]
        upstream = jnp.broadcast_to(upstream[:, None, :], (step, patches, width))
        upstream = upstream.reshape(block, width)
        product = tile_ref[...].astype(F32) * upstream
        high = product.astype(BF)
        low = (product - high.astype(F32)).astype(BF)
        dattend = nn_dot(high, gather_ref[...]) + nn_dot(low, gather_ref[...])
        attend = attend_ref[...]
        weighted = (attend * dattend).reshape(step, patches, heads)
        mean = jnp.broadcast_to(
            jnp.sum(weighted, axis=1, keepdims=True), (step, patches, heads)
        ).reshape(block, heads)
        dscores = attend * (dattend - mean)
        direct = nn_dot(attend.astype(BF), spread_ref[...]) * upstream
        through = nn_dot(dscores.astype(BF), qkt_ref[...])
        out_ref[...] = (direct + through).astype(BF)

    return call(
        kernel,
        jax.ShapeDtypeStruct((rows, width), BF),
        grid=(images // step,),
        in_specs=[
            pl.BlockSpec((step * patches, width), lambda i: (i, 0)),
            pl.BlockSpec((step * patches, heads), lambda i: (i, 0)),
            pl.BlockSpec((step, width), lambda i: (i, 0)),
            pl.BlockSpec((heads, width), lambda i: (0, 0)),
            pl.BlockSpec((heads, width), lambda i: (0, 0)),
            pl.BlockSpec((width, heads), lambda i: (0, 0)),
        ],
        out_specs=pl.BlockSpec((step * patches, width), lambda i: (i, 0)),
        flops=8 * rows * width * 128,
        moved=rows * width * 4,
    )(tiles, attend, dpooled, query_key_t, spread, gather)


def to_common(blocks, place):
    x, y_lo, core = place
    b = [[[blocks[(c * 2 + dy) * 4 + dx] for dx in range(4)] for dy in range(2)] for c in range(2)]
    b = [[[jnp.where(core == 0, b[c][dy][dx], b[1 - c][dy][dx]) for dx in range(4)] for dy in range(2)] for c in range(2)]
    b = [[[jnp.where(y_lo == 0, b[c][y][dx], b[c][1 - y][dx]) for dx in range(4)] for y in range(2)] for c in range(2)]
    for bit in (1, 2):
        moved = (x & bit) != 0
        b = [[[jnp.where(moved, b[c][y][(k - bit) % 4], b[c][y][k]) for k in range(4)] for y in range(2)] for c in range(2)]
    return [b[c][y][k] for c in range(2) for y in range(2) for k in range(4)]


def from_common(blocks, place):
    x, y_lo, core = place
    b = [[[blocks[(c * 2 + y) * 4 + k] for k in range(4)] for y in range(2)] for c in range(2)]
    for bit in (1, 2):
        moved = (x & bit) != 0
        b = [[[jnp.where(moved, b[c][y][(k + bit) % 4], b[c][y][k]) for k in range(4)] for y in range(2)] for c in range(2)]
    b = [[[jnp.where(y_lo == 0, b[c][y][dx], b[c][1 - y][dx]) for dx in range(4)] for y in range(2)] for c in range(2)]
    b = [[[jnp.where(core == 0, b[c][dy][dx], b[1 - c][dy][dx]) for dx in range(4)] for dy in range(2)] for c in range(2)]
    return [b[c][y][k] for c in range(2) for y in range(2) for k in range(4)]


def project(place, rows, own, other):
    count, width = rows.shape
    column = width // 16

    def kernel(place_ref, rows_ref, own_ref, other_ref, pre_ref, unit_ref):
        spot = place_ref[0], place_ref[1], place_ref[2]
        line = rows_ref[...].astype(BF)
        halves = nt_dot(line, own_ref[...]), nt_dot(line, other_ref[...])
        blocks = [half[:, i * column : (i + 1) * column] for half in halves for i in range(8)]
        for i, block in enumerate(to_common(blocks, spot)):
            pre_ref[:, i * column : (i + 1) * column] = block
        pre = pre_ref[...]
        inverse = lax.rsqrt(jnp.sum(pre * pre, axis=-1, keepdims=True) + EPSILON)
        unit_ref[...] = (pre * inverse).astype(BF)

    return call(
        kernel,
        (
            jax.ShapeDtypeStruct((count, width), F32),
            jax.ShapeDtypeStruct((count, width), BF),
        ),
        in_specs=[pl.BlockSpec(memory_space=SMEM)] + [pl.BlockSpec(memory_space=VMEM)] * 3,
        out_specs=[pl.BlockSpec(memory_space=VMEM)] * 2,
        flops=2 * count * width * width,
        moved=2 * width * width,
    )(place, rows, own, other)


def project_back(place, pre, parts, own, other, out_dtype):
    count, width = pre.shape
    column = width // 16

    def kernel(place_ref, pre_ref, *refs):
        part_refs, (own_ref, other_ref, out_ref, kept) = refs[: len(parts)], refs[len(parts) :]
        spot = place_ref[0], place_ref[1], place_ref[2]
        upstream = None
        for ref in part_refs:
            if len(ref.shape) == 3:
                terms = [ref[i].astype(F32) for i in range(ref.shape[0])]
            else:
                terms = [ref[...].astype(F32)]
            for term in terms:
                upstream = term if upstream is None else upstream + term
        pre = pre_ref[...]
        inverse = lax.rsqrt(jnp.sum(pre * pre, axis=-1, keepdims=True) + EPSILON)
        along = jnp.sum(pre * upstream, axis=-1, keepdims=True)
        dpre = inverse * upstream - inverse**3 * pre * along
        blocks = [dpre[:, i * column : (i + 1) * column] for i in range(16)]
        for i, block in enumerate(from_common(blocks, spot)):
            kept[:, i * column : (i + 1) * column] = block
        turned = kept[...].astype(BF)
        half = width // 2
        own_part = nn_dot(turned[:, :half], own_ref[...])
        total = own_part + nn_dot(turned[:, half:], other_ref[...])
        out_ref[...] = total.astype(BF).astype(out_dtype)

    return call(
        kernel,
        jax.ShapeDtypeStruct((count, width), out_dtype),
        in_specs=[pl.BlockSpec(memory_space=SMEM)]
        + [pl.BlockSpec(memory_space=VMEM)] * (3 + len(parts)),
        out_specs=pl.BlockSpec(memory_space=VMEM),
        scratch_shapes=[pltpu.VMEM((count, width), F32)],
        flops=2 * count * width * width,
        moved=2 * width * width,
    )(place, pre, *parts, own, other)


def grid_tile(scalars, texts, text_ids, images, positives, text_sum, cuts):
    text_count, width = texts.shape
    image_count = images.shape[0]
    block = min(256, image_count)
    steps = image_count // block

    def kernel(scalar_ref, texts_ref, ids_ref, images_ref, positives_ref, *refs):
        if text_sum is not None:
            sum_ref, *refs = refs
        image_part_ref, *text_refs = refs
        total = text_refs[-1] if cuts is not None else text_refs[0]
        step = pl.program_id(0)
        coolness, offset, scale = scalar_ref[0], scalar_ref[1], scalar_ref[2]
        texts = texts_ref[...]
        images = images_ref[...]
        logits = coolness * nt_dot(texts, images) + offset
        match = ids_ref[...] == positives_ref[...]
        steep = jnp.where(match, -scale, scale)
        slope = steep / (1.0 + jnp.exp(jnp.where(match, logits, -logits)))
        weighted = slope.astype(BF)
        image_part_ref[...] = tn_dot(weighted, texts).astype(BF)
        term = nn_dot(weighted, images)

        @pl.when(step == 0)
        def _():
            total[...] = term if text_sum is None else sum_ref[...] + term

        @pl.when(step > 0)
        def _():
            total[...] += term

        if cuts is not None:

            @pl.when(step == steps - 1)
            def _():
                start = 0
                for ref, size in zip(text_refs, cuts):
                    ref[...] = total[start : start + size, :].astype(BF)
                    start += size

    whole = pl.BlockSpec((text_count, width), lambda i: (0, 0))
    in_specs = [
        pl.BlockSpec(memory_space=SMEM),
        whole,
        pl.BlockSpec((text_count, 1), lambda i: (0, 0)),
        pl.BlockSpec((block, width), lambda i: (i, 0)),
        pl.BlockSpec((1, block), lambda i: (0, i)),
    ]
    operands = [scalars, texts, text_ids, images, positives]
    if text_sum is not None:
        in_specs.append(whole)
        operands.append(text_sum)
    outs = [jax.ShapeDtypeStruct((image_count, width), BF)]
    out_specs = [pl.BlockSpec((block, width), lambda i: (i, 0))]
    scratch = []
    if cuts is None:
        outs.append(jax.ShapeDtypeStruct((text_count, width), F32))
        out_specs.append(whole)
    else:
        for size in cuts:
            outs.append(jax.ShapeDtypeStruct((size, width), BF))
            out_specs.append(pl.BlockSpec((size, width), lambda i: (0, 0)))
        scratch.append(pltpu.VMEM((text_count, width), F32))
    return call(
        kernel,
        tuple(outs),
        grid=(steps,),
        in_specs=in_specs,
        out_specs=out_specs,
        scratch_shapes=scratch,
        flops=6 * text_count * image_count * width,
        transcendentals=text_count * image_count,
        moved=2 * width * (text_count + 2 * image_count),
    )(*operands)


def gather_matrix(piece):
    column = piece.shape[0]
    cut = column // 2 // 16 * 16
    right = take_from(piece, "x", 1, NX)
    left = take_from(piece, "x", -1, NX)
    far = jnp.concatenate(
        [take_from(right[:cut], "x", 1, NX), take_from(left[cut:], "x", -1, NX)], axis=0
    )
    beside = [
        take_from(piece, Y, 1, 4),
        take_from(right, Y, 1, 4),
        take_from(far, Y, -1, 4),
        take_from(left, Y, -1, 4),
    ]
    own = jnp.concatenate([piece, right, far, left] + beside, axis=0)
    return own, swap_cores(own)


def gather_texts(unit):
    near = jnp.concatenate(
        [unit] + [take_from(unit, "z", distance, NZ) for distance in NEAR[1:]], axis=0
    )
    ahead = take_from(near, "z", 1, NZ)
    behind = take_from(near, "z", -1, NZ)
    count = unit.shape[0]
    far = take_from(near[3 * count : 4 * count], "z", 2, NZ)
    return jnp.concatenate([near, ahead, behind, far], axis=0)


def scatter_texts(near, ahead, behind, far):
    count = far.shape[0]
    total = near.astype(F32) + take_from(ahead, "z", -1, NZ) + take_from(behind, "z", 1, NZ)
    far = take_from(far, "z", -2, NZ)
    parts = []
    for place, distance in enumerate(NEAR):
        part = total[place * count : (place + 1) * count]
        if distance == 6:
            part = part + far
        part = part.astype(BF)
        if distance:
            part = take_from(part, "z", -distance, NZ)
        parts.append(part)
    return parts


def to_all(values):
    spread = jnp.broadcast_to(values[None], (16,) + values.shape)
    return lax.all_to_all(spread, XY, 0, 0, tiled=True)


def shards(
    picture_tiles,
    query_key_product,
    pooling_exit_matrix,
    caption_embedding,
    caption_head_matrix,
    matching_caption_index,
    natural_inverse_coolness,
    score_offset,
    objective_adjoint,
):
    images, patches, width = picture_tiles.shape
    heads = query_key_product.shape[1]
    z, y_hi, y_lo, x, core = (lax.axis_index(a) for a in ("z", "y_hi", "y_lo", "x", "core"))
    place = jnp.stack([x, y_lo, core]).astype(jnp.int32)

    text_own, text_other = gather_matrix(caption_head_matrix.T)
    exit_own, exit_other = gather_matrix(pooling_exit_matrix.T)

    own_positives = to_all(matching_caption_index).reshape(1, -1)
    other_positives = swap_cores(own_positives)

    head_of = jnp.arange(width, dtype=jnp.int32) // (width // heads)
    spread = (head_of[None, :] == jnp.arange(heads, dtype=jnp.int32)[:, None]).astype(BF)
    gather = (head_of[:, None] == jnp.arange(heads, dtype=jnp.int32)[None, :]).astype(BF)
    tiles = picture_tiles.reshape(images * patches, width)
    attend, pooled = attention_forward(tiles, query_key_product, spread, patches)

    text_pre, text_unit = project(place, caption_embedding, text_own, text_other)
    texts = gather_texts(text_unit)
    image_pre, image_unit = project(place, pooled, exit_own, exit_other)
    own_images = to_all(image_unit).reshape(-1, width)
    other_images = swap_cores(own_images)

    txt = (y_lo * NX + x) * NC + core
    count = caption_embedding.shape[0]
    source = (z + jnp.array(TEXT_OFFSETS, jnp.int32)) % NZ
    first = (txt * (NZ * NYH) + source * NYH + y_hi) * count
    text_ids = (first[:, None] + jnp.arange(count, dtype=jnp.int32)[None, :]).reshape(-1, 1)

    coolness = jnp.exp(natural_inverse_coolness[0])
    scalars = jnp.stack([coolness, score_offset[0], coolness * objective_adjoint[0]])
    own_part, text_sum = grid_tile(scalars, texts, text_ids, own_images, own_positives, None, None)
    cuts = (5 * count, 5 * count, 5 * count, count)
    other_part, near, ahead, behind, far = grid_tile(
        scalars, texts, text_ids, other_images, other_positives, text_sum, cuts
    )

    chip_part = (own_part.astype(F32) + swap_cores(other_part).astype(F32)).astype(BF)
    image_parts = lax.all_to_all(chip_part.reshape(16, -1, width), XY, 0, 0, tiled=True)
    text_parts = scatter_texts(near, ahead, behind, far)

    dpooled = project_back(place, image_pre, [image_parts], exit_own, exit_other, F32)
    d_patches = attention_backward(
        tiles, attend, dpooled, query_key_product.T, spread, gather, patches
    )
    d_text = project_back(place, text_pre, text_parts, text_own, text_other, BF)
    return (d_patches.reshape(images, patches, width), d_text)


def solution(mesh):
    chips = Mesh(
        mesh.devices.reshape(NZ, NYH, NYL, NX, NC), ("z", "y_hi", "y_lo", "x", "core")
    )
    img, txt = ("z", "y_hi"), ("y_lo", "x", "core")
    return jax.shard_map(
        shards,
        mesh=chips,
        in_specs=(
            P(img + txt, None, None),
            P(),
            P(None, txt),
            P(txt + img, None),
            P(None, txt),
            P(img + txt),
            P(),
            P(),
            P(),
        ),
        out_specs=(P(img + txt, None, None), P(txt + img, None)),
        check_vma=False,
    )
```

time: 1060 us -> 261 us (0.25)
  waiting for transfers between devices: 952 us -> 25.8 us
  starting transfers between devices: 0.42 us -> 155 us
  matrix products: 36.6 us -> 0 us
  Pallas kernels: 0 us -> 31.8 us
  between operations: 16.9 us -> 3.28 us
  local copies, waits for them, and re-layouts: 24.2 us -> 35.8 us
  blocking collectives: 10.6 us -> 0 us
    reduce_scatter x2 -> x0, waiting for transfers between devices: 703 us -> none  [the longest x1 648 us: shards(): lax.psum_scatter(lax.dot_general(scaled_couples, image_rows, (((0,), (0,)...]
    all_gather x4 -> x0, waiting for transfers between devices: 248 us -> none  [the longest x1 157 us: shards(): text_rows = lax.all_gather(text_unit, 'img', axis=0, tiled=True)]
    ppermute x0 -> x35, starting transfers between devices: none -> 135 us  [the longest x30 125 us: take_from(): lax.ppermute(values, axis, [((i + distance) % size, i) for i in range(siz...]
    dot_general x11 -> x0, matrix products: 36.6 us -> none  [the longest x1 5.67 us: shards(): jnp.einsum('bhp,dh->bpd', dscores_low, query_key_product, preferred_eleme...]
    pallas_call x0 -> x8, Pallas kernels: none -> 31.8 us  [the longest x2 11.5 us: grid_tile(): call(kernel, tuple(outs), grid=(steps,), in_specs=in_specs, out_specs=out...]
    ppermute x0 -> x35, waiting for transfers between devices: none -> 25.4 us  [the longest x30 25.4 us: take_from(): lax.ppermute(values, axis, [((i + distance) % size, i) for i in range(siz...]
    unnamed x35 -> x63, local copies, waits for them, and re-layouts: 3.18 us -> 27.1 us
    all_to_all x0 -> x3, starting transfers between devices: none -> 20.1 us  [the longest x2 13.2 us: to_all(): return lax.all_to_all(spread, XY, 0, 0, tiled=True)]
  transfers between devices with their start and end apart: 6 -> 38, of which waited for: 6 -> 8; matrix products, arithmetic and copies ran while one was open for 6% -> 15% of each run, Pallas kernels for 0% -> 7%
where the time goes in v1:
time: 261 us; the launch traced here: 259 us
  starting transfers between devices  155 us (59%)
  local copies, waits for them, and re-layouts  35.8 us (14%)
  Pallas kernels  31.8 us (12%)
  waiting for transfers between devices  25.8 us (10%)
  other arithmetic  6.72 us (3%)
  between operations  3.28 us (1%)
    ppermute x30, starting transfers between devices, take_from(): lax.ppermute(values, axis, [((i + distance) % size, i) for i in range(siz...  125 us
    unnamed x63, local copies, waits for them, and re-layouts  27.1 us
    ppermute x30, waiting for transfers between devices, take_from(): lax.ppermute(values, axis, [((i + distance) % size, i) for i in range(siz...  25.4 us
    all_to_all x2, starting transfers between devices, to_all(): return lax.all_to_all(spread, XY, 0, 0, tiled=True)  13.2 us
    pallas_call x2, Pallas kernels, grid_tile(): call(kernel, tuple(outs), grid=(steps,), in_specs=in_specs, out_specs=out...  11.5 us
    ppermute x5, starting transfers between devices, swap_cores(): return lax.ppermute(values, 'core', [(0, 1), (1, 0)])  10.2 us
    all_to_all x1, starting transfers between devices, shards(): lax.all_to_all(chip_part.reshape(16, -1, width), XY, 0, 0, tiled=True)  6.93 us
    pallas_call x2, Pallas kernels, project(): call(kernel, (jax.ShapeDtypeStruct((count, width), F32), jax.ShapeDtypeSt...  6.79 us
  transfers between devices with their start and end apart: 38, of which 8 were waited for; matrix products, arithmetic and copies ran while one was open for 15% of the time, Pallas kernels for 7%

profile of v1, /device:TPU:6, one launch (start us, length us, event | category | flops | bytes accessed | tf_op | source)
XLA Modules:
  0.0 258.6 jit_solution(12698925959404785327)
XLA Ops:
  0.6 2.7 %collective-permute-start = (bf16[72,1152]{1,0:T(8,128)(2,1)}, bf16[72,1152]{1,0:T(8,128)(2,1)S(1)}, u32[]{:S(2)}, u32[]{:S(2)}) collective-permute-start(bf16[72,1152]{1,0:T(8,128)(2,1)} %bitcast.19), channel_id=1, source_target_pairs={{2,0},{4,2},{6,4},{0,6},{3,1},{5,3},{7,5},{1,7},{10,8},{12,10},{14... | collective-permute-start | bytes 497672 | tf_op jit(solution)/shard_map/ppermute | solution.py:21
  3.4 6.9 %collective-permute-start.2 = (bf16[72,1152]{1,0:T(8,128)(2,1)}, bf16[72,1152]{1,0:T(8,128)(2,1)S(1)}, u32[]{:S(2)}, u32[]{:S(2)}) collective-permute-start(bf16[72,1152]{1,0:T(8,128)(2,1)} %bitcast.20), channel_id=1, source_target_pairs={{6,0},{0,2},{2,4},{4,6},{7,1},{1,3},{3,5},{5,7},{14,8},{8,10},{10,... | collective-permute-start | bytes 497672 | tf_op jit(solution)/shard_map/ppermute | solution.py:21
  10.3 2.3 collective-permute-start.4
  12.6 1.9 collective-permute-start.9
  14.6 5.1 %collective-permute-start.11 = (bf16[72,1152]{1,0:T(8,128)(2,1)}, bf16[72,1152]{1,0:T(8,128)(2,1)S(1)}, u32[]{:S(2)}, u32[]{:S(2)}) collective-permute-start(bf16[72,1152]{1,0:T(8,128)(2,1)} %bitcast.23), channel_id=1, source_target_pairs={{6,0},{0,2},{2,4},{4,6},{7,1},{1,3},{3,5},{5,7},{14,8},{8,10},{10,... | collective-permute-start | bytes 497672 | tf_op jit(solution)/shard_map/ppermute | solution.py:21
  22.9 2.6 %collective-permute-start.13 = (bf16[72,1152]{1,0:T(8,128)(2,1)}, bf16[72,1152]{1,0:T(8,128)(2,1)S(1)}, u32[]{:S(2)}, u32[]{:S(2)}) collective-permute-start(bf16[72,1152]{1,0:T(8,128)(2,1)} %bitcast.24), channel_id=1, source_target_pairs={{8,0},{16,8},{24,16},{0,24},{9,1},{17,9},{25,17},{1,25},{10,2},{18... | collective-permute-start | bytes 497672 | tf_op jit(solution)/shard_map/ppermute | solution.py:21
  25.6 1.9 collective-permute-start.1
  28.2 5.1 %collective-permute-start.3 = (bf16[40,1152]{1,0:T(8,128)(2,1)S(1)}, bf16[40,1152]{1,0:T(8,128)(2,1)S(1)}, u32[]{:S(2)}, u32[]{:S(2)}) collective-permute-start(bf16[40,1152]{1,0:T(8,128)(2,1)S(1)} %slice.41), channel_id=1, source_target_pairs={{6,0},{0,2},{2,4},{4,6},{7,1},{1,3},{3,5},{5,7},{14,8},{8,10},{10,... | collective-permute-start | bytes 276488 | tf_op jit(solution)/shard_map/ppermute | solution.py:21
  34.0 1.9 collective-permute-start.10
  36.0 5.1 %collective-permute-start.12 = (bf16[40,1152]{1,0:T(8,128)(2,1)S(1)}, bf16[40,1152]{1,0:T(8,128)(2,1)S(1)}, u32[]{:S(2)}, u32[]{:S(2)}) collective-permute-start(bf16[40,1152]{1,0:T(8,128)(2,1)S(1)} %slice.43), channel_id=1, source_target_pairs={{6,0},{0,2},{2,4},{4,6},{7,1},{1,3},{3,5},{5,7},{14,8},{8,10},{10,... | collective-permute-start | bytes 276488 | tf_op jit(solution)/shard_map/ppermute | solution.py:21
  41.8 2.3 collective-permute-start.5
  44.8 3.5 %collective-permute-start.7 = (bf16[72,1152]{1,0:T(8,128)(2,1)S(1)}, bf16[72,1152]{1,0:T(8,128)(2,1)S(1)}, u32[]{:S(2)}, u32[]{:S(2)}) collective-permute-start(bf16[72,1152]{1,0:T(8,128)(2,1)S(1)} %collective-permute-done.2), channel_id=1, source_target_pairs={{24,0},{0,8},{8,16},{16,24},{25,1},{1,9},{9,17},{17,25},{26,2},{2,... | collective-permute-start | bytes 497672 | tf_op jit(solution)/shard_map/ppermute | solution.py:21
  49.6 3.6 %collective-permute-start.14 = (bf16[72,1152]{1,0:T(8,128)(2,1)S(1)}, bf16[72,1152]{1,0:T(8,128)(2,1)S(1)}, u32[]{:S(2)}, u32[]{:S(2)}) collective-permute-start(bf16[72,1152]{1,0:T(8,128)(2,1)S(1)} %collective-permute-done.9), channel_id=1, source_target_pairs={{8,0},{16,8},{24,16},{0,24},{9,1},{17,9},{25,17},{1,25},{10,2},{18... | collective-permute-start | bytes 497672 | tf_op jit(solution)/shard_map/ppermute | solution.py:21
  54.5 2.4 collective-permute-start.16
  57.6 3.3 %collective-permute-start.6 = (bf16[72,1152]{1,0:T(8,128)(2,1)S(1)}, bf16[72,1152]{1,0:T(8,128)(2,1)S(1)}, u32[]{:S(2)}, u32[]{:S(2)}) collective-permute-start(bf16[72,1152]{1,0:T(8,128)(2,1)S(1)} %pad_maximum_fusion), channel_id=1, source_target_pairs={{24,0},{0,8},{8,16},{16,24},{25,1},{1,9},{9,17},{17,25},{26,2},{2,... | collective-permute-start | bytes 497672 | tf_op jit(solution)/shard_map/ppermute | solution.py:21
  61.6 3.5 %collective-permute-start.15 = (bf16[72,1152]{1,0:T(8,128)(2,1)S(1)}, bf16[72,1152]{1,0:T(8,128)(2,1)S(1)}, u32[]{:S(2)}, u32[]{:S(2)}) collective-permute-start(bf16[72,1152]{1,0:T(8,128)(2,1)S(1)} %pad_maximum_fusion.1), channel_id=1, source_target_pairs={{24,0},{0,8},{8,16},{16,24},{25,1},{1,9},{9,17},{17,25},{26,2},{2,... | collective-permute-start | bytes 497672 | tf_op jit(solution)/shard_map/ppermute | solution.py:21
  66.5 3.5 %collective-permute-done.15 = bf16[72,1152]{1,0:T(8,128)(2,1)S(1)} collective-permute-done((bf16[72,1152]{1,0:T(8,128)(2,1)S(1)}, bf16[72,1152]{1,0:T(8,128)(2,1)S(1)}, u32[]{:S(2)}, u32[]{:S(2)}) %collective-permute-start.15) | collective-permute-done | bytes 165920 | tf_op jit(solution)/shard_map/ppermute | solution.py:21
  74.7 2.4 collective-permute-start.8
  77.4 2.6 %shard_map.113 = (f32[1024,16]{1,0:T(8,128)S(1)}, f32[32,1152]{1,0:T(8,128)S(1)}) custom-call(bf16[1024,1152]{1,0:T(8,128)(2,1)S(1)} %bitcast.12, bf16[1152,16]{1,0:T(8,128)(2,1)S(1)} %copy.16.qk_ref, bf16[16,1152]{1,0:T(8,128)(2,1)S(1)} %fusion.2.spread_ref), custom_call_target="tpu_custom_call" | custom-call | flops 603979776 | bytes 2359296 | tf_op jit(solution)/shard_map/pallas_call | solution.py:71
  81.0 3.7 %shard_map.115 = (f32[32,1152]{1,0:T(8,128)S(1)}, bf16[32,1152]{1,0:T(8,128)(2,1)}) custom-call(s32[3]{0:T(128)S(1)} %pad_add_fusion.place_ref, bf16[32,1152]{1,0:T(8,128)(2,1)S(1)} %copy-done.13, bf16[576,1152]{1,0:T(8,128)(2,1)} %constant_dynamic-update-slice_fusion.9.own_ref.refs_5_, bf16[576,1152]{1,0:T(8,128)(2,1)} %collective-permute-done.17.other_ref.refs_6_), custom_call_target="tpu_custom_call" | custom-call | flops 84934656 | bytes 2654208 | tf_op jit(solution)/shard_map/pallas_call | solution.py:172
  84.7 12.3 %collective-permute-start.18 = (bf16[32,1152]{1,0:T(8,128)(2,1)}, bf16[32,1152]{1,0:T(8,128)(2,1)}, u32[]{:S(2)}, u32[]{:S(2)}) collective-permute-start(bf16[32,1152]{1,0:T(8,128)(2,1)} %get-tuple-element.18), channel_id=1, source_target_pairs={{96,0},{128,32},{160,64},{192,96},{224,128},{256,160},{288,192},{3... | collective-permute-start | bytes 221192 | tf_op jit(solution)/shard_map/ppermute | solution.py:21
  100.4 9.5 %collective-permute-start.20 = (bf16[32,1152]{1,0:T(8,128)(2,1)}, bf16[32,1152]{1,0:T(8,128)(2,1)}, u32[]{:S(2)}, u32[]{:S(2)}) collective-permute-start(bf16[32,1152]{1,0:T(8,128)(2,1)} %get-tuple-element.18), channel_id=1, source_target_pairs={{192,0},{224,32},{256,64},{288,96},{320,128},{352,160},{384,192},{... | collective-permute-start | bytes 221192 | tf_op jit(solution)/shard_map/ppermute | solution.py:21
  109.9 2.1 collective-permute-start.21
  112.0 3.1 %shard_map.114 = (f32[32,1152]{1,0:T(8,128)S(1)}, bf16[32,1152]{1,0:T(8,128)(2,1)S(1)}) custom-call(s32[3]{0:T(128)S(1)} %pad_add_fusion.place_ref, f32[32,1152]{1,0:T(8,128)S(1)} %get-tuple-element.16.rows_ref, bf16[576,1152]{1,0:T(8,128)(2,1)} %constant_dynamic-update-slice_fusion.own_ref.refs_1_, bf16[576,1152]{1,0:T(8,128)(2,1)} %collective-permute-done.8.other_ref.refs_2_), custom_call_target="tpu_custom_call" | custom-call | flops 84934656 | bytes 2654208 | tf_op jit(solution)/shard_map/pallas_call | solution.py:172
  116.9 5.9 %all-to-all-start = ((bf16[16,32,1152]{2,1,0:T(8,128)(2,1)}), bf16[16,32,1152]{2,1,0:T(8,128)(2,1)S(1)}, u32[]{:S(2)}, u32[]{:S(2)}) async-start(bf16[16,32,1152]{2,1,0:T(8,128)(2,1)} %broadcast_in_dim.4), calls=%async_computation | async-start | bytes 2359296 | tf_op jit(solution)/shard_map/all_to_all | solution.py:348
  127.5 2.0 collective-permute-done.21
  131.1 5.2 %collective-permute-start.22 = (bf16[160,1152]{1,0:T(8,128)(2,1)}, bf16[160,1152]{1,0:T(8,128)(2,1)}, u32[]{:S(2)}, u32[]{:S(2)}) collective-permute-start(bf16[160,1152]{1,0:T(8,128)(2,1)} %get-tuple-element.34), channel_id=1, source_target_pairs={{32,0},{64,32},{96,64},{128,96},{160,128},{192,160},{224,192},{256... | collective-permute-start | bytes 1105928 | tf_op jit(solution)/shard_map/ppermute | solution.py:21
  136.4 1.9 collective-permute-start.23
  138.9 7.2 %all-to-all-start.1 = ((s32[16,1,32]{2,1,0:T(1,128)}), s32[16,1,32]{2,1,0:T(1,128)}, u32[]{:S(2)}, u32[]{:S(2)}) async-start(s32[16,1,32]{2,1,0:T(1,128)} %broadcast_in_dim.5), calls=%async_computation.1 | async-start | bytes 16384 | tf_op jit(solution)/shard_map/all_to_all | solution.py:348
  152.2 2.0 reduce.3
  155.0 2.1 collective-permute-start.26
  157.1 6.9 %collective-permute-start.24 = (bf16[32,1152]{1,0:T(8,128)(2,1)}, bf16[32,1152]{1,0:T(8,128)(2,1)S(1)}, u32[]{:S(2)}, u32[]{:S(2)}) collective-permute-start(bf16[32,1152]{1,0:T(8,128)(2,1)} %collective-permute-done.20), channel_id=1, source_target_pairs={{64,0},{96,32},{128,64},{160,96},{192,128},{224,160},{256,192},{28... | collective-permute-start | bytes 221192 | tf_op jit(solution)/shard_map/ppermute | solution.py:21
  170.0 5.1 %shard_map.116 = (bf16[512,1152]{1,0:T(8,128)(2,1)S(1)}, f32[512,1152]{1,0:T(8,128)S(1)}) custom-call(f32[3]{0:T(128)S(1)} %pad_maximum_fusion.2.scalar_ref, bf16[512,1152]{1,0:T(8,128)(2,1)S(1)} %copy-done.14, s32[512,1]{1,0:T(8,128)S(1)} %copy-done.6, bf16[512,1152]{1,0:T(8,128)(2,1)S(1)} %bitcast.15, s32[1,512]{1,0:T(1,128)S(1)} %reshape.83.positives_ref), custom_call_target="tpu_custom_call" | custom-call | flops 1811939328 | bytes 3538944 | tf_op jit(solution)/shard_map/pallas_call | solution.py:288
  175.1 6.5 %shard_map.117 = (bf16[512,1152]{1,0:T(8,128)(2,1)S(1)}, bf16[160,1152]{1,0:T(8,128)(2,1)S(1)}, bf16[160,1152]{1,0:T(8,128)(2,1)S(1)}, bf16[160,1152]{1,0:T(8,128)(2,1)S(1)}, bf16[32,1152]{1,0:T(8,128)(2,1)}) custom-call(f32[3]{0:T(128)S(1)} %pad_maximum_fusion.2.scalar_ref, bf16[512,1152]{1,0:T(8,128)(2,1)S(1)} %copy-done.15, s32[512,1]{1,0:T(8,128)S(1)} %copy-done.6, ...), custom_call_target="tpu_custom_call" | custom-call | flops 1811939328 | bytes 3538944 | tf_op jit(solution)/shard_map/pallas_call | solution.py:288
  183.4 4.5 %collective-permute-start.29 = (bf16[160,1152]{1,0:T(8,128)(2,1)S(1)}, bf16[160,1152]{1,0:T(8,128)(2,1)S(1)}, u32[]{:S(2)}, u32[]{:S(2)}) collective-permute-start(bf16[160,1152]{1,0:T(8,128)(2,1)S(1)} %get-tuple-element.26), channel_id=1, source_target_pairs={{32,0},{64,32},{96,64},{128,96},{160,128},{192,160},{224,192},{256... | collective-permute-start | bytes 1105928 | tf_op jit(solution)/shard_map/ppermute | solution.py:21
  188.0 1.9 collective-permute-start.28
  189.9 2.4 collective-permute-start.32
  192.3 4.2 %collective-permute-done.29 = bf16[160,1152]{1,0:T(8,128)(2,1)S(1)} collective-permute-done((bf16[160,1152]{1,0:T(8,128)(2,1)S(1)}, bf16[160,1152]{1,0:T(8,128)(2,1)S(1)}, u32[]{:S(2)}, u32[]{:S(2)}) %collective-permute-start.29) | collective-permute-done | bytes 368672 | tf_op jit(solution)/shard_map/ppermute | solution.py:21
  196.5 6.3 %collective-permute-done.28 = bf16[160,1152]{1,0:T(8,128)(2,1)S(1)} collective-permute-done((bf16[160,1152]{1,0:T(8,128)(2,1)S(1)}, bf16[160,1152]{1,0:T(8,128)(2,1)S(1)}, u32[]{:S(2)}, u32[]{:S(2)}) %collective-permute-start.28) | collective-permute-done | bytes 368672 | tf_op jit(solution)/shard_map/ppermute | solution.py:21
  205.3 6.9 %all-to-all-start.2 = ((bf16[16,32,1152]{2,1,0:T(8,128)(2,1)}), bf16[16,32,1152]{2,1,0:T(8,128)(2,1)S(1)}, u32[]{:S(2)}, u32[]{:S(2)}) async-start(bf16[16,32,1152]{2,1,0:T(8,128)(2,1)} %bitcast.17), calls=%async_computation.2 | async-start | bytes 2359296 | tf_op jit(solution)/shard_map/all_to_all | solution.py:400
  213.2 1.9 collective-permute-start.30
  215.2 6.9 %collective-permute-start.31 = (bf16[32,1152]{1,0:T(8,128)(2,1)S(1)}, bf16[32,1152]{1,0:T(8,128)(2,1)S(1)}, u32[]{:S(2)}, u32[]{:S(2)}) collective-permute-start(bf16[32,1152]{1,0:T(8,128)(2,1)S(1)} %get-tuple-element.31), channel_id=1, source_target_pairs={{96,0},{128,32},{160,64},{192,96},{224,128},{256,160},{288,192},{3... | collective-permute-start | bytes 221192 | tf_op jit(solution)/shard_map/ppermute | solution.py:21
  223.1 4.2 %collective-permute-start.33 = (bf16[32,1152]{1,0:T(8,128)(2,1)S(1)}, bf16[32,1152]{1,0:T(8,128)(2,1)S(1)}, u32[]{:S(2)}, u32[]{:S(2)}) collective-permute-start(bf16[32,1152]{1,0:T(8,128)(2,1)S(1)} %fusion.1), channel_id=1, source_target_pairs={{320,0},{352,32},{384,64},{416,96},{448,128},{480,160},{0,192},{32... | collective-permute-start | bytes 221192 | tf_op jit(solution)/shard_map/ppermute | solution.py:21
  227.3 8.7 %collective-permute-start.34 = (bf16[32,1152]{1,0:T(8,128)(2,1)S(1)}, bf16[32,1152]{1,0:T(8,128)(2,1)S(1)}, u32[]{:S(2)}, u32[]{:S(2)}) collective-permute-start(bf16[32,1152]{1,0:T(8,128)(2,1)S(1)} %get-tuple-element.30), channel_id=1, source_target_pairs={{192,0},{224,32},{256,64},{288,96},{320,128},{352,160},{384,192},{... | collective-permute-start | bytes 221192 | tf_op jit(solution)/shard_map/ppermute | solution.py:21
  237.2 8.6 %collective-permute-done.34.refs_4_ = bf16[32,1152]{1,0:T(8,128)(2,1)S(1)} collective-permute-done((bf16[32,1152]{1,0:T(8,128)(2,1)S(1)}, bf16[32,1152]{1,0:T(8,128)(2,1)S(1)}, u32[]{:S(2)}, u32[]{:S(2)}) %collective-permute-start.34) | collective-permute-done | bytes 73760 | tf_op jit(solution)/shard_map/ppermute | solution.py:21
  246.7 3.6 %shard_map.120 = bf16[32,1152]{1,0:T(8,128)(2,1)} custom-call(s32[3]{0:T(128)S(1)} %pad_add_fusion.place_ref, f32[32,1152]{1,0:T(8,128)S(1)} %copy-done.10, bf16[32,1152]{1,0:T(8,128)(2,1)S(1)} %get-tuple-element.33.refs_0_, bf16[32,1152]{1,0:T(8,128)(2,1)S(1)} %collective-permute-done.30.refs_1_, bf16[32,1152]{1,0:T(8,128)(2,1)S(1)} %collective-permute-done.31.refs_2_, ...), custom_call_target="tpu_custom_call" | custom-call | flops 84934656 | bytes 2654208 | tf_op jit(solution)/shard_map/pallas_call | solution.py:213
  251.2 3.2 %shard_map.118.dpooled_ref = f32[32,1152]{1,0:T(8,128)S(1)} custom-call(s32[3]{0:T(128)S(1)} %pad_add_fusion.place_ref, f32[32,1152]{1,0:T(8,128)S(1)} %copy-done.8, bf16[16,32,1152]{2,1,0:T(8,128)(2,1)S(1)} %all-to-all-done.2.refs_0_, bf16[576,1152]{1,0:T(8,128)(2,1)} %constant_dynamic-update-slice_fusion.own_ref.refs_1_, ...), custom_call_target="tpu_custom_call" | custom-call | flops 84934656 | bytes 2654208 | tf_op jit(solution)/shard_map/pallas_call | solution.py:213
  254.4 4.2 %shard_map.119 = bf16[1024,1152]{1,0:T(8,128)(2,1)} custom-call(bf16[1024,1152]{1,0:T(8,128)(2,1)S(1)} %bitcast.13, f32[1024,16]{1,0:T(8,128)S(1)} %copy-done.3, f32[32,1152]{1,0:T(8,128)S(1)} %shard_map.118.dpooled_ref, bf16[16,1152]{1,0:T(8,128)(2,1)S(1)} %bitcast.16, bf16[16,1152]{1,0:T(8,128)(2,1)S(1)} %copy-done.5, bf16[1152,16]{1,0:T(8,128)(2,1)S(1)} %copy-done.1), custom_call_target="tpu_custom_call" | custom-call | flops 1207959552 | bytes 4718592 | tf_op jit(solution)/shard_map/pallas_call | solution.py:117
  (126 shorter events, 49.4 us)
Async XLA Ops:
  0.6 22.3 %collective-permute-start = (bf16[72,1152]{1,0:T(8,128)(2,1)}, bf16[72,1152]{1,0:T(8,128)(2,1)S(1)}, u32[]{:S(2)}, u32[]{:S(2)}) collective-permute-start(bf16[72,1152]{1,0:T(8,128)(2,1)} %bitcast.19), channel_id=1, source_target_pairs={{2,0},{4,2},{6,4},{0,6},{3,1},{5,3},{7,5},{1,7},{10,8},{12,10},{14... | collective-permute-start | bytes 497672 | tf_op jit(solution)/shard_map/ppermute | solution.py:21
  3.4 22.2 %collective-permute-start.2 = (bf16[72,1152]{1,0:T(8,128)(2,1)}, bf16[72,1152]{1,0:T(8,128)(2,1)S(1)}, u32[]{:S(2)}, u32[]{:S(2)}) collective-permute-start(bf16[72,1152]{1,0:T(8,128)(2,1)} %bitcast.20), channel_id=1, source_target_pairs={{6,0},{0,2},{2,4},{4,6},{7,1},{1,3},{3,5},{5,7},{14,8},{8,10},{10,... | collective-permute-start | bytes 497672 | tf_op jit(solution)/shard_map/ppermute | solution.py:21
  10.3 44.2 %collective-permute-start.4 = (bf16[72,1152]{1,0:T(8,128)(2,1)}, bf16[72,1152]{1,0:T(8,128)(2,1)S(1)}, u32[]{:S(2)}, u32[]{:S(2)}) collective-permute-start(bf16[72,1152]{1,0:T(8,128)(2,1)} %bitcast.21), channel_id=1, source_target_pairs={{8,0},{16,8},{24,16},{0,24},{9,1},{17,9},{25,17},{1,25},{10,2},{18... | collective-permute-start | bytes 497672 | tf_op jit(solution)/shard_map/ppermute | solution.py:21
  12.6 15.6 %collective-permute-start.9 = (bf16[72,1152]{1,0:T(8,128)(2,1)}, bf16[72,1152]{1,0:T(8,128)(2,1)S(1)}, u32[]{:S(2)}, u32[]{:S(2)}) collective-permute-start(bf16[72,1152]{1,0:T(8,128)(2,1)} %bitcast.22), channel_id=1, source_target_pairs={{2,0},{4,2},{6,4},{0,6},{3,1},{5,3},{7,5},{1,7},{10,8},{12,10},{14... | collective-permute-start | bytes 497672 | tf_op jit(solution)/shard_map/ppermute | solution.py:21
  14.6 19.5 %collective-permute-start.11 = (bf16[72,1152]{1,0:T(8,128)(2,1)}, bf16[72,1152]{1,0:T(8,128)(2,1)S(1)}, u32[]{:S(2)}, u32[]{:S(2)}) collective-permute-start(bf16[72,1152]{1,0:T(8,128)(2,1)} %bitcast.23), channel_id=1, source_target_pairs={{6,0},{0,2},{2,4},{4,6},{7,1},{1,3},{3,5},{5,7},{14,8},{8,10},{10,... | collective-permute-start | bytes 497672 | tf_op jit(solution)/shard_map/ppermute | solution.py:21
  22.9 34.7 %collective-permute-start.13 = (bf16[72,1152]{1,0:T(8,128)(2,1)}, bf16[72,1152]{1,0:T(8,128)(2,1)S(1)}, u32[]{:S(2)}, u32[]{:S(2)}) collective-permute-start(bf16[72,1152]{1,0:T(8,128)(2,1)} %bitcast.24), channel_id=1, source_target_pairs={{8,0},{16,8},{24,16},{0,24},{9,1},{17,9},{25,17},{1,25},{10,2},{18... | collective-permute-start | bytes 497672 | tf_op jit(solution)/shard_map/ppermute | solution.py:21
  25.6 10.4 %collective-permute-start.1 = (bf16[32,1152]{1,0:T(8,128)(2,1)S(1)}, bf16[32,1152]{1,0:T(8,128)(2,1)S(1)}, u32[]{:S(2)}, u32[]{:S(2)}) collective-permute-start(bf16[32,1152]{1,0:T(8,128)(2,1)S(1)} %slice.40), channel_id=1, source_target_pairs={{2,0},{4,2},{6,4},{0,6},{3,1},{5,3},{7,5},{1,7},{10,8},{12,10},{14... | collective-permute-start | bytes 221192 | tf_op jit(solution)/shard_map/ppermute | solution.py:21
  28.2 16.6 %collective-permute-start.3 = (bf16[40,1152]{1,0:T(8,128)(2,1)S(1)}, bf16[40,1152]{1,0:T(8,128)(2,1)S(1)}, u32[]{:S(2)}, u32[]{:S(2)}) collective-permute-start(bf16[40,1152]{1,0:T(8,128)(2,1)S(1)} %slice.41), channel_id=1, source_target_pairs={{6,0},{0,2},{2,4},{4,6},{7,1},{1,3},{3,5},{5,7},{14,8},{8,10},{10,... | collective-permute-start | bytes 276488 | tf_op jit(solution)/shard_map/ppermute | solution.py:21
  34.0 7.7 %collective-permute-start.10 = (bf16[32,1152]{1,0:T(8,128)(2,1)S(1)}, bf16[32,1152]{1,0:T(8,128)(2,1)S(1)}, u32[]{:S(2)}, u32[]{:S(2)}) collective-permute-start(bf16[32,1152]{1,0:T(8,128)(2,1)S(1)} %slice.42), channel_id=1, source_target_pairs={{2,0},{4,2},{6,4},{0,6},{3,1},{5,3},{7,5},{1,7},{10,8},{12,10},{14... | collective-permute-start | bytes 221192 | tf_op jit(solution)/shard_map/ppermute | solution.py:21
  36.0 13.6 %collective-permute-start.12 = (bf16[40,1152]{1,0:T(8,128)(2,1)S(1)}, bf16[40,1152]{1,0:T(8,128)(2,1)S(1)}, u32[]{:S(2)}, u32[]{:S(2)}) collective-permute-start(bf16[40,1152]{1,0:T(8,128)(2,1)S(1)} %slice.43), channel_id=1, source_target_pairs={{6,0},{0,2},{2,4},{4,6},{7,1},{1,3},{3,5},{5,7},{14,8},{8,10},{10,... | collective-permute-start | bytes 276488 | tf_op jit(solution)/shard_map/ppermute | solution.py:21
  41.8 19.8 %collective-permute-start.5 = (bf16[72,1152]{1,0:T(8,128)(2,1)S(1)}, bf16[72,1152]{1,0:T(8,128)(2,1)S(1)}, u32[]{:S(2)}, u32[]{:S(2)}) collective-permute-start(bf16[72,1152]{1,0:T(8,128)(2,1)S(1)} %collective-permute-done), channel_id=1, source_target_pairs={{8,0},{16,8},{24,16},{0,24},{9,1},{17,9},{25,17},{1,25},{10,2},{18... | collective-permute-start | bytes 497672 | tf_op jit(solution)/shard_map/ppermute | solution.py:21
  44.8 29.3 %collective-permute-start.7 = (bf16[72,1152]{1,0:T(8,128)(2,1)S(1)}, bf16[72,1152]{1,0:T(8,128)(2,1)S(1)}, u32[]{:S(2)}, u32[]{:S(2)}) collective-permute-start(bf16[72,1152]{1,0:T(8,128)(2,1)S(1)} %collective-permute-done.2), channel_id=1, source_target_pairs={{24,0},{0,8},{8,16},{16,24},{25,1},{1,9},{9,17},{17,25},{26,2},{2,... | collective-permute-start | bytes 497672 | tf_op jit(solution)/shard_map/ppermute | solution.py:21
  49.6 16.2 %collective-permute-start.14 = (bf16[72,1152]{1,0:T(8,128)(2,1)S(1)}, bf16[72,1152]{1,0:T(8,128)(2,1)S(1)}, u32[]{:S(2)}, u32[]{:S(2)}) collective-permute-start(bf16[72,1152]{1,0:T(8,128)(2,1)S(1)} %collective-permute-done.9), channel_id=1, source_target_pairs={{8,0},{16,8},{24,16},{0,24},{9,1},{17,9},{25,17},{1,25},{10,2},{18... | collective-permute-start | bytes 497672 | tf_op jit(solution)/shard_map/ppermute | solution.py:21
  54.5 22.6 %copy-start.11 = (bf16[1152,16]{0,1:T(8,128)(2,1)S(1)}, bf16[1152,16]{0,1:T(8,128)(2,1)}, u32[]{:S(2)}) copy-start(bf16[1152,16]{0,1:T(8,128)(2,1)} %param.11) | copy-start | bytes 110596
  54.5 16.2 %collective-permute-start.16 = (bf16[72,1152]{1,0:T(8,128)(2,1)S(1)}, bf16[72,1152]{1,0:T(8,128)(2,1)S(1)}, u32[]{:S(2)}, u32[]{:S(2)}) collective-permute-start(bf16[72,1152]{1,0:T(8,128)(2,1)S(1)} %collective-permute-done.11), channel_id=1, source_target_pairs={{24,0},{0,8},{8,16},{16,24},{25,1},{1,9},{9,17},{17,25},{26,2},{2,... | collective-permute-start | bytes 497672 | tf_op jit(solution)/shard_map/ppermute | solution.py:21
  57.6 19.8 %copy-start = (bf16[32,32,1152]{2,1,0:T(8,128)(2,1)S(1)}, bf16[32,32,1152]{2,1,0:T(8,128)(2,1)}, u32[]{:S(2)}) copy-start(bf16[32,32,1152]{2,1,0:T(8,128)(2,1)} %param.10) | copy-start | bytes 7077892
  57.6 15.7 %collective-permute-start.6 = (bf16[72,1152]{1,0:T(8,128)(2,1)S(1)}, bf16[72,1152]{1,0:T(8,128)(2,1)S(1)}, u32[]{:S(2)}, u32[]{:S(2)}) collective-permute-start(bf16[72,1152]{1,0:T(8,128)(2,1)S(1)} %pad_maximum_fusion), channel_id=1, source_target_pairs={{24,0},{0,8},{8,16},{16,24},{25,1},{1,9},{9,17},{17,25},{26,2},{2,... | collective-permute-start | bytes 497672 | tf_op jit(solution)/shard_map/ppermute | solution.py:21
  61.6 8.4 %collective-permute-start.15 = (bf16[72,1152]{1,0:T(8,128)(2,1)S(1)}, bf16[72,1152]{1,0:T(8,128)(2,1)S(1)}, u32[]{:S(2)}, u32[]{:S(2)}) collective-permute-start(bf16[72,1152]{1,0:T(8,128)(2,1)S(1)} %pad_maximum_fusion.1), channel_id=1, source_target_pairs={{24,0},{0,8},{8,16},{16,24},{25,1},{1,9},{9,17},{17,25},{26,2},{2,... | collective-permute-start | bytes 497672 | tf_op jit(solution)/shard_map/ppermute | solution.py:21
  71.4 9.5 %collective-permute-start.17 = (bf16[576,1152]{1,0:T(8,128)(2,1)}, bf16[576,1152]{1,0:T(8,128)(2,1)}, u32[]{:S(2)}, u32[]{:S(2)}) collective-permute-start(bf16[576,1152]{1,0:T(8,128)(2,1)} %constant_dynamic-update-slice_fusion.9.own_ref.refs_5_), channel_id=1, source_target_pairs={{0,1},{1,0},{2,3},{3,2},{4,5},{5,4},{6,7},{7,6},{8,9},{9,8},{10,11... | collective-permute-start | bytes 3981320 | tf_op jit(solution)/shard_map/ppermute | solution.py:25
  74.7 37.3 %collective-permute-start.8 = (bf16[576,1152]{1,0:T(8,128)(2,1)}, bf16[576,1152]{1,0:T(8,128)(2,1)}, u32[]{:S(2)}, u32[]{:S(2)}) collective-permute-start(bf16[576,1152]{1,0:T(8,128)(2,1)} %constant_dynamic-update-slice_fusion.own_ref.refs_1_), channel_id=1, source_target_pairs={{0,1},{1,0},{2,3},{3,2},{4,5},{5,4},{6,7},{7,6},{8,9},{9,8},{10,11... | collective-permute-start | bytes 3981320 | tf_op jit(solution)/shard_map/ppermute | solution.py:25
  77.4 3.5 %copy-start.13 = (bf16[32,1152]{1,0:T(8,128)(2,1)S(1)}, bf16[32,1152]{1,0:T(8,128)(2,1)}, u32[]{:S(2)}) copy-start(bf16[32,1152]{1,0:T(8,128)(2,1)} %rows_ref.1) | copy-start | bytes 221188
  84.7 27.3 %copy-start.9 = (f32[32,1152]{1,0:T(8,128)}, f32[32,1152]{1,0:T(8,128)S(1)}, u32[]{:S(2)}) copy-start(f32[32,1152]{1,0:T(8,128)S(1)} %get-tuple-element.23.pre_ref) | copy-start | bytes 442372
  84.7 38.2 %collective-permute-start.18 = (bf16[32,1152]{1,0:T(8,128)(2,1)}, bf16[32,1152]{1,0:T(8,128)(2,1)}, u32[]{:S(2)}, u32[]{:S(2)}) collective-permute-start(bf16[32,1152]{1,0:T(8,128)(2,1)} %get-tuple-element.18), channel_id=1, source_target_pairs={{96,0},{128,32},{160,64},{192,96},{224,128},{256,160},{288,192},{3... | collective-permute-start | bytes 221192 | tf_op jit(solution)/shard_map/ppermute | solution.py:21
  98.5 25.9 %collective-permute-start.19 = (bf16[32,1152]{1,0:T(8,128)(2,1)}, bf16[32,1152]{1,0:T(8,128)(2,1)}, u32[]{:S(2)}, u32[]{:S(2)}) collective-permute-start(bf16[32,1152]{1,0:T(8,128)(2,1)} %get-tuple-element.18), channel_id=1, source_target_pairs={{416,0},{448,32},{480,64},{0,96},{32,128},{64,160},{96,192},{128,2... | collective-permute-start | bytes 221192 | tf_op jit(solution)/shard_map/ppermute | solution.py:21
  100.4 25.5 %collective-permute-start.20 = (bf16[32,1152]{1,0:T(8,128)(2,1)}, bf16[32,1152]{1,0:T(8,128)(2,1)}, u32[]{:S(2)}, u32[]{:S(2)}) collective-permute-start(bf16[32,1152]{1,0:T(8,128)(2,1)} %get-tuple-element.18), channel_id=1, source_target_pairs={{192,0},{224,32},{256,64},{288,96},{320,128},{352,160},{384,192},{... | collective-permute-start | bytes 221192 | tf_op jit(solution)/shard_map/ppermute | solution.py:21
  109.9 19.6 %collective-permute-start.21 = (bf16[32,1152]{1,0:T(8,128)(2,1)}, bf16[32,1152]{1,0:T(8,128)(2,1)}, u32[]{:S(2)}, u32[]{:S(2)}) collective-permute-start(bf16[32,1152]{1,0:T(8,128)(2,1)} %get-tuple-element.18), channel_id=1, source_target_pairs={{320,0},{352,32},{384,64},{416,96},{448,128},{480,160},{0,192},{32... | collective-permute-start | bytes 221192 | tf_op jit(solution)/shard_map/ppermute | solution.py:21
  116.9 19.4 %copy-start.19 = (s32[16]{0:T(128)S(1)}, s32[16]{0:T(128)}, u32[]{:S(2)}) copy-start(s32[16]{0:T(128)} %constant.55.clone) | copy-start | bytes 196
  116.9 21.4 %copy-start.18 = (s32[32]{0:T(128)S(1)}, s32[32]{0:T(128)}, u32[]{:S(2)}) copy-start(s32[32]{0:T(128)} %param.15) | copy-start | bytes 388
  116.9 21.4 %all-to-all-start = ((bf16[16,32,1152]{2,1,0:T(8,128)(2,1)}), bf16[16,32,1152]{2,1,0:T(8,128)(2,1)S(1)}, u32[]{:S(2)}, u32[]{:S(2)}) async-start(bf16[16,32,1152]{2,1,0:T(8,128)(2,1)} %broadcast_in_dim.4), calls=%async_computation | async-start | bytes 2359296 | tf_op jit(solution)/shard_map/all_to_all | solution.py:348
  131.1 32.9 %collective-permute-start.22 = (bf16[160,1152]{1,0:T(8,128)(2,1)}, bf16[160,1152]{1,0:T(8,128)(2,1)}, u32[]{:S(2)}, u32[]{:S(2)}) collective-permute-start(bf16[160,1152]{1,0:T(8,128)(2,1)} %get-tuple-element.34), channel_id=1, source_target_pairs={{32,0},{64,32},{96,64},{128,96},{160,128},{192,160},{224,192},{256... | collective-permute-start | bytes 1105928 | tf_op jit(solution)/shard_map/ppermute | solution.py:21
  136.4 29.4 %collective-permute-start.23 = (bf16[160,1152]{1,0:T(8,128)(2,1)}, bf16[160,1152]{1,0:T(8,128)(2,1)}, u32[]{:S(2)}, u32[]{:S(2)}) collective-permute-start(bf16[160,1152]{1,0:T(8,128)(2,1)} %get-tuple-element.34), channel_id=1, source_target_pairs={{480,0},{0,32},{32,64},{64,96},{96,128},{128,160},{160,192},{192,2... | collective-permute-start | bytes 1105928 | tf_op jit(solution)/shard_map/ppermute | solution.py:21
  138.9 12.7 %all-to-all-start.1 = ((s32[16,1,32]{2,1,0:T(1,128)}), s32[16,1,32]{2,1,0:T(1,128)}, u32[]{:S(2)}, u32[]{:S(2)}) async-start(s32[16,1,32]{2,1,0:T(1,128)} %broadcast_in_dim.5), calls=%async_computation.1 | async-start | bytes 16384 | tf_op jit(solution)/shard_map/all_to_all | solution.py:348
  146.2 28.9 %collective-permute-start.25 = (bf16[512,1152]{1,0:T(8,128)(2,1)S(1)}, bf16[512,1152]{1,0:T(8,128)(2,1)}, u32[]{:S(2)}, u32[]{:S(2)}) collective-permute-start(bf16[512,1152]{1,0:T(8,128)(2,1)S(1)} %bitcast.14), channel_id=1, source_target_pairs={{0,1},{1,0},{2,3},{3,2},{4,5},{5,4},{6,7},{7,6},{8,9},{9,8},{10,11... | collective-permute-start | bytes 3538952 | tf_op jit(solution)/shard_map/ppermute | solution.py:25
  155.0 13.7 %copy-start.6 = (s32[512,1]{1,0:T(8,128)S(1)}, s32[512,1]{1,0:T(8,128)}, u32[]{:S(2)}) copy-start(s32[512,1]{1,0:T(8,128)} %add.91.ids_ref) | copy-start | bytes 6148
  155.0 20.0 %collective-permute-start.26 = (s32[1,512]{1,0:T(1,128)S(1)}, s32[1,512]{1,0:T(1,128)S(1)}, u32[]{:S(2)}, u32[]{:S(2)}) collective-permute-start(s32[1,512]{1,0:T(1,128)S(1)} %reshape.83.positives_ref), channel_id=1, source_target_pairs={{0,1},{1,0},{2,3},{3,2},{4,5},{5,4},{6,7},{7,6},{8,9},{9,8},{10,11... | collective-permute-start | bytes 6152 | tf_op jit(solution)/shard_map/ppermute | solution.py:25
  157.1 10.9 %collective-permute-start.24 = (bf16[32,1152]{1,0:T(8,128)(2,1)}, bf16[32,1152]{1,0:T(8,128)(2,1)S(1)}, u32[]{:S(2)}, u32[]{:S(2)}) collective-permute-start(bf16[32,1152]{1,0:T(8,128)(2,1)} %collective-permute-done.20), channel_id=1, source_target_pairs={{64,0},{96,32},{128,64},{160,96},{192,128},{224,160},{256,192},{28... | collective-permute-start | bytes 221192 | tf_op jit(solution)/shard_map/ppermute | solution.py:21
  170.0 5.1 %copy-start.15 = (bf16[512,1152]{1,0:T(8,128)(2,1)S(1)}, bf16[512,1152]{1,0:T(8,128)(2,1)}, u32[]{:S(2)}) copy-start(bf16[512,1152]{1,0:T(8,128)(2,1)} %constant_dynamic-update-slice_fusion.23.texts_ref) | copy-start | bytes 3538948
  181.5 22.4 %collective-permute-start.27 = (bf16[512,1152]{1,0:T(8,128)(2,1)S(1)}, bf16[512,1152]{1,0:T(8,128)(2,1)S(1)}, u32[]{:S(2)}, u32[]{:S(2)}) collective-permute-start(bf16[512,1152]{1,0:T(8,128)(2,1)S(1)} %get-tuple-element.22), channel_id=1, source_target_pairs={{0,1},{1,0},{2,3},{3,2},{4,5},{5,4},{6,7},{7,6},{8,9},{9,8},{10,11... | collective-permute-start | bytes 3538952 | tf_op jit(solution)/shard_map/ppermute | solution.py:25
  183.4 13.0 %collective-permute-start.29 = (bf16[160,1152]{1,0:T(8,128)(2,1)S(1)}, bf16[160,1152]{1,0:T(8,128)(2,1)S(1)}, u32[]{:S(2)}, u32[]{:S(2)}) collective-permute-start(bf16[160,1152]{1,0:T(8,128)(2,1)S(1)} %get-tuple-element.26), channel_id=1, source_target_pairs={{32,0},{64,32},{96,64},{128,96},{160,128},{192,160},{224,192},{256... | collective-permute-start | bytes 1105928 | tf_op jit(solution)/shard_map/ppermute | solution.py:21
  188.0 14.8 %collective-permute-start.28 = (bf16[160,1152]{1,0:T(8,128)(2,1)S(1)}, bf16[160,1152]{1,0:T(8,128)(2,1)S(1)}, u32[]{:S(2)}, u32[]{:S(2)}) collective-permute-start(bf16[160,1152]{1,0:T(8,128)(2,1)S(1)} %get-tuple-element.25), channel_id=1, source_target_pairs={{480,0},{0,32},{32,64},{64,96},{96,128},{128,160},{160,192},{192,2... | collective-permute-start | bytes 1105928 | tf_op jit(solution)/shard_map/ppermute | solution.py:21
  189.9 32.2 %collective-permute-start.32 = (bf16[32,1152]{1,0:T(8,128)(2,1)}, bf16[32,1152]{1,0:T(8,128)(2,1)}, u32[]{:S(2)}, u32[]{:S(2)}) collective-permute-start(bf16[32,1152]{1,0:T(8,128)(2,1)} %get-tuple-element.27), channel_id=1, source_target_pairs={{448,0},{480,32},{0,64},{32,96},{64,128},{96,160},{128,192},{160,2... | collective-permute-start | bytes 221192 | tf_op jit(solution)/shard_map/ppermute | solution.py:21
  205.3 30.8 %copy-start.17 = (s32[1152]{0:T(1024)S(1)}, s32[1152]{0:T(1024)}, u32[]{:S(2)}) copy-start(s32[1152]{0:T(1024)} %copy-done.16) | copy-start | bytes 13828
  205.3 45.0 %all-to-all-start.2 = ((bf16[16,32,1152]{2,1,0:T(8,128)(2,1)}), bf16[16,32,1152]{2,1,0:T(8,128)(2,1)S(1)}, u32[]{:S(2)}, u32[]{:S(2)}) async-start(bf16[16,32,1152]{2,1,0:T(8,128)(2,1)} %bitcast.17), calls=%async_computation.2 | async-start | bytes 2359296 | tf_op jit(solution)/shard_map/all_to_all | solution.py:400
  213.2 23.8 %collective-permute-start.30 = (bf16[32,1152]{1,0:T(8,128)(2,1)S(1)}, bf16[32,1152]{1,0:T(8,128)(2,1)S(1)}, u32[]{:S(2)}, u32[]{:S(2)}) collective-permute-start(bf16[32,1152]{1,0:T(8,128)(2,1)S(1)} %get-tuple-element.32), channel_id=1, source_target_pairs={{416,0},{448,32},{480,64},{0,96},{32,128},{64,160},{96,192},{128,2... | collective-permute-start | bytes 221192 | tf_op jit(solution)/shard_map/ppermute | solution.py:21
  215.2 21.8 %collective-permute-start.31 = (bf16[32,1152]{1,0:T(8,128)(2,1)S(1)}, bf16[32,1152]{1,0:T(8,128)(2,1)S(1)}, u32[]{:S(2)}, u32[]{:S(2)}) collective-permute-start(bf16[32,1152]{1,0:T(8,128)(2,1)S(1)} %get-tuple-element.31), channel_id=1, source_target_pairs={{96,0},{128,32},{160,64},{192,96},{224,128},{256,160},{288,192},{3... | collective-permute-start | bytes 221192 | tf_op jit(solution)/shard_map/ppermute | solution.py:21
  223.1 14.1 %collective-permute-start.33 = (bf16[32,1152]{1,0:T(8,128)(2,1)S(1)}, bf16[32,1152]{1,0:T(8,128)(2,1)S(1)}, u32[]{:S(2)}, u32[]{:S(2)}) collective-permute-start(bf16[32,1152]{1,0:T(8,128)(2,1)S(1)} %fusion.1), channel_id=1, source_target_pairs={{320,0},{352,32},{384,64},{416,96},{448,128},{480,160},{0,192},{32... | collective-permute-start | bytes 221192 | tf_op jit(solution)/shard_map/ppermute | solution.py:21
  227.3 18.4 %collective-permute-start.34 = (bf16[32,1152]{1,0:T(8,128)(2,1)S(1)}, bf16[32,1152]{1,0:T(8,128)(2,1)S(1)}, u32[]{:S(2)}, u32[]{:S(2)}) collective-permute-start(bf16[32,1152]{1,0:T(8,128)(2,1)S(1)} %get-tuple-element.30), channel_id=1, source_target_pairs={{192,0},{224,32},{256,64},{288,96},{320,128},{352,160},{384,192},{... | collective-permute-start | bytes 221192 | tf_op jit(solution)/shard_map/ppermute | solution.py:21
  251.2 3.2 %copy-start.12 = (bf16[1152,16]{0,1:T(8,128)(2,1)S(1)}, bf16[1152,16]{0,1:T(8,128)(2,1)}, u32[]{:S(2)}) copy-start(bf16[1152,16]{0,1:T(8,128)(2,1)} %param.11) | copy-start | bytes 110596
  (10 other events, 19.5 us)

commit v2 on v1

v2 whole, which is shorter than its diff:
```python
import jax
import jax.numpy as jnp
from jax import lax
from jax.experimental import pallas as pl
from jax.experimental.pallas import tpu as pltpu
from jax.sharding import Mesh, PartitionSpec as P

EPSILON = 1e-06
INTERPRET = False
BF, F32 = jnp.bfloat16, jnp.float32
NZH, NZL, NYH, NYL, NX, NC = 4, 4, 2, 2, 4, 2
NZ = NZH * NZL
Z = ("z_hi", "z_lo")
XY = ("y_hi", "y_lo", "x")
TAIL = 128
VMEM = pltpu.VMEM
SMEM = pltpu.SMEM


def take_from(values, axis, distance, size):
    return lax.ppermute(values, axis, [((i + distance) % size, i) for i in range(size)])


def swap_cores(values):
    return lax.ppermute(values, "core", [(0, 1), (1, 0)])


def nt_dot(a, b):
    return lax.dot_general(a, b, (((1,), (1,)), ((), ())), preferred_element_type=F32)


def tn_dot(a, b):
    return lax.dot_general(a, b, (((0,), (0,)), ((), ())), preferred_element_type=F32)


def nn_dot(a, b):
    return jnp.dot(a, b, preferred_element_type=F32)


def call(kernel, out_shape, *, flops=0, transcendentals=0, moved=0, limit=16, **kw):
    return pl.pallas_call(
        kernel,
        out_shape=out_shape,
        compiler_params=pltpu.CompilerParams(vmem_limit_bytes=limit * 1024 * 1024),
        cost_estimate=pl.CostEstimate(
            flops=flops, transcendentals=transcendentals, bytes_accessed=moved
        ),
        interpret=INTERPRET,
        **kw,
    )


def attention_forward(tiles, query_key, spread, patches):
    rows, width = tiles.shape
    heads = query_key.shape[1]
    images = rows // patches
    step = min(8, images)

    def kernel(tile_ref, qk_ref, spread_ref, attend_ref, pooled_ref):
        tile = tile_ref[...]
        scores = nn_dot(tile, qk_ref[...]).reshape(step, patches, heads)
        top = jnp.max(scores, axis=1, keepdims=True)
        raised = jnp.exp(scores - top)
        attend = raised / jnp.sum(raised, axis=1, keepdims=True)
        attend = attend.reshape(step * patches, heads)
        attend_ref[...] = attend
        wide = nn_dot(attend.astype(BF), spread_ref[...])
        mixed = (wide * tile.astype(F32)).reshape(step, patches, width)
        pooled_ref[...] = jnp.sum(mixed, axis=1)

    return call(
        kernel,
        (
            jax.ShapeDtypeStruct((rows, heads), F32),
            jax.ShapeDtypeStruct((images, width), F32),
        ),
        grid=(images // step,),
        in_specs=[
            pl.BlockSpec((step * patches, width), lambda i: (i, 0)),
            pl.BlockSpec((width, heads), lambda i: (0, 0)),
            pl.BlockSpec((heads, width), lambda i: (0, 0)),
        ],
        out_specs=[
            pl.BlockSpec((step * patches, heads), lambda i: (i, 0)),
            pl.BlockSpec((step, width), lambda i: (i, 0)),
        ],
        flops=4 * rows * width * 128,
        moved=rows * width * 2,
    )(tiles, query_key, spread)


def attention_backward(tiles, attend, dpooled, query_key_t, spread, gather, patches):
    rows, width = tiles.shape
    heads = attend.shape[1]
    images = rows // patches
    step = min(8, images)

    def kernel(tile_ref, attend_ref, dpooled_ref, qkt_ref, spread_ref, gather_ref, out_ref):
        block = step * patches
        upstream = dpooled_ref[...]
        upstream = jnp.broadcast_to(upstream[:, None, :], (step, patches, width))
        upstream = upstream.reshape(block, width)
        product = tile_ref[...].astype(F32) * upstream
        high = product.astype(BF)
        low = (product - high.astype(F32)).astype(BF)
        dattend = nn_dot(high, gather_ref[...]) + nn_dot(low, gather_ref[...])
        attend = attend_ref[...]
        weighted = (attend * dattend).reshape(step, patches, heads)
        mean = jnp.broadcast_to(
            jnp.sum(weighted, axis=1, keepdims=True), (step, patches, heads)
        ).reshape(block, heads)
        dscores = attend * (dattend - mean)
        direct = nn_dot(attend.astype(BF), spread_ref[...]) * upstream
        through = nn_dot(dscores.astype(BF), qkt_ref[...])
        out_ref[...] = (direct + through).astype(BF)

    return call(
        kernel,
        jax.ShapeDtypeStruct((rows, width), BF),
        grid=(images // step,),
        in_specs=[
            pl.BlockSpec((step * patches, width), lambda i: (i, 0)),
            pl.BlockSpec((step * patches, heads), lambda i: (i, 0)),
            pl.BlockSpec((step, width), lambda i: (i, 0)),
            pl.BlockSpec((heads, width), lambda i: (0, 0)),
            pl.BlockSpec((heads, width), lambda i: (0, 0)),
            pl.BlockSpec((width, heads), lambda i: (0, 0)),
        ],
        out_specs=pl.BlockSpec((step * patches, width), lambda i: (i, 0)),
        flops=8 * rows * width * 128,
        moved=rows * width * 4,
    )(tiles, attend, dpooled, query_key_t, spread, gather)


def project(core, rows, matrix, partners=None):
    count, width = rows.shape
    half = width // 2
    tail = 0 if partners is None else TAIL

    def kernel(core_ref, rows_ref, *refs):
        matrix_refs, refs = refs[: len(matrix)], refs[len(matrix) :]
        pre_ref, unit_ref = refs[-2:]
        line = rows_ref[...].astype(BF)
        if len(matrix) == 1:
            pre = nt_dot(line, matrix_refs[0][...])
            pre_ref[...] = pre
        else:
            first = core_ref[0] == 0
            mine, theirs = nt_dot(line, matrix_refs[0][...]), nt_dot(line, matrix_refs[1][...])
            pre_ref[:, :half] = jnp.where(first, mine, theirs)
            pre_ref[:, half:] = jnp.where(first, theirs, mine)
            pre = pre_ref[...]
        inverse = lax.rsqrt(jnp.sum(pre * pre, axis=-1, keepdims=True) + EPSILON)
        unit_ref[:, :width] = (pre * inverse).astype(BF)
        if tail:
            index = refs[0][...]
            lane = lax.broadcasted_iota(jnp.int32, (count, tail), 1)
            digit = jnp.where(lane == 0, index >> 7, jnp.where(lane == 1, index & 127, 0))
            unit_ref[:, width:] = digit.astype(F32).astype(BF)

    operands = [core, rows, *matrix] + ([] if partners is None else [partners])
    return call(
        kernel,
        (
            jax.ShapeDtypeStruct((count, width), F32),
            jax.ShapeDtypeStruct((count, width + tail), BF),
        ),
        in_specs=[pl.BlockSpec(memory_space=SMEM)]
        + [pl.BlockSpec(memory_space=VMEM)] * (len(operands) - 1),
        out_specs=[pl.BlockSpec(memory_space=VMEM)] * 2,
        flops=2 * count * width * width,
        moved=2 * width * width,
    )(*operands)


def project_back(core, pre, parts, matrix, out_dtype):
    count, width = pre.shape
    half = width // 2

    def kernel(core_ref, pre_ref, parts_ref, *refs):
        matrix_refs, out_ref = refs[:-1], refs[-1]
        upstream = parts_ref[0].astype(F32)
        for i in range(1, parts_ref.shape[0]):
            upstream += parts_ref[i].astype(F32)
        pre = pre_ref[...]
        inverse = lax.rsqrt(jnp.sum(pre * pre, axis=-1, keepdims=True) + EPSILON)
        along = jnp.sum(pre * upstream, axis=-1, keepdims=True)
        dpre = inverse * upstream - inverse**3 * pre * along
        if len(matrix) == 1:
            total = nn_dot(dpre.astype(BF), matrix_refs[0][...])
        else:
            first = core_ref[0] == 0
            low, high = dpre[:, :half], dpre[:, half:]
            mine = jnp.where(first, low, high).astype(BF)
            theirs = jnp.where(first, high, low).astype(BF)
            total = nn_dot(mine, matrix_refs[0][...]) + nn_dot(theirs, matrix_refs[1][...])
        out_ref[...] = total.astype(BF).astype(out_dtype)

    return call(
        kernel,
        jax.ShapeDtypeStruct((count, width), out_dtype),
        in_specs=[pl.BlockSpec(memory_space=SMEM)]
        + [pl.BlockSpec(memory_space=VMEM)] * (2 + len(matrix)),
        out_specs=pl.BlockSpec(memory_space=VMEM),
        flops=2 * count * width * width,
        moved=2 * width * width,
    )(core, pre, parts, *matrix)


def slopes(scalar_ref, texts, ids, lines, width):
    coolness, offset, scale = scalar_ref[0], scalar_ref[1], scalar_ref[2]
    logits = coolness * nt_dot(lines[:, :width], texts) + offset
    tail = lines[:, width:].astype(F32)
    match = tail[:, 0:1] * 128.0 + tail[:, 1:2] == ids
    steep = jnp.where(match, -scale, scale)
    slope = steep / (1.0 + jnp.exp(jnp.where(match, logits, -logits)))
    return slope.astype(BF)


def first_tile(scalars, pieces, text_ids, images):
    text_count = sum(piece.shape[0] for piece in pieces)
    image_count, width = images.shape[0], images.shape[1] - TAIL
    block = min(256, image_count)

    def kernel(scalar_ref, *refs):
        piece_refs = refs[: len(pieces)]
        ids_ref, images_ref, texts_ref, image_part_ref, total_ref = refs[len(pieces) :]
        start = 0
        for ref in piece_refs:
            texts_ref[start : start + ref.shape[0], :] = ref[...]
            start += ref.shape[0]
        ids = ids_ref[...]
        for i in range(image_count // block):
            rows = slice(i * block, (i + 1) * block)
            lines = images_ref[rows, :]
            weighted = slopes(scalar_ref, texts_ref[...], ids, lines, width)
            term = tn_dot(weighted, lines[:, :width])
            if i == 0:
                total_ref[...] = term
            else:
                total_ref[...] += term
            image_part_ref[rows, :] = nn_dot(weighted, texts_ref[...])

    return call(
        kernel,
        (
            jax.ShapeDtypeStruct((text_count, width), BF),
            jax.ShapeDtypeStruct((image_count, width), F32),
            jax.ShapeDtypeStruct((text_count, width), F32),
        ),
        in_specs=[pl.BlockSpec(memory_space=SMEM)]
        + [pl.BlockSpec(memory_space=VMEM)] * (2 + len(pieces)),
        out_specs=[pl.BlockSpec(memory_space=VMEM)] * 3,
        flops=6 * text_count * image_count * width,
        transcendentals=text_count * image_count,
        moved=2 * width * (text_count + 2 * image_count),
    )(scalars, *pieces, text_ids, images)


def second_tile(scalars, texts, text_ids, images, text_sum, cuts):
    text_count, width = texts.shape
    image_count = images.shape[0]
    block = min(256, image_count)

    def kernel(scalar_ref, texts_ref, ids_ref, images_ref, sum_ref, weighted_ref, *refs):
        out_refs, total_ref = refs[:-1], refs[-1]
        ids = ids_ref[...]
        for i in range(image_count // block):
            rows = slice(i * block, (i + 1) * block)
            lines = images_ref[rows, :]
            weighted = slopes(scalar_ref, texts_ref[...], ids, lines, width)
            weighted_ref[rows, :] = weighted
            term = tn_dot(weighted, lines[:, :width])
            if i == 0:
                total_ref[...] = sum_ref[...] + term
            else:
                total_ref[...] += term
        start = 0
        for ref in out_refs:
            ref[...] = total_ref[start : start + ref.shape[0], :].astype(ref.dtype)
            start += ref.shape[0]

    return call(
        kernel,
        (
            jax.ShapeDtypeStruct((image_count, text_count), BF),
            jax.ShapeDtypeStruct((cuts[0], width), F32),
            *(jax.ShapeDtypeStruct((size, width), BF) for size in cuts[1:]),
        ),
        in_specs=[pl.BlockSpec(memory_space=SMEM)] + [pl.BlockSpec(memory_space=VMEM)] * 4,
        out_specs=[pl.BlockSpec(memory_space=VMEM)] * (1 + len(cuts)),
        scratch_shapes=[pltpu.VMEM((text_count, width), F32)],
        flops=4 * text_count * image_count * width,
        transcendentals=text_count * image_count,
        moved=2 * width * (text_count + 2 * image_count),
    )(scalars, texts, text_ids, images, text_sum)


def image_terms(weighted, texts):
    image_count, text_count = weighted.shape
    width = texts.shape[1]

    def kernel(weighted_ref, texts_ref, out_ref):
        out_ref[...] = nn_dot(weighted_ref[...], texts_ref[...]).astype(BF)

    return call(
        kernel,
        jax.ShapeDtypeStruct((image_count, width), BF),
        in_specs=[pl.BlockSpec(memory_space=VMEM)] * 2,
        out_specs=pl.BlockSpec(memory_space=VMEM),
        flops=2 * text_count * image_count * width,
        moved=2 * width * (text_count + image_count),
    )(weighted, texts)


def add_up(total, parts):
    sizes = [len(part) for part in parts]

    def kernel(total_ref, *refs):
        out_ref = refs[-1]
        start = 0
        for cut in sorted(edges):
            rows = slice(start, cut)
            value = total_ref[rows, :]
            place = 0
            for size in sizes:
                base = 0
                for ref in refs[place : place + size]:
                    end = base + ref.shape[0]
                    if base <= start and cut <= end:
                        value = value + ref[start - base : cut - base, :].astype(F32)
                    base = end
                place += size
            out_ref[rows, :] = value.astype(BF)
            start = cut

    edges = set()
    for part in parts:
        end = 0
        for array in part:
            end += array.shape[0]
            edges.add(end)
    flat = [array for part in parts for array in part]
    return call(
        kernel,
        jax.ShapeDtypeStruct(total.shape, BF),
        in_specs=[pl.BlockSpec(memory_space=VMEM)] * (1 + len(flat)),
        out_specs=pl.BlockSpec(memory_space=VMEM),
        flops=total.size,
        moved=8 * total.size,
    )(total, *flat)


def to_all(values, axes, size):
    spread = jnp.broadcast_to(values[None], (size,) + values.shape)
    return lax.all_to_all(spread, axes, 0, 0, tiled=True)


def gather_matrix(piece):
    return to_all(piece, ("y_lo", "x"), 8).reshape(-1, piece.shape[1])


def shards(
    picture_tiles,
    query_key_product,
    pooling_exit_matrix,
    caption_embedding,
    caption_head_matrix,
    matching_caption_index,
    natural_inverse_coolness,
    score_offset,
    objective_adjoint,
):
    images, patches, width = picture_tiles.shape
    heads = query_key_product.shape[1]
    z_lo, y_hi, y_lo, x, core = (lax.axis_index(a) for a in ("z_lo", "y_hi", "y_lo", "x", "core"))
    place = core.astype(jnp.int32).reshape(1)
    count = caption_embedding.shape[0]

    exit_matrix = lax.all_gather(
        pooling_exit_matrix.T, ("core", "y_lo", "x"), axis=0, tiled=True
    )
    text_own = gather_matrix(caption_head_matrix.T)

    head_of = jnp.arange(width, dtype=jnp.int32) // (width // heads)
    spread = (head_of[None, :] == jnp.arange(heads, dtype=jnp.int32)[:, None]).astype(BF)
    gather = (head_of[:, None] == jnp.arange(heads, dtype=jnp.int32)[None, :]).astype(BF)
    tiles = picture_tiles.reshape(images * patches, width)
    attend, pooled = attention_forward(tiles, query_key_product, spread, patches)
    txt = (y_lo * NX + x) * NC + core
    kind = (z_lo + jnp.array([0, 1, 3, 2], jnp.int32)) % NZL
    source = (jnp.arange(NZH, dtype=jnp.int32)[None, :] * NZL + kind[:, None]).reshape(-1)
    first = (txt * (NZ * NYH) + source * NYH + y_hi) * count
    text_ids = first[:, None] + jnp.arange(count, dtype=jnp.int32)[None, :]
    text_ids = text_ids.astype(F32).reshape(1, -1)
    coolness = jnp.exp(natural_inverse_coolness[0])
    scalars = jnp.stack([coolness, score_offset[0], coolness * objective_adjoint[0]])
    partners = matching_caption_index.reshape(-1, 1)
    text_own, pooled, attend, text_ids, scalars, gather, partners = lax.optimization_barrier(
        (text_own, pooled, attend, text_ids, scalars, gather, partners)
    )

    text_matrix = text_own, swap_cores(text_own)
    text_pre, text_unit = project(place, caption_embedding, text_matrix)
    near = to_all(text_unit, "z_hi", NZH).reshape(-1, width)

    image_pre, image_unit = project(place, pooled, (exit_matrix,), partners)
    image_unit, near = lax.optimization_barrier((image_unit, near))
    own_images = to_all(image_unit, XY, 16).reshape(-1, width + TAIL)
    cut = near.shape[0] // 2
    pieces = [
        near,
        take_from(near, Z, 1, NZ),
        take_from(near, Z, -1, NZ),
        take_from(near[:cut], Z, 2, NZ),
        take_from(near[cut:], Z, -2, NZ),
    ]
    own_images, pieces = lax.optimization_barrier((own_images, pieces))
    other_images = swap_cores(own_images)

    texts, own_part, text_sum = first_tile(scalars, pieces, text_ids, own_images)
    weighted, mine, *away = second_tile(
        scalars, texts, text_ids, other_images, text_sum, [piece.shape[0] for piece in pieces]
    )
    away = [take_from(part, Z, -d, NZ) for part, d in zip(away, (1, -1, 2, -2))]
    other_part = swap_cores(image_terms(weighted, texts))
    chip_images = add_up(own_part, [[other_part]])
    image_parts = lax.all_to_all(chip_images.reshape(16, images, width), XY, 0, 0, tiled=True)
    chip_texts = add_up(mine, [[away[0]], [away[1]], away[2:]])
    image_parts, chip_texts = lax.optimization_barrier((image_parts, chip_texts))
    text_parts = lax.all_to_all(
        chip_texts.reshape(NZH, count, width), "z_hi", 0, 0, tiled=True
    )

    dpooled = project_back(place, image_pre, image_parts, (exit_matrix,), F32)
    d_patches = attention_backward(
        tiles, attend, dpooled, query_key_product.T, spread, gather, patches
    )
    text_pre, d_patches = lax.optimization_barrier((text_pre, d_patches))
    d_text = project_back(place, text_pre, text_parts, text_matrix, BF)
    return (d_patches.reshape(images, patches, width), d_text)


def solution(mesh):
    chips = Mesh(
        mesh.devices.reshape(NZH, NZL, NYH, NYL, NX, NC),
        ("z_hi", "z_lo", "y_hi", "y_lo", "x", "core"),
    )
    img, txt = ("z_hi", "z_lo", "y_hi"), ("y_lo", "x", "core")
    return jax.shard_map(
        shards,
        mesh=chips,
        in_specs=(
            P(img + txt, None, None),
            P(),
            P(None, txt),
            P(txt + img, None),
            P(None, txt),
            P(img + txt),
            P(),
            P(),
            P(),
        ),
        out_specs=(P(img + txt, None, None), P(txt + img, None)),
        check_vma=False,
    )
```

time: 261 us -> 191 us (0.73)
  starting transfers between devices: 155 us -> 80.3 us
  waiting for transfers between devices: 25.8 us -> 50.7 us
  local copies, waits for them, and re-layouts: 35.8 us -> 18.6 us
  between operations: 3.28 us -> 16.4 us
  Pallas kernels: 31.8 us -> 21.2 us
  other arithmetic: 6.72 us -> 0.48 us
    ppermute x30 -> x8, starting transfers between devices: 125 us -> 30 us  [take_from(): lax.ppermute(values, axis, [((i + distance) % size, i) for i in range(siz...]
    all_to_all x3 -> x5, waiting for transfers between devices: 0.42 us -> 30.1 us  [the longest x3 20.4 us: to_all(): return lax.all_to_all(spread, axes, 0, 0, tiled=True)]
    all_to_all x3 -> x5, starting transfers between devices: 20.1 us -> 44 us  [the longest x3 33.1 us: to_all(): return lax.all_to_all(spread, axes, 0, 0, tiled=True)]
    unnamed x63 -> x57, local copies, waits for them, and re-layouts: 27.1 us -> 14.3 us
    ppermute x30 -> x8, waiting for transfers between devices: 25.4 us -> 14.4 us  [take_from(): lax.ppermute(values, axis, [((i + distance) % size, i) for i in range(siz...]
    ppermute x5 -> x3, waiting for transfers between devices: 0.01 us -> 5.48 us  [swap_cores(): return lax.ppermute(values, 'core', [(0, 1), (1, 0)])]
    pallas_call x2, Pallas kernels: 6.79 us -> 2 us  [project(): call(kernel, (jax.ShapeDtypeStruct((count, width), F32), jax.ShapeDtypeSt...]
    ppermute x5 -> x3, starting transfers between devices: 10.2 us -> 6.21 us  [swap_cores(): return lax.ppermute(values, 'core', [(0, 1), (1, 0)])]
  transfers between devices with their start and end apart: 38 -> 17, of which waited for: 8 -> 10; matrix products, arithmetic and copies ran while one was open for 15% -> 2% of each run, Pallas kernels for 7% -> 8%
where the time goes in v2:
time: 191 us; the launch traced here: 188 us
  starting transfers between devices  80.3 us (42%)
  waiting for transfers between devices  50.7 us (27%)
  Pallas kernels  21.2 us (11%)
  local copies, waits for them, and re-layouts  18.6 us (10%)
  between operations  16.4 us (9%)
    all_to_all x3, starting transfers between devices, to_all(): return lax.all_to_all(spread, axes, 0, 0, tiled=True)  33.1 us
    ppermute x8, starting transfers between devices, take_from(): lax.ppermute(values, axis, [((i + distance) % size, i) for i in range(siz...  30 us
    all_to_all x3, waiting for transfers between devices, to_all(): return lax.all_to_all(spread, axes, 0, 0, tiled=True)  20.4 us
    ppermute x8, waiting for transfers between devices, take_from(): lax.ppermute(values, axis, [((i + distance) % size, i) for i in range(siz...  14.4 us
    unnamed x57, local copies, waits for them, and re-layouts  14.3 us
    all_to_all x1, waiting for transfers between devices, shards(): lax.all_to_all(chip_texts.reshape(NZH, count, width), 'z_hi', 0, 0, tiled...  9.67 us
    all_to_all x1, starting transfers between devices, shards(): lax.all_to_all(chip_images.reshape(16, images, width), XY, 0, 0, tiled=True)  7.23 us
    ppermute x3, starting transfers between devices, swap_cores(): return lax.ppermute(values, 'core', [(0, 1), (1, 0)])  6.21 us
  transfers between devices with their start and end apart: 17, of which 10 were waited for; matrix products, arithmetic and copies ran while one was open for 2% of the time, Pallas kernels for 8%

profile of v2, /device:TPU:6, one launch (start us, length us, event | category | flops | bytes accessed | tf_op | source)
XLA Modules:
  0.0 187.6 jit_solution(5892422586177975073)
XLA Ops:
  7.9 2.1 %broadcast_in_dim.6 = bf16[8,72,1152]{2,1,0:T(8,128)(2,1)} broadcast(bf16[72,1152]{1,0:T(8,128)(2,1)} %bitcast.24), dimensions={1,2} | broadcast | bytes 1492992 | tf_op jit(solution)/shard_map/broadcast_in_dim | solution.py:355
  10.0 9.5 %all-to-all-start = ((bf16[8,72,1152]{2,1,0:T(8,128)(2,1)}), bf16[8,72,1152]{2,1,0:T(8,128)(2,1)S(1)}, u32[]{:S(2)}, u32[]{:S(2)}) async-start(bf16[8,72,1152]{2,1,0:T(8,128)(2,1)} %broadcast_in_dim.6), calls=%async_computation | async-start | bytes 2654208 | tf_op jit(solution)/shard_map/all_to_all | solution.py:356
  22.1 1.7 copy-done.2
  23.7 2.6 %shard_map.113 = (f32[1024,16]{1,0:T(8,128)S(1)}, f32[32,1152]{1,0:T(8,128)S(1)}) custom-call(bf16[1024,1152]{1,0:T(8,128)(2,1)S(1)} %bitcast.15, bf16[1152,16]{1,0:T(8,128)(2,1)S(1)} %copy.12.qk_ref, bf16[16,1152]{1,0:T(8,128)(2,1)S(1)} %fusion.1.spread_ref), custom_call_target="tpu_custom_call" | custom-call | flops 603979776 | bytes 2359296 | tf_op jit(solution)/shard_map/pallas_call | solution.py:71
  26.4 0.8 copy-done.5
  27.5 4.9 %all-to-all-done = bf16[8,72,1152]{2,1,0:T(8,128)(2,1)S(1)} async-done(((bf16[8,72,1152]{2,1,0:T(8,128)(2,1)}), bf16[8,72,1152]{2,1,0:T(8,128)(2,1)S(1)}, u32[]{:S(2)}, u32[]{:S(2)}) %all-to-all-start) | async-done | bytes 1327136 | tf_op jit(solution)/shard_map/all_to_all | solution.py:356
  32.3 1.9 %collective-permute-start = (bf16[576,1152]{1,0:T(8,128)(2,1)S(1)}, bf16[576,1152]{1,0:T(8,128)(2,1)S(1)}, u32[]{:S(2)}, u32[]{:S(2)}) collective-permute-start(bf16[576,1152]{1,0:T(8,128)(2,1)S(1)} %bitcast.12), channel_id=1, source_target_pairs={{0,1},{1,0},{2,3},{3,2},{4,5},{5,4},{6,7},{7,6},{8,9},{9,8},{10,11... | collective-permute-start | bytes 3981320 | tf_op jit(solution)/shard_map/ppermute | solution.py:25
  34.2 3.0 %collective-permute-done.refs_1_ = bf16[576,1152]{1,0:T(8,128)(2,1)S(1)} collective-permute-done((bf16[576,1152]{1,0:T(8,128)(2,1)S(1)}, bf16[576,1152]{1,0:T(8,128)(2,1)S(1)}, u32[]{:S(2)}, u32[]{:S(2)}) %collective-permute-start) | collective-permute-done | bytes 1327136 | tf_op jit(solution)/shard_map/ppermute | solution.py:25
  37.3 1.0 shard_map.114
  38.9 0.7 broadcast_in_dim.7
  39.7 16.5 %all-to-all-start.1 = ((bf16[4,32,1152]{2,1,0:T(8,128)(2,1)}), bf16[4,32,1152]{2,1,0:T(8,128)(2,1)S(1)}, u32[]{:S(2)}, u32[]{:S(2)}) async-start(bf16[4,32,1152]{2,1,0:T(8,128)(2,1)} %broadcast_in_dim.7), calls=%async_computation.1 | async-start | bytes 589824 | tf_op jit(solution)/shard_map/all_to_all | solution.py:356
  56.4 1.7 copy-done
  58.1 1.0 shard_map.115
  59.7 15.5 %all-to-all-done.1 = bf16[4,32,1152]{2,1,0:T(8,128)(2,1)S(1)} async-done(((bf16[4,32,1152]{2,1,0:T(8,128)(2,1)}), bf16[4,32,1152]{2,1,0:T(8,128)(2,1)S(1)}, u32[]{:S(2)}, u32[]{:S(2)}) %all-to-all-start.1) | async-done | bytes 294944 | tf_op jit(solution)/shard_map/all_to_all | solution.py:356
  75.3 1.2 broadcast_in_dim.8
  76.5 7.2 %all-to-all-start.2 = ((bf16[16,32,1280]{2,1,0:T(8,128)(2,1)}), bf16[16,32,1280]{2,1,0:T(8,128)(2,1)}, u32[]{:S(2)}, u32[]{:S(2)}) async-start(bf16[16,32,1280]{2,1,0:T(8,128)(2,1)} %broadcast_in_dim.8), calls=%async_computation.2 | async-start | bytes 2621440 | tf_op jit(solution)/shard_map/all_to_all | solution.py:356
  83.6 6.4 %collective-permute-start.1 = (bf16[128,1152]{1,0:T(8,128)(2,1)S(1)}, bf16[128,1152]{1,0:T(8,128)(2,1)S(1)}, u32[]{:S(2)}, u32[]{:S(2)}) collective-permute-start(bf16[128,1152]{1,0:T(8,128)(2,1)S(1)} %bitcast.18), channel_id=1, source_target_pairs={{32,0},{64,32},{96,64},{128,96},{160,128},{192,160},{224,192},{256... | collective-permute-start | bytes 884744 | tf_op jit(solution)/shard_map/ppermute | solution.py:21
  90.0 1.9 %collective-permute-start.2 = (bf16[128,1152]{1,0:T(8,128)(2,1)S(1)}, bf16[128,1152]{1,0:T(8,128)(2,1)S(1)}, u32[]{:S(2)}, u32[]{:S(2)}) collective-permute-start(bf16[128,1152]{1,0:T(8,128)(2,1)S(1)} %bitcast.19), channel_id=1, source_target_pairs={{480,0},{0,32},{32,64},{64,96},{96,128},{128,160},{160,192},{192,2... | collective-permute-start | bytes 884744 | tf_op jit(solution)/shard_map/ppermute | solution.py:21
  92.0 4.2 %collective-permute-start.3 = (bf16[64,1152]{1,0:T(8,128)(2,1)S(1)}, bf16[64,1152]{1,0:T(8,128)(2,1)S(1)}, u32[]{:S(2)}, u32[]{:S(2)}) collective-permute-start(bf16[64,1152]{1,0:T(8,128)(2,1)S(1)} %get-tuple-element.71), channel_id=1, source_target_pairs={{64,0},{96,32},{128,64},{160,96},{192,128},{224,160},{256,192},{28... | collective-permute-start | bytes 442376 | tf_op jit(solution)/shard_map/ppermute | solution.py:21
  96.2 2.5 %collective-permute-start.4 = (bf16[64,1152]{1,0:T(8,128)(2,1)S(1)}, bf16[64,1152]{1,0:T(8,128)(2,1)S(1)}, u32[]{:S(2)}, u32[]{:S(2)}) collective-permute-start(bf16[64,1152]{1,0:T(8,128)(2,1)S(1)} %get-tuple-element.70), channel_id=1, source_target_pairs={{448,0},{480,32},{0,64},{32,96},{64,128},{96,160},{128,192},{160,2... | collective-permute-start | bytes 442376 | tf_op jit(solution)/shard_map/ppermute | solution.py:21
  98.7 4.0 %collective-permute-done.3.refs_3_ = bf16[64,1152]{1,0:T(8,128)(2,1)S(1)} collective-permute-done((bf16[64,1152]{1,0:T(8,128)(2,1)S(1)}, bf16[64,1152]{1,0:T(8,128)(2,1)S(1)}, u32[]{:S(2)}, u32[]{:S(2)}) %collective-permute-start.3) | collective-permute-done | bytes 147488 | tf_op jit(solution)/shard_map/ppermute | solution.py:21
  103.4 4.0 %collective-permute-done.4.refs_4_ = bf16[64,1152]{1,0:T(8,128)(2,1)S(1)} collective-permute-done((bf16[64,1152]{1,0:T(8,128)(2,1)S(1)}, bf16[64,1152]{1,0:T(8,128)(2,1)S(1)}, u32[]{:S(2)}, u32[]{:S(2)}) %collective-permute-start.4) | collective-permute-done | bytes 147488 | tf_op jit(solution)/shard_map/ppermute | solution.py:21
  108.1 0.7 copy-done.18
  108.8 1.9 %collective-permute-start.5 = (bf16[512,1280]{1,0:T(8,128)(2,1)}, bf16[512,1280]{1,0:T(8,128)(2,1)S(1)}, u32[]{:S(2)}, u32[]{:S(2)}) collective-permute-start(bf16[512,1280]{1,0:T(8,128)(2,1)} %bitcast.7.refs_6_), channel_id=1, source_target_pairs={{0,1},{1,0},{2,3},{3,2},{4,5},{5,4},{6,7},{7,6},{8,9},{9,8},{10,11... | collective-permute-start | bytes 3932168 | tf_op jit(solution)/shard_map/ppermute | solution.py:25
  110.8 1.0 copy-done.19
  111.7 0.9 copy-done.23
  112.6 0.9 copy-done.25
  113.5 4.2 %shard_map.116 = (bf16[512,1152]{1,0:T(8,128)(2,1)S(1)}, f32[512,1152]{1,0:T(8,128)S(1)}, f32[512,1152]{1,0:T(8,128)S(1)}) custom-call(f32[3]{0:T(128)S(1)} %pad_maximum_fusion.scalar_ref, bf16[128,1152]{1,0:T(8,128)(2,1)S(1)} %bitcast.21, bf16[128,1152]{1,0:T(8,128)(2,1)S(1)} %collective-permute-done.1.refs_1_, bf16[128,1152]{1,0:T(8,128)(2,1)S(1)} %copy-done.19, ...), custom_call_target="tpu_custom_call" | custom-call | flops 1811939328 | bytes 3538944 | tf_op jit(solution)/shard_map/pallas_call | solution.py:244
  117.7 2.7 %shard_map.117 = (bf16[512,512]{1,0:T(8,128)(2,1)S(1)}, f32[128,1152]{1,0:T(8,128)S(1)}, bf16[128,1152]{1,0:T(8,128)(2,1)S(1)}, bf16[128,1152]{1,0:T(8,128)(2,1)...) custom-call(f32[3]{0:T(128)S(1)} %pad_maximum_fusion.scalar_ref, ...), custom_call_target="tpu_custom_call" | custom-call | flops 1207959552 | bytes 3538944 | tf_op jit(solution)/shard_map/pallas_call | solution.py:283
  120.5 0.8 shard_map.118
  121.4 2.4 %collective-permute-start.6 = (bf16[512,1152]{1,0:T(8,128)(2,1)S(1)}, bf16[512,1152]{1,0:T(8,128)(2,1)S(1)}, u32[]{:S(2)}, u32[]{:S(2)}) collective-permute-start(bf16[512,1152]{1,0:T(8,128)(2,1)S(1)} %shard_map.118), channel_id=1, source_target_pairs={{0,1},{1,0},{2,3},{3,2},{4,5},{5,4},{6,7},{7,6},{8,9},{9,8},{10,11... | collective-permute-start | bytes 3538952 | tf_op jit(solution)/shard_map/ppermute | solution.py:25
  123.8 2.5 %collective-permute-done.6.refs_0_ = bf16[512,1152]{1,0:T(8,128)(2,1)S(1)} collective-permute-done((bf16[512,1152]{1,0:T(8,128)(2,1)S(1)}, bf16[512,1152]{1,0:T(8,128)(2,1)S(1)}, u32[]{:S(2)}, u32[]{:S(2)}) %collective-permute-start.6) | collective-permute-done | bytes 1179680 | tf_op jit(solution)/shard_map/ppermute | solution.py:25
  126.5 1.0 copy-done.4
  127.5 7.2 %all-to-all-start.3 = ((bf16[16,32,1152]{2,1,0:T(8,128)(2,1)}), bf16[16,32,1152]{2,1,0:T(8,128)(2,1)}, u32[]{:S(2)}, u32[]{:S(2)}) async-start(bf16[16,32,1152]{2,1,0:T(8,128)(2,1)} %bitcast.17), calls=%async_computation.3 | async-start | bytes 2359296 | tf_op jit(solution)/shard_map/all_to_all | solution.py:428
  134.7 3.7 %collective-permute-start.7 = (bf16[128,1152]{1,0:T(8,128)(2,1)}, bf16[128,1152]{1,0:T(8,128)(2,1)S(1)}, u32[]{:S(2)}, u32[]{:S(2)}) collective-permute-start(bf16[128,1152]{1,0:T(8,128)(2,1)} %copy-done.17), channel_id=1, source_target_pairs={{480,0},{0,32},{32,64},{64,96},{96,128},{128,160},{160,192},{192,2... | collective-permute-start | bytes 884744 | tf_op jit(solution)/shard_map/ppermute | solution.py:21
  138.4 3.3 %collective-permute-start.8 = (bf16[128,1152]{1,0:T(8,128)(2,1)}, bf16[128,1152]{1,0:T(8,128)(2,1)S(1)}, u32[]{:S(2)}, u32[]{:S(2)}) collective-permute-start(bf16[128,1152]{1,0:T(8,128)(2,1)} %copy-done.16), channel_id=1, source_target_pairs={{32,0},{64,32},{96,64},{128,96},{160,128},{192,160},{224,192},{256... | collective-permute-start | bytes 884744 | tf_op jit(solution)/shard_map/ppermute | solution.py:21
  141.8 2.0 %collective-permute-start.9 = (bf16[64,1152]{1,0:T(8,128)(2,1)}, bf16[64,1152]{1,0:T(8,128)(2,1)S(1)}, u32[]{:S(2)}, u32[]{:S(2)}) collective-permute-start(bf16[64,1152]{1,0:T(8,128)(2,1)} %copy-done.21), channel_id=1, source_target_pairs={{448,0},{480,32},{0,64},{32,96},{64,128},{96,160},{128,192},{160,2... | collective-permute-start | bytes 442376 | tf_op jit(solution)/shard_map/ppermute | solution.py:21
  143.8 6.0 %collective-permute-start.10 = (bf16[64,1152]{1,0:T(8,128)(2,1)}, bf16[64,1152]{1,0:T(8,128)(2,1)S(1)}, u32[]{:S(2)}, u32[]{:S(2)}) collective-permute-start(bf16[64,1152]{1,0:T(8,128)(2,1)} %copy-done.20), channel_id=1, source_target_pairs={{64,0},{96,32},{128,64},{160,96},{192,128},{224,160},{256,192},{28... | collective-permute-start | bytes 442376 | tf_op jit(solution)/shard_map/ppermute | solution.py:21
  149.7 3.9 %collective-permute-done.9.refs_2_ = bf16[64,1152]{1,0:T(8,128)(2,1)S(1)} collective-permute-done((bf16[64,1152]{1,0:T(8,128)(2,1)}, bf16[64,1152]{1,0:T(8,128)(2,1)S(1)}, u32[]{:S(2)}, u32[]{:S(2)}) %collective-permute-start.9) | collective-permute-done | bytes 147488 | tf_op jit(solution)/shard_map/ppermute | solution.py:21
  153.6 2.4 %collective-permute-done.10.refs_3_ = bf16[64,1152]{1,0:T(8,128)(2,1)S(1)} collective-permute-done((bf16[64,1152]{1,0:T(8,128)(2,1)}, bf16[64,1152]{1,0:T(8,128)(2,1)S(1)}, u32[]{:S(2)}, u32[]{:S(2)}) %collective-permute-start.10) | collective-permute-done | bytes 147488 | tf_op jit(solution)/shard_map/ppermute | solution.py:21
  156.0 0.9 shard_map.120
  156.9 3.7 %all-to-all-start.4 = ((bf16[4,32,1152]{2,1,0:T(8,128)(2,1)}), bf16[4,32,1152]{2,1,0:T(8,128)(2,1)S(1)}, u32[]{:S(2)}, u32[]{:S(2)}) async-start(bf16[4,32,1152]{2,1,0:T(8,128)(2,1)} %bitcast.11), calls=%async_computation.4 | async-start | bytes 589824 | tf_op jit(solution)/shard_map/all_to_all | solution.py:431
  160.6 1.7 copy-done.1
  162.3 0.9 copy-done.10
  163.2 2.2 %shard_map.121.dpooled_ref = f32[32,1152]{1,0:T(8,128)S(1)} custom-call(s32[1]{0:T(128)} %bitcast.core_ref, f32[32,1152]{1,0:T(8,128)S(1)} %copy-done.10, bf16[16,32,1152]{2,1,0:T(8,128)(2,1)} %all-to-all-done.3.parts_ref, bf16[1152,1152]{1,0:T(8,128)(2,1)S(1)} %copy-done.1), custom_call_target="tpu_custom_call" | custom-call | flops 84934656 | bytes 2654208 | tf_op jit(solution)/shard_map/pallas_call | solution.py:199
  165.5 4.2 %shard_map.122 = bf16[1024,1152]{1,0:T(8,128)(2,1)} custom-call(bf16[1024,1152]{1,0:T(8,128)(2,1)S(1)} %bitcast.16, f32[1024,16]{1,0:T(8,128)S(1)} %copy-done.6, f32[32,1152]{1,0:T(8,128)S(1)} %shard_map.121.dpooled_ref, bf16[16,1152]{1,0:T(8,128)(2,1)S(1)} %bitcast.22, bf16[16,1152]{1,0:T(8,128)(2,1)S(1)} %copy-done.8, bf16[1152,16]{1,0:T(8,128)(2,1)S(1)} %fusion.gather_ref), custom_call_target="tpu_custom_call" | custom-call | flops 1207959552 | bytes 4718592 | tf_op jit(solution)/shard_map/pallas_call | solution.py:117
  169.6 9.7 %all-to-all-done.4.parts_ref = bf16[4,32,1152]{2,1,0:T(8,128)(2,1)S(1)} async-done(((bf16[4,32,1152]{2,1,0:T(8,128)(2,1)}), bf16[4,32,1152]{2,1,0:T(8,128)(2,1)S(1)}, u32[]{:S(2)}, u32[]{:S(2)}) %all-to-all-start.4) | async-done | bytes 294944 | tf_op jit(solution)/shard_map/all_to_all | solution.py:431
  179.3 1.4 shard_map.123
  (69 shorter events, 4.7 us)
Async XLA Ops:
  7.2 49.2 %all-gather.2.cloned.1.call-start = ((), (), s32[]{:S(2)}) async-start(), calls=%async_computation.5 | async-start | bytes 2820096 | tf_op jit(solution)/shard_map/all_gather | solution.py:380
  10.0 9.5 %copy-start.13 = (bf16[1152,16]{0,1:T(8,128)(2,1)S(1)}, bf16[1152,16]{0,1:T(8,128)(2,1)}, u32[]{:S(2)}) copy-start(bf16[1152,16]{0,1:T(8,128)(2,1)} %param.11) | copy-start | bytes 110596
  10.0 9.7 %copy-start.27 = (s32[4]{0:T(128)S(1)}, s32[4]{0:T(128)}, u32[]{:S(2)}) copy-start(s32[4]{0:T(128)} %constant.53.clone) | copy-start | bytes 52
  10.0 22.3 %all-to-all-start = ((bf16[8,72,1152]{2,1,0:T(8,128)(2,1)}), bf16[8,72,1152]{2,1,0:T(8,128)(2,1)S(1)}, u32[]{:S(2)}, u32[]{:S(2)}) async-start(bf16[8,72,1152]{2,1,0:T(8,128)(2,1)} %broadcast_in_dim.6), calls=%async_computation | async-start | bytes 2654208 | tf_op jit(solution)/shard_map/all_to_all | solution.py:356
  22.1 4.3 %copy-start.7 = (bf16[16,1152]{1,0:T(8,128)(2,1)}, bf16[16,1152]{1,0:T(8,128)(2,1)S(1)}, u32[]{:S(2)}) copy-start(bf16[16,1152]{1,0:T(8,128)(2,1)S(1)} %fusion.1.spread_ref) | copy-start | bytes 110596
  22.1 1.7 copy-start.2
  23.7 13.5 %copy-start.15 = (bf16[32,1152]{1,0:T(8,128)(2,1)S(1)}, bf16[32,1152]{1,0:T(8,128)(2,1)}, u32[]{:S(2)}) copy-start(bf16[32,1152]{1,0:T(8,128)(2,1)} %rows_ref.1) | copy-start | bytes 221188
  26.3 0.8 copy-start.5
  32.3 4.9 %collective-permute-start = (bf16[576,1152]{1,0:T(8,128)(2,1)S(1)}, bf16[576,1152]{1,0:T(8,128)(2,1)S(1)}, u32[]{:S(2)}, u32[]{:S(2)}) collective-permute-start(bf16[576,1152]{1,0:T(8,128)(2,1)S(1)} %bitcast.12), channel_id=1, source_target_pairs={{0,1},{1,0},{2,3},{3,2},{4,5},{5,4},{6,7},{7,6},{8,9},{9,8},{10,11... | collective-permute-start | bytes 3981320 | tf_op jit(solution)/shard_map/ppermute | solution.py:25
  37.3 18.9 %copy-start.26 = (s32[32]{0:T(128)S(1)}, s32[32]{0:T(128)}, u32[]{:S(2)}) copy-start(s32[32]{0:T(128)} %param.15) | copy-start | bytes 388
  38.3 0.7 copy-start.11
  39.7 35.6 %all-to-all-start.1 = ((bf16[4,32,1152]{2,1,0:T(8,128)(2,1)}), bf16[4,32,1152]{2,1,0:T(8,128)(2,1)S(1)}, u32[]{:S(2)}, u32[]{:S(2)}) async-start(bf16[4,32,1152]{2,1,0:T(8,128)(2,1)} %broadcast_in_dim.7), calls=%async_computation.1 | async-start | bytes 589824 | tf_op jit(solution)/shard_map/all_to_all | solution.py:356
  56.4 1.7 copy-start
  59.1 0.6 copy-start.9
  76.5 32.4 %all-to-all-start.2 = ((bf16[16,32,1280]{2,1,0:T(8,128)(2,1)}), bf16[16,32,1280]{2,1,0:T(8,128)(2,1)}, u32[]{:S(2)}, u32[]{:S(2)}) async-start(bf16[16,32,1280]{2,1,0:T(8,128)(2,1)} %broadcast_in_dim.8), calls=%async_computation.2 | async-start | bytes 2621440 | tf_op jit(solution)/shard_map/all_to_all | solution.py:356
  83.6 24.5 %collective-permute-start.1 = (bf16[128,1152]{1,0:T(8,128)(2,1)S(1)}, bf16[128,1152]{1,0:T(8,128)(2,1)S(1)}, u32[]{:S(2)}, u32[]{:S(2)}) collective-permute-start(bf16[128,1152]{1,0:T(8,128)(2,1)S(1)} %bitcast.18), channel_id=1, source_target_pairs={{32,0},{64,32},{96,64},{128,96},{160,128},{192,160},{224,192},{256... | collective-permute-start | bytes 884744 | tf_op jit(solution)/shard_map/ppermute | solution.py:21
  90.0 18.1 %collective-permute-start.2 = (bf16[128,1152]{1,0:T(8,128)(2,1)S(1)}, bf16[128,1152]{1,0:T(8,128)(2,1)S(1)}, u32[]{:S(2)}, u32[]{:S(2)}) collective-permute-start(bf16[128,1152]{1,0:T(8,128)(2,1)S(1)} %bitcast.19), channel_id=1, source_target_pairs={{480,0},{0,32},{32,64},{64,96},{96,128},{128,160},{160,192},{192,2... | collective-permute-start | bytes 884744 | tf_op jit(solution)/shard_map/ppermute | solution.py:21
  92.0 10.8 %collective-permute-start.3 = (bf16[64,1152]{1,0:T(8,128)(2,1)S(1)}, bf16[64,1152]{1,0:T(8,128)(2,1)S(1)}, u32[]{:S(2)}, u32[]{:S(2)}) collective-permute-start(bf16[64,1152]{1,0:T(8,128)(2,1)S(1)} %get-tuple-element.71), channel_id=1, source_target_pairs={{64,0},{96,32},{128,64},{160,96},{192,128},{224,160},{256,192},{28... | collective-permute-start | bytes 442376 | tf_op jit(solution)/shard_map/ppermute | solution.py:21
  96.2 11.3 %collective-permute-start.4 = (bf16[64,1152]{1,0:T(8,128)(2,1)S(1)}, bf16[64,1152]{1,0:T(8,128)(2,1)S(1)}, u32[]{:S(2)}, u32[]{:S(2)}) collective-permute-start(bf16[64,1152]{1,0:T(8,128)(2,1)S(1)} %get-tuple-element.70), channel_id=1, source_target_pairs={{448,0},{480,32},{0,64},{32,96},{64,128},{96,160},{128,192},{160,2... | collective-permute-start | bytes 442376 | tf_op jit(solution)/shard_map/ppermute | solution.py:21
  102.8 0.7 copy-start.22
  107.4 0.7 copy-start.24
  108.1 0.7 copy-start.18
  108.8 8.9 %collective-permute-start.5 = (bf16[512,1280]{1,0:T(8,128)(2,1)}, bf16[512,1280]{1,0:T(8,128)(2,1)S(1)}, u32[]{:S(2)}, u32[]{:S(2)}) collective-permute-start(bf16[512,1280]{1,0:T(8,128)(2,1)} %bitcast.7.refs_6_), channel_id=1, source_target_pairs={{0,1},{1,0},{2,3},{3,2},{4,5},{5,4},{6,7},{7,6},{8,9},{9,8},{10,11... | collective-permute-start | bytes 3932168 | tf_op jit(solution)/shard_map/ppermute | solution.py:25
  110.8 1.0 copy-start.19
  111.7 0.9 copy-start.23
  112.6 0.9 copy-start.25
  120.5 0.9 copy-start.16
  120.5 0.9 copy-start.17
  120.5 0.9 copy-start.20
  120.5 0.9 copy-start.21
  121.4 4.9 %collective-permute-start.6 = (bf16[512,1152]{1,0:T(8,128)(2,1)S(1)}, bf16[512,1152]{1,0:T(8,128)(2,1)S(1)}, u32[]{:S(2)}, u32[]{:S(2)}) collective-permute-start(bf16[512,1152]{1,0:T(8,128)(2,1)S(1)} %shard_map.118), channel_id=1, source_target_pairs={{0,1},{1,0},{2,3},{3,2},{4,5},{5,4},{6,7},{7,6},{8,9},{9,8},{10,11... | collective-permute-start | bytes 3538952 | tf_op jit(solution)/shard_map/ppermute | solution.py:25
  126.5 1.0 copy-start.4
  127.5 29.4 %all-to-all-start.3 = ((bf16[16,32,1152]{2,1,0:T(8,128)(2,1)}), bf16[16,32,1152]{2,1,0:T(8,128)(2,1)}, u32[]{:S(2)}, u32[]{:S(2)}) async-start(bf16[16,32,1152]{2,1,0:T(8,128)(2,1)} %bitcast.17), calls=%async_computation.3 | async-start | bytes 2359296 | tf_op jit(solution)/shard_map/all_to_all | solution.py:428
  134.7 21.3 %collective-permute-start.7 = (bf16[128,1152]{1,0:T(8,128)(2,1)}, bf16[128,1152]{1,0:T(8,128)(2,1)S(1)}, u32[]{:S(2)}, u32[]{:S(2)}) collective-permute-start(bf16[128,1152]{1,0:T(8,128)(2,1)} %copy-done.17), channel_id=1, source_target_pairs={{480,0},{0,32},{32,64},{64,96},{96,128},{128,160},{160,192},{192,2... | collective-permute-start | bytes 884744 | tf_op jit(solution)/shard_map/ppermute | solution.py:21
  138.4 17.6 %collective-permute-start.8 = (bf16[128,1152]{1,0:T(8,128)(2,1)}, bf16[128,1152]{1,0:T(8,128)(2,1)S(1)}, u32[]{:S(2)}, u32[]{:S(2)}) collective-permute-start(bf16[128,1152]{1,0:T(8,128)(2,1)} %copy-done.16), channel_id=1, source_target_pairs={{32,0},{64,32},{96,64},{128,96},{160,128},{192,160},{224,192},{256... | collective-permute-start | bytes 884744 | tf_op jit(solution)/shard_map/ppermute | solution.py:21
  141.8 11.9 %collective-permute-start.9 = (bf16[64,1152]{1,0:T(8,128)(2,1)}, bf16[64,1152]{1,0:T(8,128)(2,1)S(1)}, u32[]{:S(2)}, u32[]{:S(2)}) collective-permute-start(bf16[64,1152]{1,0:T(8,128)(2,1)} %copy-done.21), channel_id=1, source_target_pairs={{448,0},{480,32},{0,64},{32,96},{64,128},{96,160},{128,192},{160,2... | collective-permute-start | bytes 442376 | tf_op jit(solution)/shard_map/ppermute | solution.py:21
  143.8 12.3 %collective-permute-start.10 = (bf16[64,1152]{1,0:T(8,128)(2,1)}, bf16[64,1152]{1,0:T(8,128)(2,1)S(1)}, u32[]{:S(2)}, u32[]{:S(2)}) collective-permute-start(bf16[64,1152]{1,0:T(8,128)(2,1)} %copy-done.20), channel_id=1, source_target_pairs={{64,0},{96,32},{128,64},{160,96},{192,128},{224,160},{256,192},{28... | collective-permute-start | bytes 442376 | tf_op jit(solution)/shard_map/ppermute | solution.py:21
  156.9 22.4 %all-to-all-start.4 = ((bf16[4,32,1152]{2,1,0:T(8,128)(2,1)}), bf16[4,32,1152]{2,1,0:T(8,128)(2,1)S(1)}, u32[]{:S(2)}, u32[]{:S(2)}) async-start(bf16[4,32,1152]{2,1,0:T(8,128)(2,1)} %bitcast.11), calls=%async_computation.4 | async-start | bytes 589824 | tf_op jit(solution)/shard_map/all_to_all | solution.py:431
  160.6 1.7 copy-start.1
  162.3 0.9 copy-start.10
  163.2 2.2 %copy-start.3 = (bf16[32,32,1152]{2,1,0:T(8,128)(2,1)S(1)}, bf16[32,32,1152]{2,1,0:T(8,128)(2,1)}, u32[]{:S(2)}) copy-start(bf16[32,32,1152]{2,1,0:T(8,128)(2,1)} %param.10) | copy-start | bytes 7077892
  163.2 2.2 %copy-start.6 = (f32[1024,16]{1,0:T(8,128)S(1)}, f32[1024,16]{1,0:T(8,128)}, u32[]{:S(2)}) copy-start(f32[1024,16]{1,0:T(8,128)} %copy-done.5) | copy-start | bytes 196612
  163.2 2.2 %copy-start.8 = (bf16[16,1152]{1,0:T(8,128)(2,1)S(1)}, bf16[16,1152]{1,0:T(8,128)(2,1)}, u32[]{:S(2)}) copy-start(bf16[16,1152]{1,0:T(8,128)(2,1)} %copy-done.7) | copy-start | bytes 110596
  163.2 2.2 %copy-start.14 = (bf16[1152,16]{0,1:T(8,128)(2,1)S(1)}, bf16[1152,16]{0,1:T(8,128)(2,1)}, u32[]{:S(2)}) copy-start(bf16[1152,16]{0,1:T(8,128)(2,1)} %param.11) | copy-start | bytes 110596
  165.5 13.8 %copy-start.12 = (f32[32,1152]{1,0:T(8,128)S(1)}, f32[32,1152]{1,0:T(8,128)}, u32[]{:S(2)}) copy-start(f32[32,1152]{1,0:T(8,128)} %copy-done.11) | copy-start | bytes 442372
Sparse Core Ops, SparseCore 0:
  10.2 46.1 all-gather.1

commit v3 on v2

--- a/solution.py
+++ b/solution.py
@@ -13,6 +13,7 @@
 Z = ("z_hi", "z_lo")
 XY = ("y_hi", "y_lo", "x")
 TAIL = 128
+TEXT_OFFSETS = (-4, 0, 4, 8, -3, 1, 5, 9, -5, -1, 3, 7, 2, 6, -6, -2)
 VMEM = pltpu.VMEM
 SMEM = pltpu.SMEM
 
@@ -132,57 +133,62 @@
     )(tiles, attend, dpooled, query_key_t, spread, gather)
 
 
-def project(core, rows, matrix, partners=None):
+def unit_rows(pre):
+    inverse = lax.rsqrt(jnp.sum(pre * pre, axis=-1, keepdims=True) + EPSILON)
+    return (pre * inverse).astype(BF)
+
+
+def projected(core_ref, line, matrix_refs, pre_ref):
+    if len(matrix_refs) == 1:
+        return nt_dot(line, matrix_refs[0][...])
+    half = matrix_refs[0].shape[0]
+    first = core_ref[0] == 0
+    mine, theirs = nt_dot(line, matrix_refs[0][...]), nt_dot(line, matrix_refs[1][...])
+    pre_ref[:, :half] = jnp.where(first, mine, theirs)
+    pre_ref[:, half:] = jnp.where(first, theirs, mine)
+    return pre_ref[...]
+
+
+def unit_texts(core, pieces, matrix):
+    text_count = sum(piece.shape[0] for piece in pieces)
+    width = pieces[0].shape[1]
+    block = min(256, text_count)
+
+    def kernel(core_ref, *refs):
+        piece_refs, refs = refs[: len(pieces)], refs[len(pieces) :]
+        matrix_refs, (texts_ref, pre_ref) = refs[: len(matrix)], refs[len(matrix) :]
+        start = 0
+        for ref in piece_refs:
+            texts_ref[start : start + ref.shape[0], :] = ref[...]
+            start += ref.shape[0]
+        for i in range(text_count // block):
+            rows = slice(i * block, (i + 1) * block)
+            pre = projected(core_ref, texts_ref[rows, :], matrix_refs, pre_ref)
+            texts_ref[rows, :] = unit_rows(pre)
+
+    operands = [core, *pieces, *matrix]
+    return call(
+        kernel,
+        jax.ShapeDtypeStruct((text_count, width), BF),
+        in_specs=[pl.BlockSpec(memory_space=SMEM)]
+        + [pl.BlockSpec(memory_space=VMEM)] * (len(operands) - 1),
+        out_specs=pl.BlockSpec(memory_space=VMEM),
+        scratch_shapes=[pltpu.VMEM((block, width), F32)],
+        flops=2 * text_count * width * width,
+        moved=2 * width * width,
+    )(*operands)
+
+
+def project_back(core, rows, parts, matrix, out_dtype):
     count, width = rows.shape
     half = width // 2
-    tail = 0 if partners is None else TAIL
-
-    def kernel(core_ref, rows_ref, *refs):
-        matrix_refs, refs = refs[: len(matrix)], refs[len(matrix) :]
-        pre_ref, unit_ref = refs[-2:]
-        line = rows_ref[...].astype(BF)
-        if len(matrix) == 1:
-            pre = nt_dot(line, matrix_refs[0][...])
-            pre_ref[...] = pre
-        else:
-            first = core_ref[0] == 0
-            mine, theirs = nt_dot(line, matrix_refs[0][...]), nt_dot(line, matrix_refs[1][...])
-            pre_ref[:, :half] = jnp.where(first, mine, theirs)
-            pre_ref[:, half:] = jnp.where(first, theirs, mine)
-            pre = pre_ref[...]
-        inverse = lax.rsqrt(jnp.sum(pre * pre, axis=-1, keepdims=True) + EPSILON)
-        unit_ref[:, :width] = (pre * inverse).astype(BF)
-        if tail:
-            index = refs[0][...]
-            lane = lax.broadcasted_iota(jnp.int32, (count, tail), 1)
-            digit = jnp.where(lane == 0, index >> 7, jnp.where(lane == 1, index & 127, 0))
-            unit_ref[:, width:] = digit.astype(F32).astype(BF)
-
-    operands = [core, rows, *matrix] + ([] if partners is None else [partners])
-    return call(
-        kernel,
-        (
-            jax.ShapeDtypeStruct((count, width), F32),
-            jax.ShapeDtypeStruct((count, width + tail), BF),
-        ),
-        in_specs=[pl.BlockSpec(memory_space=SMEM)]
-        + [pl.BlockSpec(memory_space=VMEM)] * (len(operands) - 1),
-        out_specs=[pl.BlockSpec(memory_space=VMEM)] * 2,
-        flops=2 * count * width * width,
-        moved=2 * width * width,
-    )(*operands)
-
-
-def project_back(core, pre, parts, matrix, out_dtype):
-    count, width = pre.shape
-    half = width // 2
-
-    def kernel(core_ref, pre_ref, parts_ref, *refs):
-        matrix_refs, out_ref = refs[:-1], refs[-1]
+
+    def kernel(core_ref, rows_ref, parts_ref, *refs):
+        matrix_refs, (out_ref, pre_ref) = refs[: len(matrix)], refs[len(matrix) :]
+        pre = projected(core_ref, rows_ref[...].astype(BF), matrix_refs, pre_ref)
         upstream = parts_ref[0].astype(F32)
         for i in range(1, parts_ref.shape[0]):
             upstream += parts_ref[i].astype(F32)
-        pre = pre_ref[...]
         inverse = lax.rsqrt(jnp.sum(pre * pre, axis=-1, keepdims=True) + EPSILON)
         along = jnp.sum(pre * upstream, axis=-1, keepdims=True)
         dpre = inverse * upstream - inverse**3 * pre * along
@@ -202,39 +208,34 @@
         in_specs=[pl.BlockSpec(memory_space=SMEM)]
         + [pl.BlockSpec(memory_space=VMEM)] * (2 + len(matrix)),
         out_specs=pl.BlockSpec(memory_space=VMEM),
-        flops=2 * count * width * width,
+        scratch_shapes=[pltpu.VMEM((count, width), F32)],
+        flops=4 * count * width * width,
         moved=2 * width * width,
-    )(core, pre, parts, *matrix)
-
-
-def slopes(scalar_ref, texts, ids, lines, width):
+    )(core, rows, parts, *matrix)
+
+
+def slopes(scalar_ref, texts, ids, units, tail):
     coolness, offset, scale = scalar_ref[0], scalar_ref[1], scalar_ref[2]
-    logits = coolness * nt_dot(lines[:, :width], texts) + offset
-    tail = lines[:, width:].astype(F32)
+    logits = coolness * nt_dot(units, texts) + offset
+    tail = tail.astype(F32)
     match = tail[:, 0:1] * 128.0 + tail[:, 1:2] == ids
     steep = jnp.where(match, -scale, scale)
     slope = steep / (1.0 + jnp.exp(jnp.where(match, logits, -logits)))
     return slope.astype(BF)
 
 
-def first_tile(scalars, pieces, text_ids, images):
-    text_count = sum(piece.shape[0] for piece in pieces)
-    image_count, width = images.shape[0], images.shape[1] - TAIL
+def first_tile(scalars, texts, text_ids, images, matrix):
+    text_count, width = texts.shape
+    image_count = images.shape[0]
     block = min(256, image_count)
 
-    def kernel(scalar_ref, *refs):
-        piece_refs = refs[: len(pieces)]
-        ids_ref, images_ref, texts_ref, image_part_ref, total_ref = refs[len(pieces) :]
-        start = 0
-        for ref in piece_refs:
-            texts_ref[start : start + ref.shape[0], :] = ref[...]
-            start += ref.shape[0]
+    def kernel(scalar_ref, texts_ref, ids_ref, images_ref, matrix_ref, image_part_ref, total_ref):
         ids = ids_ref[...]
         for i in range(image_count // block):
             rows = slice(i * block, (i + 1) * block)
-            lines = images_ref[rows, :]
-            weighted = slopes(scalar_ref, texts_ref[...], ids, lines, width)
-            term = tn_dot(weighted, lines[:, :width])
+            units = unit_rows(nt_dot(images_ref[rows, :width], matrix_ref[...]))
+            weighted = slopes(scalar_ref, texts_ref[...], ids, units, images_ref[rows, width:])
+            term = tn_dot(weighted, units)
             if i == 0:
                 total_ref[...] = term
             else:
@@ -244,33 +245,33 @@
     return call(
         kernel,
         (
-            jax.ShapeDtypeStruct((text_count, width), BF),
             jax.ShapeDtypeStruct((image_count, width), F32),
             jax.ShapeDtypeStruct((text_count, width), F32),
         ),
-        in_specs=[pl.BlockSpec(memory_space=SMEM)]
-        + [pl.BlockSpec(memory_space=VMEM)] * (2 + len(pieces)),
-        out_specs=[pl.BlockSpec(memory_space=VMEM)] * 3,
-        flops=6 * text_count * image_count * width,
+        in_specs=[pl.BlockSpec(memory_space=SMEM)] + [pl.BlockSpec(memory_space=VMEM)] * 4,
+        out_specs=[pl.BlockSpec(memory_space=VMEM)] * 2,
+        flops=2 * image_count * width * (3 * text_count + width),
         transcendentals=text_count * image_count,
         moved=2 * width * (text_count + 2 * image_count),
-    )(scalars, *pieces, text_ids, images)
-
-
-def second_tile(scalars, texts, text_ids, images, text_sum, cuts):
+    )(scalars, texts, text_ids, images, matrix)
+
+
+def second_tile(scalars, texts, text_ids, images, matrix, text_sum, cuts):
     text_count, width = texts.shape
     image_count = images.shape[0]
     block = min(256, image_count)
 
-    def kernel(scalar_ref, texts_ref, ids_ref, images_ref, sum_ref, weighted_ref, *refs):
+    def kernel(
+        scalar_ref, texts_ref, ids_ref, images_ref, matrix_ref, sum_ref, weighted_ref, *refs
+    ):
         out_refs, total_ref = refs[:-1], refs[-1]
         ids = ids_ref[...]
         for i in range(image_count // block):
             rows = slice(i * block, (i + 1) * block)
-            lines = images_ref[rows, :]
-            weighted = slopes(scalar_ref, texts_ref[...], ids, lines, width)
+            units = unit_rows(nt_dot(images_ref[rows, :width], matrix_ref[...]))
+            weighted = slopes(scalar_ref, texts_ref[...], ids, units, images_ref[rows, width:])
             weighted_ref[rows, :] = weighted
-            term = tn_dot(weighted, lines[:, :width])
+            term = tn_dot(weighted, units)
             if i == 0:
                 total_ref[...] = sum_ref[...] + term
             else:
@@ -287,13 +288,13 @@
             jax.ShapeDtypeStruct((cuts[0], width), F32),
             *(jax.ShapeDtypeStruct((size, width), BF) for size in cuts[1:]),
         ),
-        in_specs=[pl.BlockSpec(memory_space=SMEM)] + [pl.BlockSpec(memory_space=VMEM)] * 4,
+        in_specs=[pl.BlockSpec(memory_space=SMEM)] + [pl.BlockSpec(memory_space=VMEM)] * 5,
         out_specs=[pl.BlockSpec(memory_space=VMEM)] * (1 + len(cuts)),
         scratch_shapes=[pltpu.VMEM((text_count, width), F32)],
-        flops=4 * text_count * image_count * width,
+        flops=2 * image_count * width * (2 * text_count + width),
         transcendentals=text_count * image_count,
         moved=2 * width * (text_count + 2 * image_count),
-    )(scalars, texts, text_ids, images, text_sum)
+    )(scalars, texts, text_ids, images, matrix, text_sum)
 
 
 def image_terms(weighted, texts):
@@ -313,42 +314,46 @@
     )(weighted, texts)
 
 
-def add_up(total, parts):
-    sizes = [len(part) for part in parts]
-
-    def kernel(total_ref, *refs):
-        out_ref = refs[-1]
-        start = 0
-        for cut in sorted(edges):
-            rows = slice(start, cut)
-            value = total_ref[rows, :]
-            place = 0
-            for size in sizes:
-                base = 0
-                for ref in refs[place : place + size]:
-                    end = base + ref.shape[0]
-                    if base <= start and cut <= end:
-                        value = value + ref[start - base : cut - base, :].astype(F32)
-                    base = end
-                place += size
-            out_ref[rows, :] = value.astype(BF)
-            start = cut
-
-    edges = set()
-    for part in parts:
-        end = 0
-        for array in part:
-            end += array.shape[0]
-            edges.add(end)
-    flat = [array for part in parts for array in part]
+def add_pair(total, part):
+    def kernel(total_ref, part_ref, out_ref):
+        out_ref[...] = (total_ref[...] + part_ref[...].astype(F32)).astype(BF)
+
     return call(
         kernel,
         jax.ShapeDtypeStruct(total.shape, BF),
-        in_specs=[pl.BlockSpec(memory_space=VMEM)] * (1 + len(flat)),
+        in_specs=[pl.BlockSpec(memory_space=VMEM)] * 2,
         out_specs=pl.BlockSpec(memory_space=VMEM),
         flops=total.size,
         moved=8 * total.size,
-    )(total, *flat)
+    )(total, part)
+
+
+def add_texts(spot, total, near, far_low, far_high):
+    rows, width = total.shape
+    count = rows // NZH
+
+    def kernel(spot_ref, total_ref, ahead_ref, behind_ref, low_ref, high_ref, out_ref, sum_ref):
+        for i in range(NZH):
+            piece = slice(i * count, (i + 1) * count)
+            value = total_ref[piece, :] + ahead_ref[piece, :].astype(F32)
+            value = value + behind_ref[piece, :].astype(F32)
+            if i < 2:
+                value = value + low_ref[piece, :].astype(F32)
+            if 0 < i < 3:
+                value = value + high_ref[(i - 1) * count : i * count, :].astype(F32)
+            sum_ref[i] = value.astype(BF)
+        for place in range(NZH):
+            out_ref[place] = sum_ref[(place - spot_ref[0] + 1) & (NZH - 1)]
+
+    return call(
+        kernel,
+        jax.ShapeDtypeStruct((NZH, count, width), BF),
+        in_specs=[pl.BlockSpec(memory_space=SMEM)] + [pl.BlockSpec(memory_space=VMEM)] * 5,
+        out_specs=pl.BlockSpec(memory_space=VMEM),
+        scratch_shapes=[pltpu.VMEM((NZH, count, width), BF)],
+        flops=3 * total.size,
+        moved=8 * total.size,
+    )(spot, total, *near, far_low, far_high)
 
 
 def to_all(values, axes, size):
@@ -373,14 +378,17 @@
 ):
     images, patches, width = picture_tiles.shape
     heads = query_key_product.shape[1]
-    z_lo, y_hi, y_lo, x, core = (lax.axis_index(a) for a in ("z_lo", "y_hi", "y_lo", "x", "core"))
+    z, y_hi, y_lo, x, core = (lax.axis_index(a) for a in (Z, "y_hi", "y_lo", "x", "core"))
     place = core.astype(jnp.int32).reshape(1)
+    spot = lax.axis_index("z_hi").astype(jnp.int32).reshape(1)
     count = caption_embedding.shape[0]
 
     exit_matrix = lax.all_gather(
         pooling_exit_matrix.T, ("core", "y_lo", "x"), axis=0, tiled=True
     )
     text_own = gather_matrix(caption_head_matrix.T)
+
+    near = [take_from(caption_embedding, Z, d, NZ) if d else caption_embedding for d in (-4, 0, 4, 8)]
 
     head_of = jnp.arange(width, dtype=jnp.int32) // (width // heads)
     spread = (head_of[None, :] == jnp.arange(heads, dtype=jnp.int32)[:, None]).astype(BF)
@@ -388,56 +396,53 @@
     tiles = picture_tiles.reshape(images * patches, width)
     attend, pooled = attention_forward(tiles, query_key_product, spread, patches)
     txt = (y_lo * NX + x) * NC + core
-    kind = (z_lo + jnp.array([0, 1, 3, 2], jnp.int32)) % NZL
-    source = (jnp.arange(NZH, dtype=jnp.int32)[None, :] * NZL + kind[:, None]).reshape(-1)
+    source = (z + jnp.array(TEXT_OFFSETS, jnp.int32)) % NZ
     first = (txt * (NZ * NYH) + source * NYH + y_hi) * count
     text_ids = first[:, None] + jnp.arange(count, dtype=jnp.int32)[None, :]
     text_ids = text_ids.astype(F32).reshape(1, -1)
     coolness = jnp.exp(natural_inverse_coolness[0])
     scalars = jnp.stack([coolness, score_offset[0], coolness * objective_adjoint[0]])
-    partners = matching_caption_index.reshape(-1, 1)
-    text_own, pooled, attend, text_ids, scalars, gather, partners = lax.optimization_barrier(
-        (text_own, pooled, attend, text_ids, scalars, gather, partners)
-    )
-
+    lane = jnp.arange(TAIL, dtype=jnp.int32)[None, :]
+    index = matching_caption_index[:, None]
+    digits = jnp.where(lane == 0, index >> 7, jnp.where(lane == 1, index & 127, 0))
+    lines = jnp.concatenate([pooled.astype(BF), digits.astype(F32).astype(BF)], axis=1)
+
+    text_own, lines, near, text_ids, scalars, gather = lax.optimization_barrier(
+        (text_own, lines, near, text_ids, scalars, gather)
+    )
     text_matrix = text_own, swap_cores(text_own)
-    text_pre, text_unit = project(place, caption_embedding, text_matrix)
-    near = to_all(text_unit, "z_hi", NZH).reshape(-1, width)
-
-    image_pre, image_unit = project(place, pooled, (exit_matrix,), partners)
-    image_unit, near = lax.optimization_barrier((image_unit, near))
-    own_images = to_all(image_unit, XY, 16).reshape(-1, width + TAIL)
-    cut = near.shape[0] // 2
+    own_images = to_all(lines, XY, 16).reshape(-1, width + TAIL)
+    near = jnp.concatenate(near, axis=0)
     pieces = [
         near,
         take_from(near, Z, 1, NZ),
         take_from(near, Z, -1, NZ),
-        take_from(near[:cut], Z, 2, NZ),
-        take_from(near[cut:], Z, -2, NZ),
+        take_from(near[count : 3 * count], Z, 2, NZ),
+        take_from(near[: 2 * count], Z, -2, NZ),
     ]
     own_images, pieces = lax.optimization_barrier((own_images, pieces))
     other_images = swap_cores(own_images)
 
-    texts, own_part, text_sum = first_tile(scalars, pieces, text_ids, own_images)
+    texts = unit_texts(place, pieces, text_matrix)
+    own_part, text_sum = first_tile(scalars, texts, text_ids, own_images, exit_matrix)
     weighted, mine, *away = second_tile(
-        scalars, texts, text_ids, other_images, text_sum, [piece.shape[0] for piece in pieces]
+        scalars, texts, text_ids, other_images, exit_matrix, text_sum,
+        [piece.shape[0] for piece in pieces],
     )
     away = [take_from(part, Z, -d, NZ) for part, d in zip(away, (1, -1, 2, -2))]
     other_part = swap_cores(image_terms(weighted, texts))
-    chip_images = add_up(own_part, [[other_part]])
+    chip_images = add_pair(own_part, other_part)
     image_parts = lax.all_to_all(chip_images.reshape(16, images, width), XY, 0, 0, tiled=True)
-    chip_texts = add_up(mine, [[away[0]], [away[1]], away[2:]])
+    chip_texts = add_texts(spot, mine, away[:2], away[3], away[2])
     image_parts, chip_texts = lax.optimization_barrier((image_parts, chip_texts))
-    text_parts = lax.all_to_all(
-        chip_texts.reshape(NZH, count, width), "z_hi", 0, 0, tiled=True
-    )
-
-    dpooled = project_back(place, image_pre, image_parts, (exit_matrix,), F32)
+    text_parts = lax.all_to_all(chip_texts, "z_hi", 0, 0, tiled=True)
+
+    dpooled = project_back(place, pooled, image_parts, (exit_matrix,), F32)
     d_patches = attention_backward(
         tiles, attend, dpooled, query_key_product.T, spread, gather, patches
     )
-    text_pre, d_patches = lax.optimization_barrier((text_pre, d_patches))
-    d_text = project_back(place, text_pre, text_parts, text_matrix, BF)
+    text_matrix, d_patches = lax.optimization_barrier((text_matrix, d_patches))
+    d_text = project_back(place, caption_embedding, text_parts, text_matrix, BF)
     return (d_patches.reshape(images, patches, width), d_text)
 
 

time: 191 us -> 199 us (1.042)
  Pallas kernels: 21.2 us -> 30.2 us
  waiting for transfers between devices: 50.7 us -> 45 us
  starting transfers between devices: 80.3 us -> 85.1 us
    ppermute x8 -> x11, starting transfers between devices: 30 us -> 54.3 us  [take_from(): lax.ppermute(values, axis, [((i + distance) % size, i) for i in range(siz...]
    all_to_all x3 -> x2, starting transfers between devices: 33.1 us -> 12.9 us  [to_all(): return lax.all_to_all(spread, axes, 0, 0, tiled=True)]
    all_to_all x3 -> x2, waiting for transfers between devices: 20.4 us -> 14.6 us  [to_all(): return lax.all_to_all(spread, axes, 0, 0, tiled=True)]
    pallas_call x5 -> x4, Pallas kernels: 7.23 us -> 11.1 us  [the longest x1 6.57 us: first_tile(): call(kernel, (jax.ShapeDtypeStruct((image_count, width), F32), jax.ShapeD...]
    ppermute x3, waiting for transfers between devices: 5.48 us -> 2.46 us  [swap_cores(): return lax.ppermute(values, 'core', [(0, 1), (1, 0)])]
    pallas_call x1, Pallas kernels: 2.74 us -> 5.73 us  [second_tile(): call(kernel, (jax.ShapeDtypeStruct((image_count, text_count), BF), jax.Sh...]
    pallas_call x2, Pallas kernels: 3.62 us -> 5.76 us  [project_back(): call(kernel, jax.ShapeDtypeStruct((count, width), out_dtype), in_specs=[p...]
    unnamed x57 -> x72, local copies, waits for them, and re-layouts: 14.3 us -> 16 us
  transfers between devices with their start and end apart: 17 -> 19, of which waited for: 10 -> 7; matrix products, arithmetic and copies ran while one was open for 2% -> 2% of each run, Pallas kernels for 8% -> 10%
where the time goes in v3:
time: 199 us; the launch traced here: 197 us
  starting transfers between devices  85.1 us (43%)
  waiting for transfers between devices  45 us (23%)
  Pallas kernels  30.2 us (15%)
  local copies, waits for them, and re-layouts  19.4 us (10%)
  between operations  16.5 us (8%)
    ppermute x11, starting transfers between devices, take_from(): lax.ppermute(values, axis, [((i + distance) % size, i) for i in range(siz...  54.3 us
    unnamed x72, local copies, waits for them, and re-layouts  16 us
    ppermute x11, waiting for transfers between devices, take_from(): lax.ppermute(values, axis, [((i + distance) % size, i) for i in range(siz...  15.9 us
    all_to_all x2, waiting for transfers between devices, to_all(): return lax.all_to_all(spread, axes, 0, 0, tiled=True)  14.6 us
    all_to_all x2, starting transfers between devices, to_all(): return lax.all_to_all(spread, axes, 0, 0, tiled=True)  12.9 us
    all_to_all x1, waiting for transfers between devices, shards(): text_parts = lax.all_to_all(chip_texts, 'z_hi', 0, 0, tiled=True)  11.3 us
    all_to_all x1, starting transfers between devices, shards(): lax.all_to_all(chip_images.reshape(16, images, width), XY, 0, 0, tiled=True)  7.23 us
    pallas_call x1, Pallas kernels, first_tile(): call(kernel, (jax.ShapeDtypeStruct((image_count, width), F32), jax.ShapeD...  6.57 us
  transfers between devices with their start and end apart: 19, of which 7 were waited for; matrix products, arithmetic and copies ran while one was open for 2% of the time, Pallas kernels for 10%

profile of v3, /device:TPU:6, one launch (start us, length us, event | category | flops | bytes accessed | tf_op | source)
XLA Modules:
  0.0 197.5 jit_solution(1022911418745428874)
XLA Ops:
  7.9 15.7 %collective-permute-start.2 = (bf16[32,1152]{1,0:T(8,128)(2,1)}, bf16[32,1152]{1,0:T(8,128)(2,1)S(1)}, u32[]{:S(2)}, u32[]{:S(2)}) collective-permute-start(bf16[32,1152]{1,0:T(8,128)(2,1)} %rows_ref.1), channel_id=1, source_target_pairs={{256,0},{288,32},{320,64},{352,96},{384,128},{416,160},{448,192},{... | collective-permute-start | bytes 221192 | tf_op jit(solution)/shard_map/ppermute | solution.py:22
  23.6 1.9 collective-permute-start.1
  25.6 7.8 %collective-permute-start = (bf16[32,1152]{1,0:T(8,128)(2,1)}, bf16[32,1152]{1,0:T(8,128)(2,1)S(1)}, u32[]{:S(2)}, u32[]{:S(2)}) collective-permute-start(bf16[32,1152]{1,0:T(8,128)(2,1)} %rows_ref.1), channel_id=1, source_target_pairs={{384,0},{416,32},{448,64},{480,96},{0,128},{32,160},{64,192},{96,2... | collective-permute-start | bytes 221192 | tf_op jit(solution)/shard_map/ppermute | solution.py:22
  33.4 2.1 %broadcast_in_dim.40 = bf16[8,72,1152]{2,1,0:T(8,128)(2,1)} broadcast(bf16[72,1152]{1,0:T(8,128)(2,1)} %bitcast.15), dimensions={1,2} | broadcast | bytes 1492992 | tf_op jit(solution)/shard_map/broadcast_in_dim | solution.py:360
  35.5 5.9 %all-to-all-start = ((bf16[8,72,1152]{2,1,0:T(8,128)(2,1)}), bf16[8,72,1152]{2,1,0:T(8,128)(2,1)}, u32[]{:S(2)}, u32[]{:S(2)}) async-start(bf16[8,72,1152]{2,1,0:T(8,128)(2,1)} %broadcast_in_dim.40), calls=%async_computation | async-start | bytes 2654208 | tf_op jit(solution)/shard_map/all_to_all | solution.py:361
  41.9 2.6 %shard_map.113 = (f32[1024,16]{1,0:T(8,128)S(1)}, f32[32,1152]{1,0:T(8,128)S(1)}) custom-call(bf16[1024,1152]{1,0:T(8,128)(2,1)S(1)} %bitcast.10, bf16[1152,16]{1,0:T(8,128)(2,1)S(1)} %copy.12.qk_ref, bf16[16,1152]{1,0:T(8,128)(2,1)S(1)} %fusion.1.spread_ref), custom_call_target="tpu_custom_call" | custom-call | flops 603979776 | bytes 2359296 | tf_op jit(solution)/shard_map/pallas_call | solution.py:72
  44.5 0.8 copy-done.12
  47.5 0.9 fusion.gather_ref
  48.5 14.6 %all-to-all-done = bf16[8,72,1152]{2,1,0:T(8,128)(2,1)} async-done(((bf16[8,72,1152]{2,1,0:T(8,128)(2,1)}), bf16[8,72,1152]{2,1,0:T(8,128)(2,1)}, u32[]{:S(2)}, u32[]{:S(2)}) %all-to-all-start) | async-done | bytes 1327136 | tf_op jit(solution)/shard_map/all_to_all | solution.py:361
  63.1 1.2 broadcast_in_dim.62
  64.3 7.0 %all-to-all-start.1 = ((bf16[16,32,1280]{2,1,0:T(8,128)(2,1)}), bf16[16,32,1280]{2,1,0:T(8,128)(2,1)}, u32[]{:S(2)}, u32[]{:S(2)}) async-start(bf16[16,32,1280]{2,1,0:T(8,128)(2,1)} %broadcast_in_dim.62), calls=%async_computation.1 | async-start | bytes 2621440 | tf_op jit(solution)/shard_map/all_to_all | solution.py:361
  71.2 1.9 collective-permute-start.3
  73.2 3.2 %collective-permute-start.5 = (bf16[128,1152]{1,0:T(8,128)(2,1)S(1)}, bf16[128,1152]{1,0:T(8,128)(2,1)S(1)}, u32[]{:S(2)}, u32[]{:S(2)}) collective-permute-start(bf16[128,1152]{1,0:T(8,128)(2,1)S(1)} %constant_dynamic-update-slice_fusion.refs_0_), channel_id=1, source_target_pairs={{480,0},{0,32},{32,64},{64,96},{96,128},{128,160},{160,192},{192,2... | collective-permute-start | bytes 884744 | tf_op jit(solution)/shard_map/ppermute | solution.py:22
  76.5 3.8 %collective-permute-start.4 = (bf16[128,1152]{1,0:T(8,128)(2,1)S(1)}, bf16[128,1152]{1,0:T(8,128)(2,1)S(1)}, u32[]{:S(2)}, u32[]{:S(2)}) collective-permute-start(bf16[128,1152]{1,0:T(8,128)(2,1)S(1)} %constant_dynamic-update-slice_fusion.refs_0_), channel_id=1, source_target_pairs={{32,0},{64,32},{96,64},{128,96},{160,128},{192,160},{224,192},{256... | collective-permute-start | bytes 884744 | tf_op jit(solution)/shard_map/ppermute | solution.py:22
  80.3 2.9 %collective-permute-start.7 = (bf16[64,1152]{1,0:T(8,128)(2,1)S(1)}, bf16[64,1152]{1,0:T(8,128)(2,1)S(1)}, u32[]{:S(2)}, u32[]{:S(2)}) collective-permute-start(bf16[64,1152]{1,0:T(8,128)(2,1)S(1)} %get-tuple-element.62), channel_id=1, source_target_pairs={{448,0},{480,32},{0,64},{32,96},{64,128},{96,160},{128,192},{160,2... | collective-permute-start | bytes 442376 | tf_op jit(solution)/shard_map/ppermute | solution.py:22
  83.3 5.0 %collective-permute-start.6 = (bf16[64,1152]{1,0:T(8,128)(2,1)S(1)}, bf16[64,1152]{1,0:T(8,128)(2,1)S(1)}, u32[]{:S(2)}, u32[]{:S(2)}) collective-permute-start(bf16[64,1152]{1,0:T(8,128)(2,1)S(1)} %get-tuple-element.63), channel_id=1, source_target_pairs={{64,0},{96,32},{128,64},{160,96},{192,128},{224,160},{256,192},{28... | collective-permute-start | bytes 442376 | tf_op jit(solution)/shard_map/ppermute | solution.py:22
  88.3 4.4 %collective-permute-done.7.refs_4_ = bf16[64,1152]{1,0:T(8,128)(2,1)S(1)} collective-permute-done((bf16[64,1152]{1,0:T(8,128)(2,1)S(1)}, bf16[64,1152]{1,0:T(8,128)(2,1)S(1)}, u32[]{:S(2)}, u32[]{:S(2)}) %collective-permute-start.7) | collective-permute-done | bytes 147488 | tf_op jit(solution)/shard_map/ppermute | solution.py:22
  93.4 1.5 collective-permute-done.6.refs_3_
  95.6 0.7 copy-done.22
  97.1 2.1 %collective-permute-start.8 = (bf16[512,1280]{1,0:T(8,128)(2,1)}, bf16[512,1280]{1,0:T(8,128)(2,1)}, u32[]{:S(2)}, u32[]{:S(2)}) collective-permute-start(bf16[512,1280]{1,0:T(8,128)(2,1)} %bitcast.4.images_ref), channel_id=1, source_target_pairs={{0,1},{1,0},{2,3},{3,2},{4,5},{5,4},{6,7},{7,6},{8,9},{9,8},{10,11... | collective-permute-start | bytes 3932168 | tf_op jit(solution)/shard_map/ppermute | solution.py:26
  99.2 1.0 copy-done.19
  100.1 1.0 copy-done.23
  101.1 1.0 copy-done.25
  102.1 0.9 copy-done.29
  103.0 0.9 copy-done.31
  103.9 4.2 %shard_map.114.texts_ref = bf16[512,1152]{1,0:T(8,128)(2,1)S(1)} custom-call(s32[1]{0:T(128)} %bitcast.3.core_ref, bf16[128,1152]{1,0:T(8,128)(2,1)S(1)} %copy-done.19, bf16[128,1152]{1,0:T(8,128)(2,1)S(1)} %copy-done.25, bf16[128,1152]{1,0:T(8,128)(2,1)S(1)} %copy-done.23, bf16[64,1152]{1,0:T(8,128)(2,1)S(1)} %copy-done.31, ...), custom_call_target="tpu_custom_call" | custom-call | flops 1358954496 | bytes 2654208 | tf_op jit(solution)/shard_map/pallas_call | solution.py:170
  108.1 1.7 copy-done.2
  109.9 6.6 %shard_map.115 = (f32[512,1152]{1,0:T(8,128)S(1)}, f32[512,1152]{1,0:T(8,128)S(1)}) custom-call(f32[3]{0:T(128)S(1)} %pad_maximum_fusion.3.scalar_ref, bf16[512,1152]{1,0:T(8,128)(2,1)S(1)} %shard_map.114.texts_ref, f32[1,512]{1,0:T(1,128)S(1)} %convert_element_type.35.ids_ref, bf16[512,1280]{1,0:T(8,128)(2,1)} %bitcast.4.images_ref, ...), custom_call_target="tpu_custom_call" | custom-call | flops 3170893824 | bytes 3538944 | tf_op jit(solution)/shard_map/pallas_call | solution.py:245
  116.4 5.7 %shard_map.116 = (bf16[512,512]{1,0:T(8,128)(2,1)S(1)}, f32[128,1152]{1,0:T(8,128)S(1)}, bf16[128,1152]{1,0:T(8,128)(2,1)S(1)}, bf16[128,1152]{1,0:T(8,128)(2,1)...) custom-call(f32[3]{0:T(128)S(1)} %pad_maximum_fusion.3.scalar_ref, ...), custom_call_target="tpu_custom_call" | custom-call | flops 2566914048 | bytes 3538944 | tf_op jit(solution)/shard_map/pallas_call | solution.py:284
  122.2 0.8 shard_map.117
  123.3 2.4 %collective-permute-start.9 = (bf16[512,1152]{1,0:T(8,128)(2,1)S(1)}, bf16[512,1152]{1,0:T(8,128)(2,1)S(1)}, u32[]{:S(2)}, u32[]{:S(2)}) collective-permute-start(bf16[512,1152]{1,0:T(8,128)(2,1)S(1)} %shard_map.117), channel_id=1, source_target_pairs={{0,1},{1,0},{2,3},{3,2},{4,5},{5,4},{6,7},{7,6},{8,9},{9,8},{10,11... | collective-permute-start | bytes 3538952 | tf_op jit(solution)/shard_map/ppermute | solution.py:26
  125.7 2.5 %collective-permute-done.9.part_ref = bf16[512,1152]{1,0:T(8,128)(2,1)S(1)} collective-permute-done((bf16[512,1152]{1,0:T(8,128)(2,1)S(1)}, bf16[512,1152]{1,0:T(8,128)(2,1)S(1)}, u32[]{:S(2)}, u32[]{:S(2)}) %collective-permute-start.9) | collective-permute-done | bytes 1179680 | tf_op jit(solution)/shard_map/ppermute | solution.py:26
  128.4 1.0 copy-done.1
  129.4 7.2 %all-to-all-start.2 = ((bf16[16,32,1152]{2,1,0:T(8,128)(2,1)}), bf16[16,32,1152]{2,1,0:T(8,128)(2,1)S(1)}, u32[]{:S(2)}, u32[]{:S(2)}) async-start(bf16[16,32,1152]{2,1,0:T(8,128)(2,1)} %bitcast.12), calls=%async_computation.2 | async-start | bytes 2359296 | tf_op jit(solution)/shard_map/all_to_all | solution.py:435
  136.6 1.9 collective-permute-start.10
  138.5 5.1 %collective-permute-start.11 = (bf16[128,1152]{1,0:T(8,128)(2,1)}, bf16[128,1152]{1,0:T(8,128)(2,1)S(1)}, u32[]{:S(2)}, u32[]{:S(2)}) collective-permute-start(bf16[128,1152]{1,0:T(8,128)(2,1)} %copy-done.20), channel_id=1, source_target_pairs={{32,0},{64,32},{96,64},{128,96},{160,128},{192,160},{224,192},{256... | collective-permute-start | bytes 884744 | tf_op jit(solution)/shard_map/ppermute | solution.py:22
  143.7 4.7 %collective-permute-start.12 = (bf16[64,1152]{1,0:T(8,128)(2,1)}, bf16[64,1152]{1,0:T(8,128)(2,1)S(1)}, u32[]{:S(2)}, u32[]{:S(2)}) collective-permute-start(bf16[64,1152]{1,0:T(8,128)(2,1)} %copy-done.27), channel_id=1, source_target_pairs={{64,0},{96,32},{128,64},{160,96},{192,128},{224,160},{256,192},{28... | collective-permute-start | bytes 442376 | tf_op jit(solution)/shard_map/ppermute | solution.py:22
  148.4 2.0 %collective-permute-start.13 = (bf16[64,1152]{1,0:T(8,128)(2,1)}, bf16[64,1152]{1,0:T(8,128)(2,1)S(1)}, u32[]{:S(2)}, u32[]{:S(2)}) collective-permute-start(bf16[64,1152]{1,0:T(8,128)(2,1)} %copy-done.26), channel_id=1, source_target_pairs={{448,0},{480,32},{0,64},{32,96},{64,128},{96,160},{128,192},{160,2... | collective-permute-start | bytes 442376 | tf_op jit(solution)/shard_map/ppermute | solution.py:22
  150.4 8.6 %collective-permute-done.12.low_ref = bf16[64,1152]{1,0:T(8,128)(2,1)S(1)} collective-permute-done((bf16[64,1152]{1,0:T(8,128)(2,1)}, bf16[64,1152]{1,0:T(8,128)(2,1)S(1)}, u32[]{:S(2)}, u32[]{:S(2)}) %collective-permute-start.12) | collective-permute-done | bytes 147488 | tf_op jit(solution)/shard_map/ppermute | solution.py:22
  159.0 1.4 collective-permute-done.13.high_ref
  160.4 1.1 copy-done.11
  162.3 4.3 %all-to-all-start.3 = ((bf16[4,32,1152]{2,1,0:T(8,128)(2,1)}), bf16[4,32,1152]{2,1,0:T(8,128)(2,1)}, u32[]{:S(2)}, u32[]{:S(2)}) async-start(bf16[4,32,1152]{2,1,0:T(8,128)(2,1)} %copy-done.5), calls=%async_computation.3 | async-start | bytes 589824 | tf_op jit(solution)/shard_map/all_to_all | solution.py:438
  166.7 1.7 copy-done.3
  168.4 0.9 copy-done.9
  169.3 1.6 shard_map.120.dpooled_ref
  171.0 4.2 %shard_map.121 = bf16[1024,1152]{1,0:T(8,128)(2,1)} custom-call(bf16[1024,1152]{1,0:T(8,128)(2,1)S(1)} %bitcast.11, f32[1024,16]{1,0:T(8,128)S(1)} %copy-done.13, f32[32,1152]{1,0:T(8,128)S(1)} %shard_map.120.dpooled_ref, bf16[16,1152]{1,0:T(8,128)(2,1)S(1)} %bitcast.13, bf16[16,1152]{1,0:T(8,128)(2,1)S(1)} %copy-done.15, bf16[1152,16]{1,0:T(8,128)(2,1)S(1)} %copy-done.4), custom_call_target="tpu_custom_call" | custom-call | flops 1207959552 | bytes 4718592 | tf_op jit(solution)/shard_map/pallas_call | solution.py:118
  175.2 11.3 %all-to-all-done.3.parts_ref = bf16[4,32,1152]{2,1,0:T(8,128)(2,1)} async-done(((bf16[4,32,1152]{2,1,0:T(8,128)(2,1)}), bf16[4,32,1152]{2,1,0:T(8,128)(2,1)}, u32[]{:S(2)}, u32[]{:S(2)}) %all-to-all-start.3) | async-done | bytes 294944 | tf_op jit(solution)/shard_map/all_to_all | solution.py:438
  186.5 4.1 %shard_map.122 = bf16[32,1152]{1,0:T(8,128)(2,1)} custom-call(s32[1]{0:T(128)} %bitcast.3.core_ref, bf16[32,1152]{1,0:T(8,128)(2,1)S(1)} %copy-done.7, bf16[4,32,1152]{2,1,0:T(8,128)(2,1)} %all-to-all-done.3.parts_ref, bf16[576,1152]{1,0:T(8,128)(2,1)} %bitcast.1.refs_5_.refs_0_, bf16[576,1152]{1,0:T(8,128)(2,1)} %collective-permute-done.3.refs_6_.refs_1_), custom_call_target="tpu_custom_call" | custom-call | flops 169869312 | bytes 2654208 | tf_op jit(solution)/shard_map/pallas_call | solution.py:205
  (89 shorter events, 4.9 us)
Async XLA Ops:
  7.2 100.9 %all-gather.2.cloned.1.call-start = ((), (), s32[]{:S(2)}) async-start(), calls=%async_computation.4 | async-start | bytes 2820096 | tf_op jit(solution)/shard_map/all_gather | solution.py:386
  7.9 40.6 %collective-permute-start.2 = (bf16[32,1152]{1,0:T(8,128)(2,1)}, bf16[32,1152]{1,0:T(8,128)(2,1)S(1)}, u32[]{:S(2)}, u32[]{:S(2)}) collective-permute-start(bf16[32,1152]{1,0:T(8,128)(2,1)} %rows_ref.1), channel_id=1, source_target_pairs={{256,0},{288,32},{320,64},{352,96},{384,128},{416,160},{448,192},{... | collective-permute-start | bytes 221192 | tf_op jit(solution)/shard_map/ppermute | solution.py:22
  23.6 24.9 %collective-permute-start.1 = (bf16[32,1152]{1,0:T(8,128)(2,1)}, bf16[32,1152]{1,0:T(8,128)(2,1)S(1)}, u32[]{:S(2)}, u32[]{:S(2)}) collective-permute-start(bf16[32,1152]{1,0:T(8,128)(2,1)} %rows_ref.1), channel_id=1, source_target_pairs={{128,0},{160,32},{192,64},{224,96},{256,128},{288,160},{320,192},{... | collective-permute-start | bytes 221192 | tf_op jit(solution)/shard_map/ppermute | solution.py:22
  25.6 23.0 %collective-permute-start = (bf16[32,1152]{1,0:T(8,128)(2,1)}, bf16[32,1152]{1,0:T(8,128)(2,1)S(1)}, u32[]{:S(2)}, u32[]{:S(2)}) collective-permute-start(bf16[32,1152]{1,0:T(8,128)(2,1)} %rows_ref.1), channel_id=1, source_target_pairs={{384,0},{416,32},{448,64},{480,96},{0,128},{32,160},{64,192},{96,2... | collective-permute-start | bytes 221192 | tf_op jit(solution)/shard_map/ppermute | solution.py:22
  35.5 5.9 %copy-start.16 = (bf16[1152,16]{0,1:T(8,128)(2,1)S(1)}, bf16[1152,16]{0,1:T(8,128)(2,1)}, u32[]{:S(2)}) copy-start(bf16[1152,16]{0,1:T(8,128)(2,1)} %param.11) | copy-start | bytes 110596
  35.5 6.2 %copy-start.32 = (s32[16]{0:T(128)S(1)}, s32[16]{0:T(128)}, u32[]{:S(2)}) copy-start(s32[16]{0:T(128)} %constant.65.clone) | copy-start | bytes 196
  35.5 6.2 %copy-start.33 = (s32[32]{0:T(128)S(1)}, s32[32]{0:T(128)}, u32[]{:S(2)}) copy-start(s32[32]{0:T(128)} %param.15) | copy-start | bytes 388
  35.5 6.4 %copy-start = (bf16[32,32,1152]{2,1,0:T(8,128)(2,1)S(1)}, bf16[32,32,1152]{2,1,0:T(8,128)(2,1)}, u32[]{:S(2)}) copy-start(bf16[32,32,1152]{2,1,0:T(8,128)(2,1)} %param.10) | copy-start | bytes 7077892
  35.5 27.6 %all-to-all-start = ((bf16[8,72,1152]{2,1,0:T(8,128)(2,1)}), bf16[8,72,1152]{2,1,0:T(8,128)(2,1)}, u32[]{:S(2)}, u32[]{:S(2)}) async-start(bf16[8,72,1152]{2,1,0:T(8,128)(2,1)} %broadcast_in_dim.40), calls=%async_computation | async-start | bytes 2654208 | tf_op jit(solution)/shard_map/all_to_all | solution.py:361
  41.8 2.7 %copy-start.14 = (bf16[16,1152]{1,0:T(8,128)(2,1)}, bf16[16,1152]{1,0:T(8,128)(2,1)S(1)}, u32[]{:S(2)}) copy-start(bf16[16,1152]{1,0:T(8,128)(2,1)S(1)} %fusion.1.spread_ref) | copy-start | bytes 110596
  44.5 0.8 copy-start.12
  45.3 18.9 %copy-start.8 = (f32[32,1152]{1,0:T(8,128)}, f32[32,1152]{1,0:T(8,128)S(1)}, u32[]{:S(2)}) copy-start(f32[32,1152]{1,0:T(8,128)S(1)} %get-tuple-element.32.rows_ref) | copy-start | bytes 442372
  64.3 8.9 %copy-start.6 = (bf16[32,1152]{1,0:T(8,128)(2,1)S(1)}, bf16[32,1152]{1,0:T(8,128)(2,1)}, u32[]{:S(2)}) copy-start(bf16[32,1152]{1,0:T(8,128)(2,1)} %rows_ref.1) | copy-start | bytes 221188
  64.3 32.8 %all-to-all-start.1 = ((bf16[16,32,1280]{2,1,0:T(8,128)(2,1)}), bf16[16,32,1280]{2,1,0:T(8,128)(2,1)}, u32[]{:S(2)}, u32[]{:S(2)}) async-start(bf16[16,32,1280]{2,1,0:T(8,128)(2,1)} %broadcast_in_dim.62), calls=%async_computation.1 | async-start | bytes 2621440 | tf_op jit(solution)/shard_map/all_to_all | solution.py:361
  71.2 27.9 %collective-permute-start.3 = (bf16[576,1152]{1,0:T(8,128)(2,1)}, bf16[576,1152]{1,0:T(8,128)(2,1)}, u32[]{:S(2)}, u32[]{:S(2)}) collective-permute-start(bf16[576,1152]{1,0:T(8,128)(2,1)} %bitcast.1.refs_5_.refs_0_), channel_id=1, source_target_pairs={{0,1},{1,0},{2,3},{3,2},{4,5},{5,4},{6,7},{7,6},{8,9},{9,8},{10,11... | collective-permute-start | bytes 3981320 | tf_op jit(solution)/shard_map/ppermute | solution.py:26
  73.2 7.1 %copy-start.18 = (bf16[128,1152]{1,0:T(8,128)(2,1)}, bf16[128,1152]{1,0:T(8,128)(2,1)S(1)}, u32[]{:S(2)}) copy-start(bf16[128,1152]{1,0:T(8,128)(2,1)S(1)} %constant_dynamic-update-slice_fusion.refs_0_) | copy-start | bytes 884740
  73.2 22.4 %collective-permute-start.5 = (bf16[128,1152]{1,0:T(8,128)(2,1)S(1)}, bf16[128,1152]{1,0:T(8,128)(2,1)S(1)}, u32[]{:S(2)}, u32[]{:S(2)}) collective-permute-start(bf16[128,1152]{1,0:T(8,128)(2,1)S(1)} %constant_dynamic-update-slice_fusion.refs_0_), channel_id=1, source_target_pairs={{480,0},{0,32},{32,64},{64,96},{96,128},{128,160},{160,192},{192,2... | collective-permute-start | bytes 884744 | tf_op jit(solution)/shard_map/ppermute | solution.py:22
  76.5 19.9 %collective-permute-start.4 = (bf16[128,1152]{1,0:T(8,128)(2,1)S(1)}, bf16[128,1152]{1,0:T(8,128)(2,1)S(1)}, u32[]{:S(2)}, u32[]{:S(2)}) collective-permute-start(bf16[128,1152]{1,0:T(8,128)(2,1)S(1)} %constant_dynamic-update-slice_fusion.refs_0_), channel_id=1, source_target_pairs={{32,0},{64,32},{96,64},{128,96},{160,128},{192,160},{224,192},{256... | collective-permute-start | bytes 884744 | tf_op jit(solution)/shard_map/ppermute | solution.py:22
  80.3 12.4 %collective-permute-start.7 = (bf16[64,1152]{1,0:T(8,128)(2,1)S(1)}, bf16[64,1152]{1,0:T(8,128)(2,1)S(1)}, u32[]{:S(2)}, u32[]{:S(2)}) collective-permute-start(bf16[64,1152]{1,0:T(8,128)(2,1)S(1)} %get-tuple-element.62), channel_id=1, source_target_pairs={{448,0},{480,32},{0,64},{32,96},{64,128},{96,160},{128,192},{160,2... | collective-permute-start | bytes 442376 | tf_op jit(solution)/shard_map/ppermute | solution.py:22
  83.3 11.6 %collective-permute-start.6 = (bf16[64,1152]{1,0:T(8,128)(2,1)S(1)}, bf16[64,1152]{1,0:T(8,128)(2,1)S(1)}, u32[]{:S(2)}, u32[]{:S(2)}) collective-permute-start(bf16[64,1152]{1,0:T(8,128)(2,1)S(1)} %get-tuple-element.63), channel_id=1, source_target_pairs={{64,0},{96,32},{128,64},{160,96},{192,128},{224,160},{256,192},{28... | collective-permute-start | bytes 442376 | tf_op jit(solution)/shard_map/ppermute | solution.py:22
  97.1 19.4 %collective-permute-start.8 = (bf16[512,1280]{1,0:T(8,128)(2,1)}, bf16[512,1280]{1,0:T(8,128)(2,1)}, u32[]{:S(2)}, u32[]{:S(2)}) collective-permute-start(bf16[512,1280]{1,0:T(8,128)(2,1)} %bitcast.4.images_ref), channel_id=1, source_target_pairs={{0,1},{1,0},{2,3},{3,2},{4,5},{5,4},{6,7},{7,6},{8,9},{9,8},{10,11... | collective-permute-start | bytes 3932168 | tf_op jit(solution)/shard_map/ppermute | solution.py:26
  99.2 1.0 copy-start.19
  100.1 1.0 copy-start.23
  101.1 1.0 copy-start.25
  102.1 0.9 copy-start.29
  103.0 0.9 copy-start.31
  108.1 1.8 copy-start.2
  122.2 0.9 copy-start.10
  122.2 0.9 copy-start.20
  122.2 1.0 copy-start.21
  122.2 1.0 copy-start.26
  122.2 1.1 copy-start.27
  123.3 4.9 %collective-permute-start.9 = (bf16[512,1152]{1,0:T(8,128)(2,1)S(1)}, bf16[512,1152]{1,0:T(8,128)(2,1)S(1)}, u32[]{:S(2)}, u32[]{:S(2)}) collective-permute-start(bf16[512,1152]{1,0:T(8,128)(2,1)S(1)} %shard_map.117), channel_id=1, source_target_pairs={{0,1},{1,0},{2,3},{3,2},{4,5},{5,4},{6,7},{7,6},{8,9},{9,8},{10,11... | collective-permute-start | bytes 3538952 | tf_op jit(solution)/shard_map/ppermute | solution.py:26
  128.3 1.0 copy-start.1
  129.4 33.0 %all-to-all-start.2 = ((bf16[16,32,1152]{2,1,0:T(8,128)(2,1)}), bf16[16,32,1152]{2,1,0:T(8,128)(2,1)S(1)}, u32[]{:S(2)}, u32[]{:S(2)}) async-start(bf16[16,32,1152]{2,1,0:T(8,128)(2,1)} %bitcast.12), calls=%async_computation.2 | async-start | bytes 2359296 | tf_op jit(solution)/shard_map/all_to_all | solution.py:435
  136.6 23.8 %collective-permute-start.10 = (bf16[128,1152]{1,0:T(8,128)(2,1)}, bf16[128,1152]{1,0:T(8,128)(2,1)S(1)}, u32[]{:S(2)}, u32[]{:S(2)}) collective-permute-start(bf16[128,1152]{1,0:T(8,128)(2,1)} %copy-done.21), channel_id=1, source_target_pairs={{480,0},{0,32},{32,64},{64,96},{96,128},{128,160},{160,192},{192,2... | collective-permute-start | bytes 884744 | tf_op jit(solution)/shard_map/ppermute | solution.py:22
  138.5 21.8 %collective-permute-start.11 = (bf16[128,1152]{1,0:T(8,128)(2,1)}, bf16[128,1152]{1,0:T(8,128)(2,1)S(1)}, u32[]{:S(2)}, u32[]{:S(2)}) collective-permute-start(bf16[128,1152]{1,0:T(8,128)(2,1)} %copy-done.20), channel_id=1, source_target_pairs={{32,0},{64,32},{96,64},{128,96},{160,128},{192,160},{224,192},{256... | collective-permute-start | bytes 884744 | tf_op jit(solution)/shard_map/ppermute | solution.py:22
  143.7 15.3 %collective-permute-start.12 = (bf16[64,1152]{1,0:T(8,128)(2,1)}, bf16[64,1152]{1,0:T(8,128)(2,1)S(1)}, u32[]{:S(2)}, u32[]{:S(2)}) collective-permute-start(bf16[64,1152]{1,0:T(8,128)(2,1)} %copy-done.27), channel_id=1, source_target_pairs={{64,0},{96,32},{128,64},{160,96},{192,128},{224,160},{256,192},{28... | collective-permute-start | bytes 442376 | tf_op jit(solution)/shard_map/ppermute | solution.py:22
  148.4 12.0 %collective-permute-start.13 = (bf16[64,1152]{1,0:T(8,128)(2,1)}, bf16[64,1152]{1,0:T(8,128)(2,1)S(1)}, u32[]{:S(2)}, u32[]{:S(2)}) collective-permute-start(bf16[64,1152]{1,0:T(8,128)(2,1)} %copy-done.26), channel_id=1, source_target_pairs={{448,0},{480,32},{0,64},{32,96},{64,128},{96,160},{128,192},{160,2... | collective-permute-start | bytes 442376 | tf_op jit(solution)/shard_map/ppermute | solution.py:22
  160.4 1.1 copy-start.11
  162.3 24.2 %all-to-all-start.3 = ((bf16[4,32,1152]{2,1,0:T(8,128)(2,1)}), bf16[4,32,1152]{2,1,0:T(8,128)(2,1)}, u32[]{:S(2)}, u32[]{:S(2)}) async-start(bf16[4,32,1152]{2,1,0:T(8,128)(2,1)} %copy-done.5), calls=%async_computation.3 | async-start | bytes 589824 | tf_op jit(solution)/shard_map/all_to_all | solution.py:438
  166.6 1.8 copy-start.3
  168.4 0.9 copy-start.9
  169.3 1.6 copy-start.4
  169.3 1.6 copy-start.13
  169.3 1.7 copy-start.15
  169.3 1.7 copy-start.17
  171.0 15.5 %copy-start.7 = (bf16[32,1152]{1,0:T(8,128)(2,1)S(1)}, bf16[32,1152]{1,0:T(8,128)(2,1)}, u32[]{:S(2)}) copy-start(bf16[32,1152]{1,0:T(8,128)(2,1)} %rows_ref.1) | copy-start | bytes 221188
  (5 other events, 3.5 us)
Sparse Core Ops, SparseCore 0:
  10.2 55.8 all-gather.1

commit v4 on v3

--- a/solution.py
+++ b/solution.py
@@ -151,41 +151,57 @@
 
 def unit_texts(core, pieces, matrix):
     text_count = sum(piece.shape[0] for piece in pieces)
+    count = pieces[0].shape[0] // NZH
     width = pieces[0].shape[1]
     block = min(256, text_count)
 
     def kernel(core_ref, *refs):
         piece_refs, refs = refs[: len(pieces)], refs[len(pieces) :]
-        matrix_refs, (texts_ref, pre_ref) = refs[: len(matrix)], refs[len(matrix) :]
-        start = 0
-        for ref in piece_refs:
-            texts_ref[start : start + ref.shape[0], :] = ref[...]
+        matrix_refs, (texts_ref, own_ref, pre_ref, sems) = refs[: len(matrix)], refs[len(matrix) :]
+        copies, start = [], 0
+        for i, ref in enumerate(piece_refs):
+            rows = pl.ds(start, ref.shape[0])
+            copies.append(pltpu.make_async_copy(ref, texts_ref.at[rows], sems.at[i]))
             start += ref.shape[0]
+        for copy in copies:
+            copy.start()
+        for copy in copies:
+            copy.wait()
         for i in range(text_count // block):
             rows = slice(i * block, (i + 1) * block)
             pre = projected(core_ref, texts_ref[rows, :], matrix_refs, pre_ref)
             texts_ref[rows, :] = unit_rows(pre)
-
-    operands = [core, *pieces, *matrix]
-    return call(
-        kernel,
-        jax.ShapeDtypeStruct((text_count, width), BF),
+            if i == 0:
+                own_ref[...] = pre[count : 2 * count]
+
+    return call(
+        kernel,
+        (
+            jax.ShapeDtypeStruct((text_count, width), BF),
+            jax.ShapeDtypeStruct((count, width), F32),
+        ),
         in_specs=[pl.BlockSpec(memory_space=SMEM)]
-        + [pl.BlockSpec(memory_space=VMEM)] * (len(operands) - 1),
-        out_specs=pl.BlockSpec(memory_space=VMEM),
-        scratch_shapes=[pltpu.VMEM((block, width), F32)],
+        + [pl.BlockSpec(memory_space=pl.ANY)] * len(pieces)
+        + [pl.BlockSpec(memory_space=VMEM)] * len(matrix),
+        out_specs=[pl.BlockSpec(memory_space=VMEM)] * 2,
+        scratch_shapes=[
+            pltpu.VMEM((block, width), F32),
+            pltpu.SemaphoreType.DMA((len(pieces),)),
+        ],
         flops=2 * text_count * width * width,
         moved=2 * width * width,
-    )(*operands)
-
-
-def project_back(core, rows, parts, matrix, out_dtype):
+    )(core, *pieces, *matrix)
+
+
+def project_back(core, rows, parts, matrix, out_dtype, before=False):
     count, width = rows.shape
     half = width // 2
 
     def kernel(core_ref, rows_ref, parts_ref, *refs):
         matrix_refs, (out_ref, pre_ref) = refs[: len(matrix)], refs[len(matrix) :]
-        pre = projected(core_ref, rows_ref[...].astype(BF), matrix_refs, pre_ref)
+        pre = rows_ref[...]
+        if not before:
+            pre = projected(core_ref, pre.astype(BF), matrix_refs, pre_ref)
         upstream = parts_ref[0].astype(F32)
         for i in range(1, parts_ref.shape[0]):
             upstream += parts_ref[i].astype(F32)
@@ -224,16 +240,20 @@
     return slope.astype(BF)
 
 
-def first_tile(scalars, texts, text_ids, images, matrix):
+def first_tile(core, scalars, texts, text_ids, images, matrix):
     text_count, width = texts.shape
     image_count = images.shape[0]
     block = min(256, image_count)
 
-    def kernel(scalar_ref, texts_ref, ids_ref, images_ref, matrix_ref, image_part_ref, total_ref):
+    def kernel(
+        core_ref, scalar_ref, texts_ref, ids_ref, images_ref, mine_ref, theirs_ref,
+        image_part_ref, total_ref, pre_ref,
+    ):
         ids = ids_ref[...]
         for i in range(image_count // block):
             rows = slice(i * block, (i + 1) * block)
-            units = unit_rows(nt_dot(images_ref[rows, :width], matrix_ref[...]))
+            line = images_ref[rows, :width]
+            units = unit_rows(projected(core_ref, line, (mine_ref, theirs_ref), pre_ref))
             weighted = slopes(scalar_ref, texts_ref[...], ids, units, images_ref[rows, width:])
             term = tn_dot(weighted, units)
             if i == 0:
@@ -248,27 +268,30 @@
             jax.ShapeDtypeStruct((image_count, width), F32),
             jax.ShapeDtypeStruct((text_count, width), F32),
         ),
-        in_specs=[pl.BlockSpec(memory_space=SMEM)] + [pl.BlockSpec(memory_space=VMEM)] * 4,
+        in_specs=[pl.BlockSpec(memory_space=SMEM)] * 2 + [pl.BlockSpec(memory_space=VMEM)] * 5,
         out_specs=[pl.BlockSpec(memory_space=VMEM)] * 2,
+        scratch_shapes=[pltpu.VMEM((block, width), F32)],
         flops=2 * image_count * width * (3 * text_count + width),
         transcendentals=text_count * image_count,
         moved=2 * width * (text_count + 2 * image_count),
-    )(scalars, texts, text_ids, images, matrix)
-
-
-def second_tile(scalars, texts, text_ids, images, matrix, text_sum, cuts):
+    )(core, scalars, texts, text_ids, images, *matrix)
+
+
+def second_tile(core, scalars, texts, text_ids, images, matrix, text_sum, cuts):
     text_count, width = texts.shape
     image_count = images.shape[0]
     block = min(256, image_count)
 
     def kernel(
-        scalar_ref, texts_ref, ids_ref, images_ref, matrix_ref, sum_ref, weighted_ref, *refs
+        core_ref, scalar_ref, texts_ref, ids_ref, images_ref, mine_ref, theirs_ref, sum_ref,
+        weighted_ref, *refs,
     ):
-        out_refs, total_ref = refs[:-1], refs[-1]
+        out_refs, (total_ref, pre_ref) = refs[:-2], refs[-2:]
         ids = ids_ref[...]
         for i in range(image_count // block):
             rows = slice(i * block, (i + 1) * block)
-            units = unit_rows(nt_dot(images_ref[rows, :width], matrix_ref[...]))
+            line = images_ref[rows, :width]
+            units = unit_rows(projected(core_ref, line, (mine_ref, theirs_ref), pre_ref))
             weighted = slopes(scalar_ref, texts_ref[...], ids, units, images_ref[rows, width:])
             weighted_ref[rows, :] = weighted
             term = tn_dot(weighted, units)
@@ -288,13 +311,13 @@
             jax.ShapeDtypeStruct((cuts[0], width), F32),
             *(jax.ShapeDtypeStruct((size, width), BF) for size in cuts[1:]),
         ),
-        in_specs=[pl.BlockSpec(memory_space=SMEM)] + [pl.BlockSpec(memory_space=VMEM)] * 5,
+        in_specs=[pl.BlockSpec(memory_space=SMEM)] * 2 + [pl.BlockSpec(memory_space=VMEM)] * 6,
         out_specs=[pl.BlockSpec(memory_space=VMEM)] * (1 + len(cuts)),
-        scratch_shapes=[pltpu.VMEM((text_count, width), F32)],
+        scratch_shapes=[pltpu.VMEM((text_count, width), F32), pltpu.VMEM((block, width), F32)],
         flops=2 * image_count * width * (2 * text_count + width),
         transcendentals=text_count * image_count,
         moved=2 * width * (text_count + 2 * image_count),
-    )(scalars, texts, text_ids, images, matrix, text_sum)
+    )(core, scalars, texts, text_ids, images, *matrix, text_sum)
 
 
 def image_terms(weighted, texts):
@@ -362,7 +385,15 @@
 
 
 def gather_matrix(piece):
-    return to_all(piece, ("y_lo", "x"), 8).reshape(-1, piece.shape[1])
+    return lax.all_gather(piece, ("y_lo", "x"), axis=0, tiled=True)
+
+
+def corner(*arrays):
+    return sum(array[(0,) * (array.ndim - 1)][:1].astype(F32) for array in arrays)
+
+
+def after(index, number):
+    return index + (number != number).astype(jnp.int32)
 
 
 def shards(
@@ -383,13 +414,11 @@
     spot = lax.axis_index("z_hi").astype(jnp.int32).reshape(1)
     count = caption_embedding.shape[0]
 
-    exit_matrix = lax.all_gather(
-        pooling_exit_matrix.T, ("core", "y_lo", "x"), axis=0, tiled=True
-    )
     text_own = gather_matrix(caption_head_matrix.T)
-
-    near = [take_from(caption_embedding, Z, d, NZ) if d else caption_embedding for d in (-4, 0, 4, 8)]
-
+    exit_own = gather_matrix(pooling_exit_matrix.T)
+
+    captions = caption_embedding
+    near = [take_from(captions, Z, d, NZ) if d else captions for d in (-4, 0, 4, 8)]
     head_of = jnp.arange(width, dtype=jnp.int32) // (width // heads)
     spread = (head_of[None, :] == jnp.arange(heads, dtype=jnp.int32)[:, None]).astype(BF)
     gather = (head_of[:, None] == jnp.arange(heads, dtype=jnp.int32)[None, :]).astype(BF)
@@ -407,10 +436,6 @@
     digits = jnp.where(lane == 0, index >> 7, jnp.where(lane == 1, index & 127, 0))
     lines = jnp.concatenate([pooled.astype(BF), digits.astype(F32).astype(BF)], axis=1)
 
-    text_own, lines, near, text_ids, scalars, gather = lax.optimization_barrier(
-        (text_own, lines, near, text_ids, scalars, gather)
-    )
-    text_matrix = text_own, swap_cores(text_own)
     own_images = to_all(lines, XY, 16).reshape(-1, width + TAIL)
     near = jnp.concatenate(near, axis=0)
     pieces = [
@@ -420,29 +445,34 @@
         take_from(near[count : 3 * count], Z, 2, NZ),
         take_from(near[: 2 * count], Z, -2, NZ),
     ]
-    own_images, pieces = lax.optimization_barrier((own_images, pieces))
-    other_images = swap_cores(own_images)
-
-    texts = unit_texts(place, pieces, text_matrix)
-    own_part, text_sum = first_tile(scalars, texts, text_ids, own_images, exit_matrix)
+    text_matrix = text_own, swap_cores(text_own)
+    held_exit, held_images, there = lax.optimization_barrier(
+        (exit_own, own_images, corner(*pieces[1:]))
+    )
+    exit_matrix = exit_own, swap_cores(held_exit)
+    other_images = swap_cores(held_images)
+
+    texts, text_pre = unit_texts(after(place, there), pieces, text_matrix)
+    own_part, text_sum = first_tile(
+        place, scalars, texts, text_ids, own_images, exit_matrix
+    )
     weighted, mine, *away = second_tile(
-        scalars, texts, text_ids, other_images, exit_matrix, text_sum,
+        place, scalars, texts, text_ids, other_images, exit_matrix, text_sum,
         [piece.shape[0] for piece in pieces],
     )
     away = [take_from(part, Z, -d, NZ) for part, d in zip(away, (1, -1, 2, -2))]
     other_part = swap_cores(image_terms(weighted, texts))
     chip_images = add_pair(own_part, other_part)
     image_parts = lax.all_to_all(chip_images.reshape(16, images, width), XY, 0, 0, tiled=True)
-    chip_texts = add_texts(spot, mine, away[:2], away[3], away[2])
-    image_parts, chip_texts = lax.optimization_barrier((image_parts, chip_texts))
+    chip_texts = add_texts(after(spot, corner(image_parts)), mine, away[:2], away[3], away[2])
     text_parts = lax.all_to_all(chip_texts, "z_hi", 0, 0, tiled=True)
 
-    dpooled = project_back(place, pooled, image_parts, (exit_matrix,), F32)
+    dpooled = project_back(place, pooled, image_parts, exit_matrix, F32)
     d_patches = attention_backward(
         tiles, attend, dpooled, query_key_product.T, spread, gather, patches
     )
-    text_matrix, d_patches = lax.optimization_barrier((text_matrix, d_patches))
-    d_text = project_back(place, caption_embedding, text_parts, text_matrix, BF)
+    d_text = project_back(
+        after(place, corner(d_patches)), text_pre, text_parts, text_matrix, BF, before=True)
     return (d_patches.reshape(images, patches, width), d_text)
 
 

time: 199 us -> 227 us (1.14)
  waiting for transfers between devices: 45 us -> 68.9 us
  between operations: 16.5 us -> 21.5 us
  local copies, waits for them, and re-layouts: 19.4 us -> 16.9 us
  Pallas kernels: 30.2 us -> 32.6 us
    all_gather x1 -> x2, waiting for transfers between devices: 0.02 us -> 48 us  [gather_matrix(): return lax.all_gather(piece, ('y_lo', 'x'), axis=0, tiled=True)]
    all_to_all x2 -> x1, waiting for transfers between devices: 14.6 us -> 0.01 us  [to_all(): return lax.all_to_all(spread, axes, 0, 0, tiled=True)]
    ppermute x11, waiting for transfers between devices: 15.9 us -> 6.81 us  [take_from(): lax.ppermute(values, axis, [((i + distance) % size, i) for i in range(siz...]
    all_to_all x2 -> x1, starting transfers between devices: 12.9 us -> 7.54 us  [to_all(): return lax.all_to_all(spread, axes, 0, 0, tiled=True)]
    unnamed x72 -> x48, local copies, waits for them, and re-layouts: 16 us -> 11.8 us
    all_to_all x1, starting transfers between devices: 4.32 us -> 8.5 us  [shards(): text_parts = lax.all_to_all(chip_texts, 'z_hi', 0, 0, tiled=True)]
    slice x0 -> x6, local copies, waits for them, and re-layouts: none -> 3.83 us  [corner(): array[(0,) * (array.ndim - 1)][:1].astype(F32)]
    ppermute x3 -> x4, starting transfers between devices: 6.4 us -> 8.33 us  [swap_cores(): return lax.ppermute(values, 'core', [(0, 1), (1, 0)])]
  transfers between devices with their start and end apart: 19 -> 20, of which waited for: 7 -> 7; matrix products, arithmetic and copies ran while one was open for 2% -> 3% of each run, Pallas kernels for 10% -> 9%
where the time goes in v4:
time: 227 us; the launch traced here: 225 us
  starting transfers between devices  85 us (37%)
  waiting for transfers between devices  68.9 us (30%)
  Pallas kernels  32.6 us (14%)
  between operations  21.5 us (9%)
  local copies, waits for them, and re-layouts  16.9 us (7%)
    ppermute x11, starting transfers between devices, take_from(): lax.ppermute(values, axis, [((i + distance) % size, i) for i in range(siz...  52.9 us
    all_gather x2, waiting for transfers between devices, gather_matrix(): return lax.all_gather(piece, ('y_lo', 'x'), axis=0, tiled=True)  48 us
    unnamed x48, local copies, waits for them, and re-layouts  11.8 us
    all_to_all x1, waiting for transfers between devices, shards(): text_parts = lax.all_to_all(chip_texts, 'z_hi', 0, 0, tiled=True)  9.21 us
    all_to_all x1, starting transfers between devices, shards(): text_parts = lax.all_to_all(chip_texts, 'z_hi', 0, 0, tiled=True)  8.5 us
    ppermute x4, starting transfers between devices, swap_cores(): return lax.ppermute(values, 'core', [(0, 1), (1, 0)])  8.33 us
    all_to_all x1, starting transfers between devices, shards(): lax.all_to_all(chip_images.reshape(16, images, width), XY, 0, 0, tiled=True)  7.64 us
    all_to_all x1, starting transfers between devices, to_all(): return lax.all_to_all(spread, axes, 0, 0, tiled=True)  7.54 us
  transfers between devices with their start and end apart: 20, of which 7 were waited for; matrix products, arithmetic and copies ran while one was open for 3% of the time, Pallas kernels for 9%

profile of v4, /device:TPU:6, one launch (start us, length us, event | category | flops | bytes accessed | tf_op | source)
XLA Modules:
  0.0 225.4 jit_solution(1839459116362028663)
XLA Ops:
  7.2 0.7 all-gather.5.cloned.1.call-update
  7.9 9.1 %collective-permute-start = (bf16[32,1152]{1,0:T(8,128)(2,1)}, bf16[32,1152]{1,0:T(8,128)(2,1)S(1)}, u32[]{:S(2)}, u32[]{:S(2)}) collective-permute-start(bf16[32,1152]{1,0:T(8,128)(2,1)} %param.13), channel_id=1, source_target_pairs={{384,0},{416,32},{448,64},{480,96},{0,128},{32,160},{64,192},{96,2... | collective-permute-start | bytes 221192 | tf_op jit(solution)/shard_map/ppermute | solution.py:22
  17.1 5.6 %collective-permute-start.1 = (bf16[32,1152]{1,0:T(8,128)(2,1)}, bf16[32,1152]{1,0:T(8,128)(2,1)S(1)}, u32[]{:S(2)}, u32[]{:S(2)}) collective-permute-start(bf16[32,1152]{1,0:T(8,128)(2,1)} %param.13), channel_id=1, source_target_pairs={{128,0},{160,32},{192,64},{224,96},{256,128},{288,160},{320,192},{... | collective-permute-start | bytes 221192 | tf_op jit(solution)/shard_map/ppermute | solution.py:22
  22.6 10.8 %collective-permute-start.2 = (bf16[32,1152]{1,0:T(8,128)(2,1)}, bf16[32,1152]{1,0:T(8,128)(2,1)S(1)}, u32[]{:S(2)}, u32[]{:S(2)}) collective-permute-start(bf16[32,1152]{1,0:T(8,128)(2,1)} %param.13), channel_id=1, source_target_pairs={{256,0},{288,32},{320,64},{352,96},{384,128},{416,160},{448,192},{... | collective-permute-start | bytes 221192 | tf_op jit(solution)/shard_map/ppermute | solution.py:22
  33.5 1.0 copy.12.qk_ref
  34.5 1.7 copy-done
  36.2 2.6 %shard_map.113 = (f32[1024,16]{1,0:T(8,128)S(1)}, f32[32,1152]{1,0:T(8,128)S(1)}) custom-call(bf16[1024,1152]{1,0:T(8,128)(2,1)S(1)} %bitcast.12, bf16[1152,16]{1,0:T(8,128)(2,1)S(1)} %copy.12.qk_ref, bf16[16,1152]{1,0:T(8,128)(2,1)S(1)} %fusion.1.spread_ref), custom_call_target="tpu_custom_call" | custom-call | flops 603979776 | bytes 2359296 | tf_op jit(solution)/shard_map/pallas_call | solution.py:72
  38.8 0.9 copy-done.8
  39.8 1.2 broadcast_in_dim.55
  41.0 7.5 %all-to-all-start = ((bf16[16,32,1280]{2,1,0:T(8,128)(2,1)}), bf16[16,32,1280]{2,1,0:T(8,128)(2,1)}, u32[]{:S(2)}, u32[]{:S(2)}) async-start(bf16[16,32,1280]{2,1,0:T(8,128)(2,1)} %broadcast_in_dim.55), calls=%async_computation | async-start | bytes 2621440 | tf_op jit(solution)/shard_map/all_to_all | solution.py:384
  48.6 2.0 collective-permute-start.3
  50.7 3.8 %collective-permute-start.4 = (bf16[128,1152]{1,0:T(8,128)(2,1)S(1)}, bf16[128,1152]{1,0:T(8,128)(2,1)S(1)}, u32[]{:S(2)}, u32[]{:S(2)}) collective-permute-start(bf16[128,1152]{1,0:T(8,128)(2,1)S(1)} %constant_dynamic-update-slice_fusion.refs_0_), channel_id=1, source_target_pairs={{480,0},{0,32},{32,64},{64,96},{96,128},{128,160},{160,192},{192,2... | collective-permute-start | bytes 884744 | tf_op jit(solution)/shard_map/ppermute | solution.py:22
  54.5 1.9 collective-permute-start.5
  56.5 4.8 %collective-permute-start.6 = (bf16[64,1152]{1,0:T(8,128)(2,1)S(1)}, bf16[64,1152]{1,0:T(8,128)(2,1)S(1)}, u32[]{:S(2)}, u32[]{:S(2)}) collective-permute-start(bf16[64,1152]{1,0:T(8,128)(2,1)S(1)} %get-tuple-element.32), channel_id=1, source_target_pairs={{448,0},{480,32},{0,64},{32,96},{64,128},{96,160},{128,192},{160,2... | collective-permute-start | bytes 442376 | tf_op jit(solution)/shard_map/ppermute | solution.py:22
  61.3 7.1 %all-gather.5.cloned.1.call-done.refs_5_.refs_0_ = bf16[576,1152]{1,0:T(8,128)(2,1)} async-done(((bf16[72,1152]{1,0:T(8,128)(2,1)}), bf16[576,1152]{1,0:T(8,128)(2,1)}) %all-gather.5.cloned.1.call-update) | async-done | bytes 1327120 | tf_op jit(solution)/shard_map/all_gather | solution.py:388
  68.4 1.9 collective-permute-start.7
  72.5 0.7 copy-done.13
  75.8 40.9 %all-gather.3.cloned.1.call-done.mine_ref.refs_0_ = bf16[576,1152]{1,0:T(8,128)(2,1)} async-done(((bf16[72,1152]{1,0:T(8,128)(2,1)}), bf16[576,1152]{1,0:T(8,128)(2,1)}) %all-gather.3.cloned.1.call-update) | async-done | bytes 1327120 | tf_op jit(solution)/shard_map/all_gather | solution.py:388
  116.7 1.9 collective-permute-start.8
  118.6 2.6 %collective-permute-start.9 = (bf16[512,1280]{1,0:T(8,128)(2,1)}, bf16[512,1280]{1,0:T(8,128)(2,1)}, u32[]{:S(2)}, u32[]{:S(2)}) collective-permute-start(bf16[512,1280]{1,0:T(8,128)(2,1)} %bitcast.3.images_ref), channel_id=1, source_target_pairs={{0,1},{1,0},{2,3},{3,2},{4,5},{5,4},{6,7},{7,6},{8,9},{9,8},{10,11... | collective-permute-start | bytes 3932168 | tf_op jit(solution)/shard_map/ppermute | solution.py:26
  123.5 1.1 copy-done.5
  124.6 1.3 copy-done.2
  125.9 1.3 copy-done.6
  127.2 1.0 copy-done.14
  128.2 3.1 %shard_map.114 = (bf16[512,1152]{1,0:T(8,128)(2,1)S(1)}, f32[32,1152]{1,0:T(8,128)S(1)}) custom-call(s32[1]{0:T(128)S(6)} %add.90.core_ref, bf16[128,1152]{1,0:T(8,128)(2,1)S(1)} %constant_dynamic-update-slice_fusion.refs_0_, bf16[128,1152]{1,0:T(8,128)(2,1)S(1)} %collective-permute-done.3.refs_1_, bf16[128,1152]{1,0:T(8,128)(2,1)S(1)} %copy-done.14, ...), custom_call_target="tpu_custom_call" | custom-call | flops 1358954496 | bytes 2654208 | tf_op jit(solution)/shard_map/pallas_call | solution.py:177
  131.3 7.3 %shard_map.115 = (f32[512,1152]{1,0:T(8,128)S(1)}, f32[512,1152]{1,0:T(8,128)S(1)}) custom-call(s32[1]{0:T(128)} %bitcast.1.core_ref, f32[3]{0:T(128)S(1)} %pad_maximum_fusion.3.scalar_ref, bf16[512,1152]{1,0:T(8,128)(2,1)S(1)} %get-tuple-element.20.texts_ref, f32[1,512]{1,0:T(1,128)S(1)} %convert_element_type.79.ids_ref, ...), custom_call_target="tpu_custom_call" | custom-call | flops 3170893824 | bytes 3538944 | tf_op jit(solution)/shard_map/pallas_call | solution.py:265
  138.7 6.7 %shard_map.116 = (bf16[512,512]{1,0:T(8,128)(2,1)S(1)}, f32[128,1152]{1,0:T(8,128)S(1)}, bf16[128,1152]{1,0:T(8,128)(2,1)S(1)}, bf16[128,1152]{1,0:T(8,128)(2,1)...) custom-call(s32[1]{0:T(128)} %bitcast.1.core_ref, f32[3]{0:T(128)S(1)} %pad_maximum_fusion.3.scalar_ref, ...), custom_call_target="tpu_custom_call" | custom-call | flops 2566914048 | bytes 3538944 | tf_op jit(solution)/shard_map/pallas_call | solution.py:307
  145.4 0.7 copy-done.15
  146.1 0.7 copy-done.16
  148.2 0.8 shard_map.117
  149.0 1.9 collective-permute-start.10
  151.0 2.8 %collective-permute-done.10.part_ref = bf16[512,1152]{1,0:T(8,128)(2,1)S(1)} collective-permute-done((bf16[512,1152]{1,0:T(8,128)(2,1)S(1)}, bf16[512,1152]{1,0:T(8,128)(2,1)S(1)}, u32[]{:S(2)}, u32[]{:S(2)}) %collective-permute-start.10) | collective-permute-done | bytes 1179680 | tf_op jit(solution)/shard_map/ppermute | solution.py:26
  153.8 1.2 shard_map.118
  155.0 7.6 %all-to-all-start.1 = ((bf16[16,32,1152]{2,1,0:T(8,128)(2,1)}), bf16[16,32,1152]{2,1,0:T(8,128)(2,1)S(1)}, u32[]{:S(2)}, u32[]{:S(2)}) async-start(bf16[16,32,1152]{2,1,0:T(8,128)(2,1)} %bitcast.6), calls=%async_computation.1 | async-start | bytes 2359296 | tf_op jit(solution)/shard_map/all_to_all | solution.py:466
  162.6 3.4 %collective-permute-start.11 = (bf16[128,1152]{1,0:T(8,128)(2,1)}, bf16[128,1152]{1,0:T(8,128)(2,1)}, u32[]{:S(2)}, u32[]{:S(2)}) collective-permute-start(bf16[128,1152]{1,0:T(8,128)(2,1)} %copy-done.16), channel_id=1, source_target_pairs={{480,0},{0,32},{32,64},{64,96},{96,128},{128,160},{160,192},{192,2... | collective-permute-start | bytes 884744 | tf_op jit(solution)/shard_map/ppermute | solution.py:22
  166.1 4.6 %collective-permute-start.12 = (bf16[128,1152]{1,0:T(8,128)(2,1)}, bf16[128,1152]{1,0:T(8,128)(2,1)}, u32[]{:S(2)}, u32[]{:S(2)}) collective-permute-start(bf16[128,1152]{1,0:T(8,128)(2,1)} %copy-done.15), channel_id=1, source_target_pairs={{32,0},{64,32},{96,64},{128,96},{160,128},{192,160},{224,192},{256... | collective-permute-start | bytes 884744 | tf_op jit(solution)/shard_map/ppermute | solution.py:22
  170.7 4.7 %collective-permute-start.13 = (bf16[64,1152]{1,0:T(8,128)(2,1)}, bf16[64,1152]{1,0:T(8,128)(2,1)S(1)}, u32[]{:S(2)}, u32[]{:S(2)}) collective-permute-start(bf16[64,1152]{1,0:T(8,128)(2,1)} %copy-done.18), channel_id=1, source_target_pairs={{64,0},{96,32},{128,64},{160,96},{192,128},{224,160},{256,192},{28... | collective-permute-start | bytes 442376 | tf_op jit(solution)/shard_map/ppermute | solution.py:22
  175.4 2.0 collective-permute-start.14
  177.5 1.4 all-to-all-done.1.parts_ref
  180.7 2.9 %collective-permute-done.13.low_ref = bf16[64,1152]{1,0:T(8,128)(2,1)S(1)} collective-permute-done((bf16[64,1152]{1,0:T(8,128)(2,1)}, bf16[64,1152]{1,0:T(8,128)(2,1)S(1)}, u32[]{:S(2)}, u32[]{:S(2)}) %collective-permute-start.13) | collective-permute-done | bytes 147488 | tf_op jit(solution)/shard_map/ppermute | solution.py:22
  183.5 3.9 %collective-permute-done.14.high_ref = bf16[64,1152]{1,0:T(8,128)(2,1)} collective-permute-done((bf16[64,1152]{1,0:T(8,128)(2,1)}, bf16[64,1152]{1,0:T(8,128)(2,1)}, u32[]{:S(2)}, u32[]{:S(2)}) %collective-permute-start.14) | collective-permute-done | bytes 147488 | tf_op jit(solution)/shard_map/ppermute | solution.py:22
  187.5 2.0 shard_map.121
  189.5 8.5 %all-to-all-start.2 = ((bf16[4,32,1152]{2,1,0:T(8,128)(2,1)}), bf16[4,32,1152]{2,1,0:T(8,128)(2,1)S(1)}, u32[]{:S(2)}, u32[]{:S(2)}) async-start(bf16[4,32,1152]{2,1,0:T(8,128)(2,1)} %shard_map.121), calls=%async_computation.2 | async-start | bytes 589824 | tf_op jit(solution)/shard_map/all_to_all | solution.py:468
  198.2 3.2 %shard_map.119.dpooled_ref = f32[32,1152]{1,0:T(8,128)S(1)} custom-call(s32[1]{0:T(128)} %bitcast.1.core_ref, f32[32,1152]{1,0:T(8,128)S(1)} %get-tuple-element.18.rows_ref, bf16[16,32,1152]{2,1,0:T(8,128)(2,1)S(1)} %all-to-all-done.1.parts_ref, bf16[576,1152]{1,0:T(8,128)(2,1)S(1)} %copy-done.4, bf16[576,1152]{1,0:T(8,128)(2,1)} %collective-permute-done.8.theirs_ref.refs_1_), custom_call_target="tpu_custom_call" | custom-call | flops 169869312 | bytes 2654208 | tf_op jit(solution)/shard_map/pallas_call | solution.py:221
  201.5 4.2 %shard_map.120 = bf16[1024,1152]{1,0:T(8,128)(2,1)} custom-call(bf16[1024,1152]{1,0:T(8,128)(2,1)S(1)} %bitcast.13, f32[1024,16]{1,0:T(8,128)S(1)} %copy-done.9, f32[32,1152]{1,0:T(8,128)S(1)} %shard_map.119.dpooled_ref, bf16[16,1152]{1,0:T(8,128)(2,1)S(1)} %bitcast.14, bf16[16,1152]{1,0:T(8,128)(2,1)S(1)} %fusion.1.spread_ref, ...), custom_call_target="tpu_custom_call" | custom-call | flops 1207959552 | bytes 4718592 | tf_op jit(solution)/shard_map/pallas_call | solution.py:118
  205.6 1.2 slice.50
  207.9 9.2 %all-to-all-done.2.parts_ref = bf16[4,32,1152]{2,1,0:T(8,128)(2,1)S(1)} async-done(((bf16[4,32,1152]{2,1,0:T(8,128)(2,1)}), bf16[4,32,1152]{2,1,0:T(8,128)(2,1)S(1)}, u32[]{:S(2)}, u32[]{:S(2)}) %all-to-all-start.2) | async-done | bytes 294944 | tf_op jit(solution)/shard_map/all_to_all | solution.py:468
  217.1 1.4 shard_map.122
  (73 shorter events, 4.8 us)
Async XLA Ops:
  7.2 61.2 %all-gather.5.cloned.1.call-start = ((), (), s32[]{:S(2)}) async-start(), calls=%async_computation.4 | async-start | bytes 1492992 | tf_op jit(solution)/shard_map/all_gather | solution.py:388
  7.9 108.8 %all-gather.3.cloned.1.call-start = ((), (), s32[]{:S(2)}) async-start(), calls=%async_computation.3 | async-start | bytes 1492992 | tf_op jit(solution)/shard_map/all_gather | solution.py:388
  7.9 40.6 %collective-permute-start = (bf16[32,1152]{1,0:T(8,128)(2,1)}, bf16[32,1152]{1,0:T(8,128)(2,1)S(1)}, u32[]{:S(2)}, u32[]{:S(2)}) collective-permute-start(bf16[32,1152]{1,0:T(8,128)(2,1)} %param.13), channel_id=1, source_target_pairs={{384,0},{416,32},{448,64},{480,96},{0,128},{32,160},{64,192},{96,2... | collective-permute-start | bytes 221192 | tf_op jit(solution)/shard_map/ppermute | solution.py:22
  17.1 31.5 %collective-permute-start.1 = (bf16[32,1152]{1,0:T(8,128)(2,1)}, bf16[32,1152]{1,0:T(8,128)(2,1)S(1)}, u32[]{:S(2)}, u32[]{:S(2)}) collective-permute-start(bf16[32,1152]{1,0:T(8,128)(2,1)} %param.13), channel_id=1, source_target_pairs={{128,0},{160,32},{192,64},{224,96},{256,128},{288,160},{320,192},{... | collective-permute-start | bytes 221192 | tf_op jit(solution)/shard_map/ppermute | solution.py:22
  22.6 26.0 %collective-permute-start.2 = (bf16[32,1152]{1,0:T(8,128)(2,1)}, bf16[32,1152]{1,0:T(8,128)(2,1)S(1)}, u32[]{:S(2)}, u32[]{:S(2)}) collective-permute-start(bf16[32,1152]{1,0:T(8,128)(2,1)} %param.13), channel_id=1, source_target_pairs={{256,0},{288,32},{320,64},{352,96},{384,128},{416,160},{448,192},{... | collective-permute-start | bytes 221192 | tf_op jit(solution)/shard_map/ppermute | solution.py:22
  34.5 1.7 copy-start
  36.2 3.5 %copy-start.21 = (s32[32]{0:T(128)S(1)}, s32[32]{0:T(128)}, u32[]{:S(2)}) copy-start(s32[32]{0:T(128)} %param.15) | copy-start | bytes 388
  38.8 0.9 copy-start.8
  41.0 7.6 %copy-start.19 = (bf16[32,1152]{1,0:T(8,128)(2,1)S(1)}, bf16[32,1152]{1,0:T(8,128)(2,1)}, u32[]{:S(2)}) copy-start(bf16[32,1152]{1,0:T(8,128)(2,1)} %param.13) | copy-start | bytes 221188
  41.0 82.2 %copy-start.20 = (s32[16]{0:T(128)S(1)}, s32[16]{0:T(128)}, u32[]{:S(2)}) copy-start(s32[16]{0:T(128)} %constant.65.clone) | copy-start | bytes 196
  41.0 34.8 %all-to-all-start = ((bf16[16,32,1280]{2,1,0:T(8,128)(2,1)}), bf16[16,32,1280]{2,1,0:T(8,128)(2,1)}, u32[]{:S(2)}, u32[]{:S(2)}) async-start(bf16[16,32,1280]{2,1,0:T(8,128)(2,1)} %broadcast_in_dim.55), calls=%async_computation | async-start | bytes 2621440 | tf_op jit(solution)/shard_map/all_to_all | solution.py:384
  48.6 22.7 %collective-permute-start.3 = (bf16[128,1152]{1,0:T(8,128)(2,1)S(1)}, bf16[128,1152]{1,0:T(8,128)(2,1)S(1)}, u32[]{:S(2)}, u32[]{:S(2)}) collective-permute-start(bf16[128,1152]{1,0:T(8,128)(2,1)S(1)} %constant_dynamic-update-slice_fusion.refs_0_), channel_id=1, source_target_pairs={{32,0},{64,32},{96,64},{128,96},{160,128},{192,160},{224,192},{256... | collective-permute-start | bytes 884744 | tf_op jit(solution)/shard_map/ppermute | solution.py:22
  50.7 21.2 %collective-permute-start.4 = (bf16[128,1152]{1,0:T(8,128)(2,1)S(1)}, bf16[128,1152]{1,0:T(8,128)(2,1)S(1)}, u32[]{:S(2)}, u32[]{:S(2)}) collective-permute-start(bf16[128,1152]{1,0:T(8,128)(2,1)S(1)} %constant_dynamic-update-slice_fusion.refs_0_), channel_id=1, source_target_pairs={{480,0},{0,32},{32,64},{64,96},{96,128},{128,160},{160,192},{192,2... | collective-permute-start | bytes 884744 | tf_op jit(solution)/shard_map/ppermute | solution.py:22
  54.5 15.8 %collective-permute-start.5 = (bf16[64,1152]{1,0:T(8,128)(2,1)S(1)}, bf16[64,1152]{1,0:T(8,128)(2,1)S(1)}, u32[]{:S(2)}, u32[]{:S(2)}) collective-permute-start(bf16[64,1152]{1,0:T(8,128)(2,1)S(1)} %get-tuple-element.33), channel_id=1, source_target_pairs={{64,0},{96,32},{128,64},{160,96},{192,128},{224,160},{256,192},{28... | collective-permute-start | bytes 442376 | tf_op jit(solution)/shard_map/ppermute | solution.py:22
  56.5 14.4 %collective-permute-start.6 = (bf16[64,1152]{1,0:T(8,128)(2,1)S(1)}, bf16[64,1152]{1,0:T(8,128)(2,1)S(1)}, u32[]{:S(2)}, u32[]{:S(2)}) collective-permute-start(bf16[64,1152]{1,0:T(8,128)(2,1)S(1)} %get-tuple-element.32), channel_id=1, source_target_pairs={{448,0},{480,32},{0,64},{32,96},{64,128},{96,160},{128,192},{160,2... | collective-permute-start | bytes 442376 | tf_op jit(solution)/shard_map/ppermute | solution.py:22
  68.4 55.1 %collective-permute-start.7 = (bf16[576,1152]{1,0:T(8,128)(2,1)}, bf16[576,1152]{1,0:T(8,128)(2,1)S(1)}, u32[]{:S(2)}, u32[]{:S(2)}) collective-permute-start(bf16[576,1152]{1,0:T(8,128)(2,1)} %all-gather.5.cloned.1.call-done.refs_5_.refs_0_), channel_id=1, source_target_pairs={{0,1},{1,0},{2,3},{3,2},{4,5},{5,4},{6,7},{7,6},{8,9},{9,8},{10,11... | collective-permute-start | bytes 3981320 | tf_op jit(solution)/shard_map/ppermute | solution.py:26
  72.5 0.7 copy-start.13
  116.7 14.6 %collective-permute-start.8 = (bf16[576,1152]{1,0:T(8,128)(2,1)}, bf16[576,1152]{1,0:T(8,128)(2,1)}, u32[]{:S(2)}, u32[]{:S(2)}) collective-permute-start(bf16[576,1152]{1,0:T(8,128)(2,1)} %all-gather.3.cloned.1.call-done.mine_ref.refs_0_), channel_id=1, source_target_pairs={{0,1},{1,0},{2,3},{3,2},{4,5},{5,4},{6,7},{7,6},{8,9},{9,8},{10,11... | collective-permute-start | bytes 3981320 | tf_op jit(solution)/shard_map/ppermute | solution.py:26
  118.6 20.0 %collective-permute-start.9 = (bf16[512,1280]{1,0:T(8,128)(2,1)}, bf16[512,1280]{1,0:T(8,128)(2,1)}, u32[]{:S(2)}, u32[]{:S(2)}) collective-permute-start(bf16[512,1280]{1,0:T(8,128)(2,1)} %bitcast.3.images_ref), channel_id=1, source_target_pairs={{0,1},{1,0},{2,3},{3,2},{4,5},{5,4},{6,7},{7,6},{8,9},{9,8},{10,11... | collective-permute-start | bytes 3932168 | tf_op jit(solution)/shard_map/ppermute | solution.py:26
  123.5 1.1 copy-start.5
  124.6 1.3 copy-start.2
  125.9 1.3 copy-start.6
  127.2 1.0 copy-start.14
  128.2 3.2 %copy-start.4 = (bf16[576,1152]{1,0:T(8,128)(2,1)S(1)}, bf16[576,1152]{1,0:T(8,128)(2,1)}, u32[]{:S(2)}) copy-start(bf16[576,1152]{1,0:T(8,128)(2,1)} %all-gather.3.cloned.1.call-done.mine_ref.refs_0_) | copy-start | bytes 3981316
  131.3 7.3 %copy-start.10 = (f32[32,1152]{1,0:T(8,128)}, f32[32,1152]{1,0:T(8,128)S(1)}, u32[]{:S(2)}) copy-start(f32[32,1152]{1,0:T(8,128)S(1)} %get-tuple-element.26.rows_ref) | copy-start | bytes 442372
  145.4 0.7 copy-start.15
  146.1 0.7 copy-start.16
  146.9 0.6 copy-start.17
  147.5 0.7 copy-start.18
  149.0 4.7 %collective-permute-start.10 = (bf16[512,1152]{1,0:T(8,128)(2,1)S(1)}, bf16[512,1152]{1,0:T(8,128)(2,1)S(1)}, u32[]{:S(2)}, u32[]{:S(2)}) collective-permute-start(bf16[512,1152]{1,0:T(8,128)(2,1)S(1)} %shard_map.117), channel_id=1, source_target_pairs={{0,1},{1,0},{2,3},{3,2},{4,5},{5,4},{6,7},{7,6},{8,9},{9,8},{10,11... | collective-permute-start | bytes 3538952 | tf_op jit(solution)/shard_map/ppermute | solution.py:26
  155.0 23.9 %all-to-all-start.1 = ((bf16[16,32,1152]{2,1,0:T(8,128)(2,1)}), bf16[16,32,1152]{2,1,0:T(8,128)(2,1)S(1)}, u32[]{:S(2)}, u32[]{:S(2)}) async-start(bf16[16,32,1152]{2,1,0:T(8,128)(2,1)} %bitcast.6), calls=%async_computation.1 | async-start | bytes 2359296 | tf_op jit(solution)/shard_map/all_to_all | solution.py:466
  162.6 24.8 %collective-permute-start.11 = (bf16[128,1152]{1,0:T(8,128)(2,1)}, bf16[128,1152]{1,0:T(8,128)(2,1)}, u32[]{:S(2)}, u32[]{:S(2)}) collective-permute-start(bf16[128,1152]{1,0:T(8,128)(2,1)} %copy-done.16), channel_id=1, source_target_pairs={{480,0},{0,32},{32,64},{64,96},{96,128},{128,160},{160,192},{192,2... | collective-permute-start | bytes 884744 | tf_op jit(solution)/shard_map/ppermute | solution.py:22
  166.1 21.4 %collective-permute-start.12 = (bf16[128,1152]{1,0:T(8,128)(2,1)}, bf16[128,1152]{1,0:T(8,128)(2,1)}, u32[]{:S(2)}, u32[]{:S(2)}) collective-permute-start(bf16[128,1152]{1,0:T(8,128)(2,1)} %copy-done.15), channel_id=1, source_target_pairs={{32,0},{64,32},{96,64},{128,96},{160,128},{192,160},{224,192},{256... | collective-permute-start | bytes 884744 | tf_op jit(solution)/shard_map/ppermute | solution.py:22
  170.7 12.8 %collective-permute-start.13 = (bf16[64,1152]{1,0:T(8,128)(2,1)}, bf16[64,1152]{1,0:T(8,128)(2,1)S(1)}, u32[]{:S(2)}, u32[]{:S(2)}) collective-permute-start(bf16[64,1152]{1,0:T(8,128)(2,1)} %copy-done.18), channel_id=1, source_target_pairs={{64,0},{96,32},{128,64},{160,96},{192,128},{224,160},{256,192},{28... | collective-permute-start | bytes 442376 | tf_op jit(solution)/shard_map/ppermute | solution.py:22
  175.4 12.0 %collective-permute-start.14 = (bf16[64,1152]{1,0:T(8,128)(2,1)}, bf16[64,1152]{1,0:T(8,128)(2,1)}, u32[]{:S(2)}, u32[]{:S(2)}) collective-permute-start(bf16[64,1152]{1,0:T(8,128)(2,1)} %copy-done.17), channel_id=1, source_target_pairs={{448,0},{480,32},{0,64},{32,96},{64,128},{96,160},{128,192},{160,2... | collective-permute-start | bytes 442376 | tf_op jit(solution)/shard_map/ppermute | solution.py:22
  189.5 27.6 %all-to-all-start.2 = ((bf16[4,32,1152]{2,1,0:T(8,128)(2,1)}), bf16[4,32,1152]{2,1,0:T(8,128)(2,1)S(1)}, u32[]{:S(2)}, u32[]{:S(2)}) async-start(bf16[4,32,1152]{2,1,0:T(8,128)(2,1)} %shard_map.121), calls=%async_computation.2 | async-start | bytes 589824 | tf_op jit(solution)/shard_map/all_to_all | solution.py:468
  198.2 3.2 %copy-start.1 = (bf16[32,32,1152]{2,1,0:T(8,128)(2,1)S(1)}, bf16[32,32,1152]{2,1,0:T(8,128)(2,1)}, u32[]{:S(2)}) copy-start(bf16[32,32,1152]{2,1,0:T(8,128)(2,1)} %param.10) | copy-start | bytes 7077892
  198.2 3.2 %copy-start.9 = (f32[1024,16]{1,0:T(8,128)S(1)}, f32[1024,16]{1,0:T(8,128)}, u32[]{:S(2)}) copy-start(f32[1024,16]{1,0:T(8,128)} %copy-done.8) | copy-start | bytes 196612
  198.2 3.2 %copy-start.12 = (bf16[1152,16]{0,1:T(8,128)(2,1)S(1)}, bf16[1152,16]{0,1:T(8,128)(2,1)}, u32[]{:S(2)}) copy-start(bf16[1152,16]{0,1:T(8,128)(2,1)} %param.11) | copy-start | bytes 110596
  201.4 15.7 %copy-start.3 = (bf16[576,1152]{1,0:T(8,128)(2,1)S(1)}, bf16[576,1152]{1,0:T(8,128)(2,1)}, u32[]{:S(2)}) copy-start(bf16[576,1152]{1,0:T(8,128)(2,1)} %all-gather.5.cloned.1.call-done.refs_5_.refs_0_) | copy-start | bytes 3981316
  201.4 15.7 %copy-start.7 = (bf16[576,1152]{1,0:T(8,128)(2,1)S(1)}, bf16[576,1152]{1,0:T(8,128)(2,1)}, u32[]{:S(2)}) copy-start(bf16[576,1152]{1,0:T(8,128)(2,1)} %copy-done.5) | copy-start | bytes 3981316
  201.5 15.7 %copy-start.11 = (f32[32,1152]{1,0:T(8,128)S(1)}, f32[32,1152]{1,0:T(8,128)}, u32[]{:S(2)}) copy-start(f32[32,1152]{1,0:T(8,128)} %copy-done.10) | copy-start | bytes 442372
Sparse Core Ops, SparseCore 0:
  10.1 58.2 all-gather.4
  70.5 46.2 all-gather.2

commit v5 on v4

--- a/solution.py
+++ b/solution.py
@@ -384,10 +384,6 @@
     return lax.all_to_all(spread, axes, 0, 0, tiled=True)
 
 
-def gather_matrix(piece):
-    return lax.all_gather(piece, ("y_lo", "x"), axis=0, tiled=True)
-
-
 def corner(*arrays):
     return sum(array[(0,) * (array.ndim - 1)][:1].astype(F32) for array in arrays)
 
@@ -414,8 +410,9 @@
     spot = lax.axis_index("z_hi").astype(jnp.int32).reshape(1)
     count = caption_embedding.shape[0]
 
-    text_own = gather_matrix(caption_head_matrix.T)
-    exit_own = gather_matrix(pooling_exit_matrix.T)
+    text_matrix = (
+        lax.all_gather(caption_head_matrix.T, ("core", "y_lo", "x"), axis=0, tiled=True),
+    )
 
     captions = caption_embedding
     near = [take_from(captions, Z, d, NZ) if d else captions for d in (-4, 0, 4, 8)]
@@ -445,14 +442,13 @@
         take_from(near[count : 3 * count], Z, 2, NZ),
         take_from(near[: 2 * count], Z, -2, NZ),
     ]
-    text_matrix = text_own, swap_cores(text_own)
-    held_exit, held_images, there = lax.optimization_barrier(
-        (exit_own, own_images, corner(*pieces[1:]))
-    )
-    exit_matrix = exit_own, swap_cores(held_exit)
+    exit_piece, there = lax.optimization_barrier((pooling_exit_matrix.T, corner(own_images)))
+    exit_own = to_all(exit_piece, ("y_lo", "x"), 8).reshape(-1, width)
+    held_images, arrived = lax.optimization_barrier((own_images, corner(*pieces[1:])))
+    exit_matrix = exit_own, swap_cores(exit_own)
     other_images = swap_cores(held_images)
 
-    texts, text_pre = unit_texts(after(place, there), pieces, text_matrix)
+    texts, text_pre = unit_texts(after(place, there + arrived), pieces, text_matrix)
     own_part, text_sum = first_tile(
         place, scalars, texts, text_ids, own_images, exit_matrix
     )

time: 227 us -> 215 us (0.947)
  waiting for transfers between devices: 68.9 us -> 28.6 us
  blocking collectives: 0 us -> 28.8 us
  Pallas kernels: 32.6 us -> 28.4 us
    all_gather x2 -> x1, waiting for transfers between devices: 48 us -> 0.01 us  [shards(): lax.all_gather(caption_head_matrix.T, ('core', 'y_lo', 'x'), axis=0, tile...]
    all_to_all x0 -> x1, blocking collectives: none -> 28.8 us  [to_all(): return lax.all_to_all(spread, axes, 0, 0, tiled=True)]
    ppermute x11, waiting for transfers between devices: 6.81 us -> 14.8 us  [take_from(): lax.ppermute(values, axis, [((i + distance) % size, i) for i in range(siz...]
    ppermute x11, starting transfers between devices: 52.9 us -> 58.8 us  [take_from(): lax.ppermute(values, axis, [((i + distance) % size, i) for i in range(siz...]
    all_to_all x1, starting transfers between devices: 8.5 us -> 5.64 us  [shards(): text_parts = lax.all_to_all(chip_texts, 'z_hi', 0, 0, tiled=True)]
    ppermute x4 -> x3, starting transfers between devices: 8.33 us -> 6.43 us  [swap_cores(): return lax.ppermute(values, 'core', [(0, 1), (1, 0)])]
    slice x6 -> x7, local copies, waits for them, and re-layouts: 3.83 us -> 5.21 us  [corner(): array[(0,) * (array.ndim - 1)][:1].astype(F32)]
    unnamed x48 -> x62, local copies, waits for them, and re-layouts: 11.8 us -> 12.5 us
  transfers between devices with their start and end apart: 20 -> 18, of which waited for: 7 -> 8; matrix products, arithmetic and copies ran while one was open for 3% -> 4% of each run, Pallas kernels for 9% -> 8%
where the time goes in v5:
time: 215 us; the launch traced here: 212 us
  starting transfers between devices  82.9 us (39%)
  blocking collectives  28.8 us (13%)
  waiting for transfers between devices  28.6 us (13%)
  Pallas kernels  28.4 us (13%)
  between operations  22.4 us (10%)
  local copies, waits for them, and re-layouts  19.1 us (9%)
    ppermute x11, starting transfers between devices, take_from(): lax.ppermute(values, axis, [((i + distance) % size, i) for i in range(siz...  58.8 us
    all_to_all x1, blocking collectives, to_all(): return lax.all_to_all(spread, axes, 0, 0, tiled=True)  28.8 us
    ppermute x11, waiting for transfers between devices, take_from(): lax.ppermute(values, axis, [((i + distance) % size, i) for i in range(siz...  14.8 us
    unnamed x62, local copies, waits for them, and re-layouts  12.5 us
    all_to_all x1, waiting for transfers between devices, shards(): text_parts = lax.all_to_all(chip_texts, 'z_hi', 0, 0, tiled=True)  8.33 us
    ppermute x3, starting transfers between devices, swap_cores(): return lax.ppermute(values, 'core', [(0, 1), (1, 0)])  6.43 us
    pallas_call x1, Pallas kernels, second_tile(): call(kernel, (jax.ShapeDtypeStruct((image_count, text_count), BF), jax.Sh...  6.29 us
    pallas_call x1, Pallas kernels, first_tile(): call(kernel, (jax.ShapeDtypeStruct((image_count, width), F32), jax.ShapeD...  6.09 us
  transfers between devices with their start and end apart: 18, of which 8 were waited for; matrix products, arithmetic and copies ran while one was open for 4% of the time, Pallas kernels for 8%

profile of v5, /device:TPU:6, one launch (start us, length us, event | category | flops | bytes accessed | tf_op | source)
XLA Modules:
  0.0 211.7 jit_solution(8299647969639942338)
XLA Ops:
  7.2 0.7 all-gather.2.cloned.1.call-update
  7.9 1.0 copy.12.qk_ref
  8.9 1.7 copy-done
  10.6 2.6 %shard_map.113 = (f32[1024,16]{1,0:T(8,128)S(1)}, f32[32,1152]{1,0:T(8,128)S(1)}) custom-call(bf16[1024,1152]{1,0:T(8,128)(2,1)S(1)} %bitcast.15, bf16[1152,16]{1,0:T(8,128)(2,1)S(1)} %copy.12.qk_ref, bf16[16,1152]{1,0:T(8,128)(2,1)S(1)} %fusion.1.spread_ref), custom_call_target="tpu_custom_call" | custom-call | flops 603979776 | bytes 2359296 | tf_op jit(solution)/shard_map/pallas_call | solution.py:72
  13.2 0.8 copy-done.9
  14.3 28.8 %all_to_all.20 = bf16[16,32,1280]{2,1,0:T(8,128)(2,1)S(1)} all-to-all(bf16[16,32,1280]{2,1,0:T(8,128)(2,1)S(1)} %broadcast_in_dim.61), channel_id=1, replica_groups=mesh['z_hi'=4,'z_lo'=4,'y_hi'=2,'y_lo'=2,'x'=4,'core'=2] {'y_hi','y_lo',..., dimensions={0} | all-to-all | bytes 2621440 | tf_op jit(solution)/shard_map/all_to_all | solution.py:384
  44.3 1.2 broadcast_in_dim.62
  45.5 6.1 %all-to-all-start.1 = ((bf16[8,72,1152]{2,1,0:T(8,128)(2,1)}), bf16[8,72,1152]{2,1,0:T(8,128)(2,1)S(1)}, u32[]{:S(2)}, u32[]{:S(2)}) async-start(bf16[8,72,1152]{2,1,0:T(8,128)(2,1)} %broadcast_in_dim.62), calls=%async_computation.1 | async-start | bytes 2654208 | tf_op jit(solution)/shard_map/all_to_all | solution.py:384
  51.5 9.3 %collective-permute-start = (bf16[32,1152]{1,0:T(8,128)(2,1)S(1)}, bf16[32,1152]{1,0:T(8,128)(2,1)S(1)}, u32[]{:S(2)}, u32[]{:S(2)}) collective-permute-start(bf16[32,1152]{1,0:T(8,128)(2,1)S(1)} %copy-done.24), channel_id=1, source_target_pairs={{384,0},{416,32},{448,64},{480,96},{0,128},{32,160},{64,192},{96,2... | collective-permute-start | bytes 221192 | tf_op jit(solution)/shard_map/ppermute | solution.py:22
  60.8 6.0 %collective-permute-start.1 = (bf16[32,1152]{1,0:T(8,128)(2,1)S(1)}, bf16[32,1152]{1,0:T(8,128)(2,1)S(1)}, u32[]{:S(2)}, u32[]{:S(2)}) collective-permute-start(bf16[32,1152]{1,0:T(8,128)(2,1)S(1)} %copy-done.24), channel_id=1, source_target_pairs={{128,0},{160,32},{192,64},{224,96},{256,128},{288,160},{320,192},{... | collective-permute-start | bytes 221192 | tf_op jit(solution)/shard_map/ppermute | solution.py:22
  66.9 10.8 %collective-permute-start.2 = (bf16[32,1152]{1,0:T(8,128)(2,1)S(1)}, bf16[32,1152]{1,0:T(8,128)(2,1)S(1)}, u32[]{:S(2)}, u32[]{:S(2)}) collective-permute-start(bf16[32,1152]{1,0:T(8,128)(2,1)S(1)} %copy-done.24), channel_id=1, source_target_pairs={{256,0},{288,32},{320,64},{352,96},{384,128},{416,160},{448,192},{... | collective-permute-start | bytes 221192 | tf_op jit(solution)/shard_map/ppermute | solution.py:22
  77.7 4.1 %collective-permute-done.2 = bf16[32,1152]{1,0:T(8,128)(2,1)S(1)} collective-permute-done((bf16[32,1152]{1,0:T(8,128)(2,1)S(1)}, bf16[32,1152]{1,0:T(8,128)(2,1)S(1)}, u32[]{:S(2)}, u32[]{:S(2)}) %collective-permute-start.2) | collective-permute-done | bytes 73760 | tf_op jit(solution)/shard_map/ppermute | solution.py:22
  81.8 10.0 %collective-permute-start.3 = (bf16[128,1152]{1,0:T(8,128)(2,1)S(1)}, bf16[128,1152]{1,0:T(8,128)(2,1)S(1)}, u32[]{:S(2)}, u32[]{:S(2)}) collective-permute-start(bf16[128,1152]{1,0:T(8,128)(2,1)S(1)} %constant_dynamic-update-slice_fusion.refs_0_), channel_id=1, source_target_pairs={{32,0},{64,32},{96,64},{128,96},{160,128},{192,160},{224,192},{256... | collective-permute-start | bytes 884744 | tf_op jit(solution)/shard_map/ppermute | solution.py:22
  91.9 1.9 collective-permute-start.4
  93.8 1.9 collective-permute-start.7
  95.7 0.9 pad_maximum_fusion.1
  96.7 3.4 %collective-permute-start.5 = (bf16[64,1152]{1,0:T(8,128)(2,1)S(1)}, bf16[64,1152]{1,0:T(8,128)(2,1)S(1)}, u32[]{:S(2)}, u32[]{:S(2)}) collective-permute-start(bf16[64,1152]{1,0:T(8,128)(2,1)S(1)} %get-tuple-element.35), channel_id=1, source_target_pairs={{64,0},{96,32},{128,64},{160,96},{192,128},{224,160},{256,192},{28... | collective-permute-start | bytes 442376 | tf_op jit(solution)/shard_map/ppermute | solution.py:22
  100.0 3.4 %collective-permute-start.6 = (bf16[64,1152]{1,0:T(8,128)(2,1)S(1)}, bf16[64,1152]{1,0:T(8,128)(2,1)S(1)}, u32[]{:S(2)}, u32[]{:S(2)}) collective-permute-start(bf16[64,1152]{1,0:T(8,128)(2,1)S(1)} %get-tuple-element.34), channel_id=1, source_target_pairs={{448,0},{480,32},{0,64},{32,96},{64,128},{96,160},{128,192},{160,2... | collective-permute-start | bytes 442376 | tf_op jit(solution)/shard_map/ppermute | solution.py:22
  103.4 4.8 %collective-permute-done.5.refs_3_ = bf16[64,1152]{1,0:T(8,128)(2,1)S(1)} collective-permute-done((bf16[64,1152]{1,0:T(8,128)(2,1)S(1)}, bf16[64,1152]{1,0:T(8,128)(2,1)S(1)}, u32[]{:S(2)}, u32[]{:S(2)}) %collective-permute-start.5) | collective-permute-done | bytes 147488 | tf_op jit(solution)/shard_map/ppermute | solution.py:22
  109.4 3.8 %collective-permute-done.6.refs_4_ = bf16[64,1152]{1,0:T(8,128)(2,1)S(1)} collective-permute-done((bf16[64,1152]{1,0:T(8,128)(2,1)S(1)}, bf16[64,1152]{1,0:T(8,128)(2,1)S(1)}, u32[]{:S(2)}, u32[]{:S(2)}) %collective-permute-start.6) | collective-permute-done | bytes 147488 | tf_op jit(solution)/shard_map/ppermute | solution.py:22
  115.0 1.2 slice.55
  118.9 2.1 collective-permute-start.8
  123.3 1.8 copy-done.3
  125.0 0.9 copy-done.19
  125.9 0.9 copy-done.21
  126.8 3.3 %shard_map.114 = (bf16[512,1152]{1,0:T(8,128)(2,1)S(1)}, f32[32,1152]{1,0:T(8,128)S(1)}) custom-call(s32[1]{0:T(128)S(6)} %add.94.core_ref, bf16[128,1152]{1,0:T(8,128)(2,1)S(1)} %constant_dynamic-update-slice_fusion.refs_0_, bf16[128,1152]{1,0:T(8,128)(2,1)S(1)} %collective-permute-done.3.refs_1_, bf16[128,1152]{1,0:T(8,128)(2,1)} %collective-permute-done.4.refs_2_, ...), custom_call_target="tpu_custom_call" | custom-call | flops 1358954496 | bytes 2654208 | tf_op jit(solution)/shard_map/pallas_call | solution.py:177
  130.1 6.1 %shard_map.115 = (f32[512,1152]{1,0:T(8,128)S(1)}, f32[512,1152]{1,0:T(8,128)S(1)}) custom-call(s32[1]{0:T(128)} %bitcast.1.core_ref, f32[3]{0:T(128)S(1)} %pad_maximum_fusion.3.scalar_ref, bf16[512,1152]{1,0:T(8,128)(2,1)S(1)} %get-tuple-element.22.texts_ref, f32[1,512]{1,0:T(1,128)S(1)} %convert_element_type.87.ids_ref, bf16[512,1280]{1,0:T(8,128)(2,1)S(1)} %bitcast.24, ...), custom_call_target="tpu_custom_call" | custom-call | flops 3170893824 | bytes 3538944 | tf_op jit(solution)/shard_map/pallas_call | solution.py:265
  136.3 6.3 %shard_map.116 = (bf16[512,512]{1,0:T(8,128)(2,1)S(1)}, f32[128,1152]{1,0:T(8,128)S(1)}, bf16[128,1152]{1,0:T(8,128)(2,1)S(1)}, bf16[128,1152]{1,0:T(8,128)(2,1)...) custom-call(s32[1]{0:T(128)} %bitcast.1.core_ref, f32[3]{0:T(128)S(1)} %pad_maximum_fusion.3.scalar_ref, ...), custom_call_target="tpu_custom_call" | custom-call | flops 2566914048 | bytes 3538944 | tf_op jit(solution)/shard_map/pallas_call | solution.py:307
  142.6 0.9 shard_map.117
  143.5 2.4 %collective-permute-start.9 = (bf16[512,1152]{1,0:T(8,128)(2,1)S(1)}, bf16[512,1152]{1,0:T(8,128)(2,1)S(1)}, u32[]{:S(2)}, u32[]{:S(2)}) collective-permute-start(bf16[512,1152]{1,0:T(8,128)(2,1)S(1)} %shard_map.117), channel_id=1, source_target_pairs={{0,1},{1,0},{2,3},{3,2},{4,5},{5,4},{6,7},{7,6},{8,9},{9,8},{10,11... | collective-permute-start | bytes 3538952 | tf_op jit(solution)/shard_map/ppermute | solution.py:26
  145.9 2.5 %collective-permute-done.9.part_ref = bf16[512,1152]{1,0:T(8,128)(2,1)S(1)} collective-permute-done((bf16[512,1152]{1,0:T(8,128)(2,1)S(1)}, bf16[512,1152]{1,0:T(8,128)(2,1)S(1)}, u32[]{:S(2)}, u32[]{:S(2)}) %collective-permute-start.9) | collective-permute-done | bytes 1179680 | tf_op jit(solution)/shard_map/ppermute | solution.py:26
  148.6 1.0 copy-done.2
  149.6 6.0 %all-to-all-start.2 = ((bf16[16,32,1152]{2,1,0:T(8,128)(2,1)}), bf16[16,32,1152]{2,1,0:T(8,128)(2,1)S(1)}, u32[]{:S(2)}, u32[]{:S(2)}) async-start(bf16[16,32,1152]{2,1,0:T(8,128)(2,1)} %bitcast.21), calls=%async_computation.2 | async-start | bytes 2359296 | tf_op jit(solution)/shard_map/all_to_all | solution.py:462
  155.6 3.0 %collective-permute-start.10 = (bf16[128,1152]{1,0:T(8,128)(2,1)}, bf16[128,1152]{1,0:T(8,128)(2,1)S(1)}, u32[]{:S(2)}, u32[]{:S(2)}) collective-permute-start(bf16[128,1152]{1,0:T(8,128)(2,1)} %copy-done.17), channel_id=1, source_target_pairs={{480,0},{0,32},{32,64},{64,96},{96,128},{128,160},{160,192},{192,2... | collective-permute-start | bytes 884744 | tf_op jit(solution)/shard_map/ppermute | solution.py:22
  158.6 4.0 %collective-permute-start.11 = (bf16[128,1152]{1,0:T(8,128)(2,1)}, bf16[128,1152]{1,0:T(8,128)(2,1)}, u32[]{:S(2)}, u32[]{:S(2)}) collective-permute-start(bf16[128,1152]{1,0:T(8,128)(2,1)} %copy-done.16), channel_id=1, source_target_pairs={{32,0},{64,32},{96,64},{128,96},{160,128},{192,160},{224,192},{256... | collective-permute-start | bytes 884744 | tf_op jit(solution)/shard_map/ppermute | solution.py:22
  162.6 1.9 collective-permute-start.12
  164.6 5.0 %collective-permute-start.13 = (bf16[64,1152]{1,0:T(8,128)(2,1)}, bf16[64,1152]{1,0:T(8,128)(2,1)}, u32[]{:S(2)}, u32[]{:S(2)}) collective-permute-start(bf16[64,1152]{1,0:T(8,128)(2,1)} %copy-done.22), channel_id=1, source_target_pairs={{448,0},{480,32},{0,64},{32,96},{64,128},{96,160},{128,192},{160,2... | collective-permute-start | bytes 442376 | tf_op jit(solution)/shard_map/ppermute | solution.py:22
  169.6 2.4 %all-to-all-done.2.parts_ref = bf16[16,32,1152]{2,1,0:T(8,128)(2,1)S(1)} async-done(((bf16[16,32,1152]{2,1,0:T(8,128)(2,1)}), bf16[16,32,1152]{2,1,0:T(8,128)(2,1)S(1)}, u32[]{:S(2)}, u32[]{:S(2)}) %all-to-all-start.2) | async-done | bytes 1179680 | tf_op jit(solution)/shard_map/all_to_all | solution.py:462
  174.0 1.3 collective-permute-done.12.low_ref
  176.0 2.0 shard_map.121
  178.0 5.6 %all-to-all-start.3 = ((bf16[4,32,1152]{2,1,0:T(8,128)(2,1)}), bf16[4,32,1152]{2,1,0:T(8,128)(2,1)S(1)}, u32[]{:S(2)}, u32[]{:S(2)}) async-start(bf16[4,32,1152]{2,1,0:T(8,128)(2,1)} %shard_map.121), calls=%async_computation.3 | async-start | bytes 589824 | tf_op jit(solution)/shard_map/all_to_all | solution.py:464
  183.8 1.3 copy-done.6
  185.2 1.7 shard_map.119.dpooled_ref
  186.9 4.2 %shard_map.120 = bf16[1024,1152]{1,0:T(8,128)(2,1)} custom-call(bf16[1024,1152]{1,0:T(8,128)(2,1)S(1)} %bitcast.16, f32[1024,16]{1,0:T(8,128)S(1)} %copy-done.10, f32[32,1152]{1,0:T(8,128)S(1)} %shard_map.119.dpooled_ref, bf16[16,1152]{1,0:T(8,128)(2,1)S(1)} %bitcast.25, bf16[16,1152]{1,0:T(8,128)(2,1)S(1)} %copy-done.12, bf16[1152,16]{1,0:T(8,128)(2,1)S(1)} %fusion.gather_ref), custom_call_target="tpu_custom_call" | custom-call | flops 1207959552 | bytes 4718592 | tf_op jit(solution)/shard_map/pallas_call | solution.py:118
  191.1 1.2 slice.58
  193.5 8.3 %all-to-all-done.3.parts_ref = bf16[4,32,1152]{2,1,0:T(8,128)(2,1)S(1)} async-done(((bf16[4,32,1152]{2,1,0:T(8,128)(2,1)}), bf16[4,32,1152]{2,1,0:T(8,128)(2,1)S(1)}, u32[]{:S(2)}, u32[]{:S(2)}) %all-to-all-start.3) | async-done | bytes 294944 | tf_op jit(solution)/shard_map/all_to_all | solution.py:464
  201.8 1.7 copy-done.4
  203.6 1.3 shard_map.122
  (85 shorter events, 5.9 us)
Async XLA Ops:
  7.2 116.1 %all-gather.2.cloned.1.call-start = ((), (), s32[]{:S(2)}) async-start(), calls=%async_computation.4 | async-start | bytes 2820096 | tf_op jit(solution)/shard_map/all_gather | solution.py:414
  8.9 4.3 %copy-start.11 = (bf16[16,1152]{1,0:T(8,128)(2,1)}, bf16[16,1152]{1,0:T(8,128)(2,1)S(1)}, u32[]{:S(2)}) copy-start(bf16[16,1152]{1,0:T(8,128)(2,1)S(1)} %fusion.1.spread_ref) | copy-start | bytes 110596
  8.9 1.7 copy-start
  10.6 3.4 %copy-start.28 = (s32[32]{0:T(128)S(1)}, s32[32]{0:T(128)}, u32[]{:S(2)}) copy-start(s32[32]{0:T(128)} %param.15) | copy-start | bytes 388
  13.2 0.8 copy-start.9
  14.3 30.0 %copy-start.26 = (bf16[1152,72]{0,1:T(8,128)(2,1)S(1)}, bf16[1152,72]{0,1:T(8,128)(2,1)}, u32[]{:S(2)}) copy-start(bf16[1152,72]{0,1:T(8,128)(2,1)} %param.12) | copy-start | bytes 497668
  43.1 2.4 %copy-start.7 = (bf16[16,32,1280]{2,1,0:T(8,128)(2,1)}, bf16[16,32,1280]{2,1,0:T(8,128)(2,1)S(1)}, u32[]{:S(2)}) copy-start(bf16[16,32,1280]{2,1,0:T(8,128)(2,1)S(1)} %all_to_all.20) | copy-start | bytes 3932164
  45.5 6.1 %copy-start.24 = (bf16[32,1152]{1,0:T(8,128)(2,1)S(1)}, bf16[32,1152]{1,0:T(8,128)(2,1)}, u32[]{:S(2)}) copy-start(bf16[32,1152]{1,0:T(8,128)(2,1)} %param.13) | copy-start | bytes 221188
  45.5 77.5 %copy-start.27 = (s32[16]{0:T(128)S(1)}, s32[16]{0:T(128)}, u32[]{:S(2)}) copy-start(s32[16]{0:T(128)} %constant.65.clone) | copy-start | bytes 196
  45.5 48.3 %all-to-all-start.1 = ((bf16[8,72,1152]{2,1,0:T(8,128)(2,1)}), bf16[8,72,1152]{2,1,0:T(8,128)(2,1)S(1)}, u32[]{:S(2)}, u32[]{:S(2)}) async-start(bf16[8,72,1152]{2,1,0:T(8,128)(2,1)} %broadcast_in_dim.62), calls=%async_computation.1 | async-start | bytes 2654208 | tf_op jit(solution)/shard_map/all_to_all | solution.py:384
  51.5 26.1 %collective-permute-start = (bf16[32,1152]{1,0:T(8,128)(2,1)S(1)}, bf16[32,1152]{1,0:T(8,128)(2,1)S(1)}, u32[]{:S(2)}, u32[]{:S(2)}) collective-permute-start(bf16[32,1152]{1,0:T(8,128)(2,1)S(1)} %copy-done.24), channel_id=1, source_target_pairs={{384,0},{416,32},{448,64},{480,96},{0,128},{32,160},{64,192},{96,2... | collective-permute-start | bytes 221192 | tf_op jit(solution)/shard_map/ppermute | solution.py:22
  60.8 16.9 %collective-permute-start.1 = (bf16[32,1152]{1,0:T(8,128)(2,1)S(1)}, bf16[32,1152]{1,0:T(8,128)(2,1)S(1)}, u32[]{:S(2)}, u32[]{:S(2)}) collective-permute-start(bf16[32,1152]{1,0:T(8,128)(2,1)S(1)} %copy-done.24), channel_id=1, source_target_pairs={{128,0},{160,32},{192,64},{224,96},{256,128},{288,160},{320,192},{... | collective-permute-start | bytes 221192 | tf_op jit(solution)/shard_map/ppermute | solution.py:22
  66.9 15.0 %collective-permute-start.2 = (bf16[32,1152]{1,0:T(8,128)(2,1)S(1)}, bf16[32,1152]{1,0:T(8,128)(2,1)S(1)}, u32[]{:S(2)}, u32[]{:S(2)}) collective-permute-start(bf16[32,1152]{1,0:T(8,128)(2,1)S(1)} %copy-done.24), channel_id=1, source_target_pairs={{256,0},{288,32},{320,64},{352,96},{384,128},{416,160},{448,192},{... | collective-permute-start | bytes 221192 | tf_op jit(solution)/shard_map/ppermute | solution.py:22
  77.7 14.2 %copy-start.25 = (bf16[32,1152]{1,0:T(8,128)(2,1)}, bf16[32,1152]{1,0:T(8,128)(2,1)S(1)}, u32[]{:S(2)}) copy-start(bf16[32,1152]{1,0:T(8,128)(2,1)S(1)} %collective-permute-done.1) | copy-start | bytes 221188
  81.8 32.7 %collective-permute-start.3 = (bf16[128,1152]{1,0:T(8,128)(2,1)S(1)}, bf16[128,1152]{1,0:T(8,128)(2,1)S(1)}, u32[]{:S(2)}, u32[]{:S(2)}) collective-permute-start(bf16[128,1152]{1,0:T(8,128)(2,1)S(1)} %constant_dynamic-update-slice_fusion.refs_0_), channel_id=1, source_target_pairs={{32,0},{64,32},{96,64},{128,96},{160,128},{192,160},{224,192},{256... | collective-permute-start | bytes 884744 | tf_op jit(solution)/shard_map/ppermute | solution.py:22
  91.9 23.2 %collective-permute-start.4 = (bf16[128,1152]{1,0:T(8,128)(2,1)S(1)}, bf16[128,1152]{1,0:T(8,128)(2,1)}, u32[]{:S(2)}, u32[]{:S(2)}) collective-permute-start(bf16[128,1152]{1,0:T(8,128)(2,1)S(1)} %constant_dynamic-update-slice_fusion.refs_0_), channel_id=1, source_target_pairs={{480,0},{0,32},{32,64},{64,96},{96,128},{128,160},{160,192},{192,2... | collective-permute-start | bytes 884744 | tf_op jit(solution)/shard_map/ppermute | solution.py:22
  93.8 36.3 %collective-permute-start.7 = (bf16[576,1152]{1,0:T(8,128)(2,1)S(1)}, bf16[576,1152]{1,0:T(8,128)(2,1)S(1)}, u32[]{:S(2)}, u32[]{:S(2)}) collective-permute-start(bf16[576,1152]{1,0:T(8,128)(2,1)S(1)} %bitcast.17), channel_id=1, source_target_pairs={{0,1},{1,0},{2,3},{3,2},{4,5},{5,4},{6,7},{7,6},{8,9},{9,8},{10,11... | collective-permute-start | bytes 3981320 | tf_op jit(solution)/shard_map/ppermute | solution.py:26
  96.7 11.6 %collective-permute-start.5 = (bf16[64,1152]{1,0:T(8,128)(2,1)S(1)}, bf16[64,1152]{1,0:T(8,128)(2,1)S(1)}, u32[]{:S(2)}, u32[]{:S(2)}) collective-permute-start(bf16[64,1152]{1,0:T(8,128)(2,1)S(1)} %get-tuple-element.35), channel_id=1, source_target_pairs={{64,0},{96,32},{128,64},{160,96},{192,128},{224,160},{256,192},{28... | collective-permute-start | bytes 442376 | tf_op jit(solution)/shard_map/ppermute | solution.py:22
  100.0 13.2 %collective-permute-start.6 = (bf16[64,1152]{1,0:T(8,128)(2,1)S(1)}, bf16[64,1152]{1,0:T(8,128)(2,1)S(1)}, u32[]{:S(2)}, u32[]{:S(2)}) collective-permute-start(bf16[64,1152]{1,0:T(8,128)(2,1)S(1)} %get-tuple-element.34), channel_id=1, source_target_pairs={{448,0},{480,32},{0,64},{32,96},{64,128},{96,160},{128,192},{160,2... | collective-permute-start | bytes 442376 | tf_op jit(solution)/shard_map/ppermute | solution.py:22
  108.8 0.7 copy-start.18
  113.9 0.6 copy-start.20
  118.9 17.4 %collective-permute-start.8 = (bf16[512,1280]{1,0:T(8,128)(2,1)}, bf16[512,1280]{1,0:T(8,128)(2,1)}, u32[]{:S(2)}, u32[]{:S(2)}) collective-permute-start(bf16[512,1280]{1,0:T(8,128)(2,1)} %bitcast.23), channel_id=1, source_target_pairs={{0,1},{1,0},{2,3},{3,2},{4,5},{5,4},{6,7},{7,6},{8,9},{9,8},{10,11... | collective-permute-start | bytes 3932168 | tf_op jit(solution)/shard_map/ppermute | solution.py:26
  123.2 1.8 copy-start.3
  125.0 0.9 copy-start.19
  125.9 0.9 copy-start.21
  126.8 3.3 %copy-start.8 = (bf16[16,32,1280]{2,1,0:T(8,128)(2,1)S(1)}, bf16[16,32,1280]{2,1,0:T(8,128)(2,1)}, u32[]{:S(2)}) copy-start(bf16[16,32,1280]{2,1,0:T(8,128)(2,1)} %copy-done.7) | copy-start | bytes 3932164
  130.1 6.1 %copy-start.13 = (f32[32,1152]{1,0:T(8,128)}, f32[32,1152]{1,0:T(8,128)S(1)}, u32[]{:S(2)}) copy-start(f32[32,1152]{1,0:T(8,128)S(1)} %get-tuple-element.28.rows_ref) | copy-start | bytes 442372
  130.1 6.1 %copy-start.5 = (bf16[576,1152]{1,0:T(8,128)(2,1)}, bf16[576,1152]{1,0:T(8,128)(2,1)S(1)}, u32[]{:S(2)}) copy-start(bf16[576,1152]{1,0:T(8,128)(2,1)S(1)} %collective-permute-done.7.theirs_ref.refs_1_) | copy-start | bytes 3981316
  142.6 0.9 copy-start.22
  142.6 0.9 copy-start.23
  142.6 6.0 %copy-start.16 = (bf16[128,1152]{1,0:T(8,128)(2,1)}, bf16[128,1152]{1,0:T(8,128)(2,1)S(1)}, u32[]{:S(2)}) copy-start(bf16[128,1152]{1,0:T(8,128)(2,1)S(1)} %get-tuple-element.31) | copy-start | bytes 884740
  142.6 6.0 %copy-start.17 = (bf16[128,1152]{1,0:T(8,128)(2,1)}, bf16[128,1152]{1,0:T(8,128)(2,1)S(1)}, u32[]{:S(2)}) copy-start(bf16[128,1152]{1,0:T(8,128)(2,1)S(1)} %get-tuple-element.30) | copy-start | bytes 884740
  143.5 4.9 %collective-permute-start.9 = (bf16[512,1152]{1,0:T(8,128)(2,1)S(1)}, bf16[512,1152]{1,0:T(8,128)(2,1)S(1)}, u32[]{:S(2)}, u32[]{:S(2)}) collective-permute-start(bf16[512,1152]{1,0:T(8,128)(2,1)S(1)} %shard_map.117), channel_id=1, source_target_pairs={{0,1},{1,0},{2,3},{3,2},{4,5},{5,4},{6,7},{7,6},{8,9},{9,8},{10,11... | collective-permute-start | bytes 3538952 | tf_op jit(solution)/shard_map/ppermute | solution.py:26
  148.6 1.0 copy-start.2
  149.6 22.4 %all-to-all-start.2 = ((bf16[16,32,1152]{2,1,0:T(8,128)(2,1)}), bf16[16,32,1152]{2,1,0:T(8,128)(2,1)S(1)}, u32[]{:S(2)}, u32[]{:S(2)}) async-start(bf16[16,32,1152]{2,1,0:T(8,128)(2,1)} %bitcast.21), calls=%async_computation.2 | async-start | bytes 2359296 | tf_op jit(solution)/shard_map/all_to_all | solution.py:462
  155.6 20.4 %collective-permute-start.10 = (bf16[128,1152]{1,0:T(8,128)(2,1)}, bf16[128,1152]{1,0:T(8,128)(2,1)S(1)}, u32[]{:S(2)}, u32[]{:S(2)}) collective-permute-start(bf16[128,1152]{1,0:T(8,128)(2,1)} %copy-done.17), channel_id=1, source_target_pairs={{480,0},{0,32},{32,64},{64,96},{96,128},{128,160},{160,192},{192,2... | collective-permute-start | bytes 884744 | tf_op jit(solution)/shard_map/ppermute | solution.py:22
  158.6 17.4 %collective-permute-start.11 = (bf16[128,1152]{1,0:T(8,128)(2,1)}, bf16[128,1152]{1,0:T(8,128)(2,1)}, u32[]{:S(2)}, u32[]{:S(2)}) collective-permute-start(bf16[128,1152]{1,0:T(8,128)(2,1)} %copy-done.16), channel_id=1, source_target_pairs={{32,0},{64,32},{96,64},{128,96},{160,128},{192,160},{224,192},{256... | collective-permute-start | bytes 884744 | tf_op jit(solution)/shard_map/ppermute | solution.py:22
  162.6 12.7 %collective-permute-start.12 = (bf16[64,1152]{1,0:T(8,128)(2,1)}, bf16[64,1152]{1,0:T(8,128)(2,1)}, u32[]{:S(2)}, u32[]{:S(2)}) collective-permute-start(bf16[64,1152]{1,0:T(8,128)(2,1)} %copy-done.23), channel_id=1, source_target_pairs={{64,0},{96,32},{128,64},{160,96},{192,128},{224,160},{256,192},{28... | collective-permute-start | bytes 442376 | tf_op jit(solution)/shard_map/ppermute | solution.py:22
  164.6 11.4 %collective-permute-start.13 = (bf16[64,1152]{1,0:T(8,128)(2,1)}, bf16[64,1152]{1,0:T(8,128)(2,1)}, u32[]{:S(2)}, u32[]{:S(2)}) collective-permute-start(bf16[64,1152]{1,0:T(8,128)(2,1)} %copy-done.22), channel_id=1, source_target_pairs={{448,0},{480,32},{0,64},{32,96},{64,128},{96,160},{128,192},{160,2... | collective-permute-start | bytes 442376 | tf_op jit(solution)/shard_map/ppermute | solution.py:22
  178.0 23.8 %all-to-all-start.3 = ((bf16[4,32,1152]{2,1,0:T(8,128)(2,1)}), bf16[4,32,1152]{2,1,0:T(8,128)(2,1)S(1)}, u32[]{:S(2)}, u32[]{:S(2)}) async-start(bf16[4,32,1152]{2,1,0:T(8,128)(2,1)} %shard_map.121), calls=%async_computation.3 | async-start | bytes 589824 | tf_op jit(solution)/shard_map/all_to_all | solution.py:464
  183.8 1.3 copy-start.6
  185.2 1.7 copy-start.1
  185.2 1.7 copy-start.10
  185.2 1.7 copy-start.12
  185.2 1.8 copy-start.15
  186.9 14.9 %copy-start.14 = (f32[32,1152]{1,0:T(8,128)S(1)}, f32[32,1152]{1,0:T(8,128)}, u32[]{:S(2)}) copy-start(f32[32,1152]{1,0:T(8,128)} %copy-done.13) | copy-start | bytes 442372
  201.8 1.8 copy-start.4
Sparse Core Ops, SparseCore 0:
  10.2 55.4 all-gather.1

commit v6 on v2

--- a/solution.py
+++ b/solution.py
@@ -224,11 +224,16 @@
 
     def kernel(scalar_ref, *refs):
         piece_refs = refs[: len(pieces)]
-        ids_ref, images_ref, texts_ref, image_part_ref, total_ref = refs[len(pieces) :]
-        start = 0
-        for ref in piece_refs:
-            texts_ref[start : start + ref.shape[0], :] = ref[...]
+        ids_ref, images_ref, texts_ref, image_part_ref, total_ref, sems = refs[len(pieces) :]
+        copies, start = [], 0
+        for i, ref in enumerate(piece_refs):
+            rows = pl.ds(start, ref.shape[0])
+            copies.append(pltpu.make_async_copy(ref, texts_ref.at[rows], sems.at[i]))
             start += ref.shape[0]
+        for copy in copies:
+            copy.start()
+        for copy in copies:
+            copy.wait()
         ids = ids_ref[...]
         for i in range(image_count // block):
             rows = slice(i * block, (i + 1) * block)
@@ -249,8 +254,10 @@
             jax.ShapeDtypeStruct((text_count, width), F32),
         ),
         in_specs=[pl.BlockSpec(memory_space=SMEM)]
-        + [pl.BlockSpec(memory_space=VMEM)] * (2 + len(pieces)),
+        + [pl.BlockSpec(memory_space=pl.ANY)] * len(pieces)
+        + [pl.BlockSpec(memory_space=VMEM)] * 2,
         out_specs=[pl.BlockSpec(memory_space=VMEM)] * 3,
+        scratch_shapes=[pltpu.SemaphoreType.DMA((len(pieces),))],
         flops=6 * text_count * image_count * width,
         transcendentals=text_count * image_count,
         moved=2 * width * (text_count + 2 * image_count),
@@ -415,10 +422,12 @@
         take_from(near[:cut], Z, 2, NZ),
         take_from(near[cut:], Z, -2, NZ),
     ]
-    own_images, pieces = lax.optimization_barrier((own_images, pieces))
-    other_images = swap_cores(own_images)
-
-    texts, own_part, text_sum = first_tile(scalars, pieces, text_ids, own_images)
+    there = sum(piece[0, :1].astype(F32) for piece in pieces[1:])
+    held_images, there = lax.optimization_barrier((own_images, there))
+    other_images = swap_cores(held_images)
+    first_scalars = scalars + (there != there).astype(F32)
+
+    texts, own_part, text_sum = first_tile(first_scalars, pieces, text_ids, own_images)
     weighted, mine, *away = second_tile(
         scalars, texts, text_ids, other_images, text_sum, [piece.shape[0] for piece in pieces]
     )

time: 191 us -> 195 us (1.021)
  between operations: 16.4 us -> 19 us
  local copies, waits for them, and re-layouts: 18.6 us -> 20.8 us
    slice x0 -> x4, local copies, waits for them, and re-layouts: none -> 2.2 us  [shards(): there = sum((piece[0, :1].astype(F32) for piece in pieces[1:]))]
  transfers between devices with their start and end apart: 17 -> 17, of which waited for: 10 -> 10; matrix products, arithmetic and copies ran while one was open for 2% -> 3% of each run, Pallas kernels for 8% -> 9%
where the time goes in v6:
time: 195 us; the launch traced here: 192 us
  starting transfers between devices  80.3 us (41%)
  waiting for transfers between devices  50.2 us (26%)
  Pallas kernels  21.8 us (11%)
  local copies, waits for them, and re-layouts  20.8 us (11%)
  between operations  19 us (10%)
    all_to_all x3, starting transfers between devices, to_all(): return lax.all_to_all(spread, axes, 0, 0, tiled=True)  33.1 us
    ppermute x8, starting transfers between devices, take_from(): lax.ppermute(values, axis, [((i + distance) % size, i) for i in range(siz...  30 us
    all_to_all x3, waiting for transfers between devices, to_all(): return lax.all_to_all(spread, axes, 0, 0, tiled=True)  20.4 us
    unnamed x57, local copies, waits for them, and re-layouts  14.3 us
    ppermute x8, waiting for transfers between devices, take_from(): lax.ppermute(values, axis, [((i + distance) % size, i) for i in range(siz...  13.8 us
    all_to_all x1, waiting for transfers between devices, shards(): lax.all_to_all(chip_texts.reshape(NZH, count, width), 'z_hi', 0, 0, tiled...  9.66 us
    all_to_all x1, starting transfers between devices, shards(): lax.all_to_all(chip_images.reshape(16, images, width), XY, 0, 0, tiled=True)  7.24 us
    ppermute x3, starting transfers between devices, swap_cores(): return lax.ppermute(values, 'core', [(0, 1), (1, 0)])  6.23 us
  transfers between devices with their start and end apart: 17, of which 10 were waited for; matrix products, arithmetic and copies ran while one was open for 3% of the time, Pallas kernels for 9%

profile of v6, /device:TPU:6, one launch (start us, length us, event | category | flops | bytes accessed | tf_op | source)
XLA Modules:
  0.0 192.4 jit_solution(6926681084738714302)
XLA Ops:
  7.9 2.1 %broadcast_in_dim.6 = bf16[8,72,1152]{2,1,0:T(8,128)(2,1)} broadcast(bf16[72,1152]{1,0:T(8,128)(2,1)} %bitcast.26), dimensions={1,2} | broadcast | bytes 1492992 | tf_op jit(solution)/shard_map/broadcast_in_dim | solution.py:362
  10.0 9.5 %all-to-all-start = ((bf16[8,72,1152]{2,1,0:T(8,128)(2,1)}), bf16[8,72,1152]{2,1,0:T(8,128)(2,1)S(1)}, u32[]{:S(2)}, u32[]{:S(2)}) async-start(bf16[8,72,1152]{2,1,0:T(8,128)(2,1)} %broadcast_in_dim.6), calls=%async_computation | async-start | bytes 2654208 | tf_op jit(solution)/shard_map/all_to_all | solution.py:363
  22.1 1.7 copy-done.2
  23.7 2.6 %shard_map.113 = (f32[1024,16]{1,0:T(8,128)S(1)}, f32[32,1152]{1,0:T(8,128)S(1)}) custom-call(bf16[1024,1152]{1,0:T(8,128)(2,1)S(1)} %bitcast.17, bf16[1152,16]{1,0:T(8,128)(2,1)S(1)} %copy.12.qk_ref, bf16[16,1152]{1,0:T(8,128)(2,1)S(1)} %fusion.1.spread_ref), custom_call_target="tpu_custom_call" | custom-call | flops 603979776 | bytes 2359296 | tf_op jit(solution)/shard_map/pallas_call | solution.py:71
  26.4 0.8 copy-done.5
  27.5 4.9 %all-to-all-done = bf16[8,72,1152]{2,1,0:T(8,128)(2,1)S(1)} async-done(((bf16[8,72,1152]{2,1,0:T(8,128)(2,1)}), bf16[8,72,1152]{2,1,0:T(8,128)(2,1)S(1)}, u32[]{:S(2)}, u32[]{:S(2)}) %all-to-all-start) | async-done | bytes 1327136 | tf_op jit(solution)/shard_map/all_to_all | solution.py:363
  32.3 1.9 collective-permute-start
  34.2 3.0 %collective-permute-done.refs_1_ = bf16[576,1152]{1,0:T(8,128)(2,1)S(1)} collective-permute-done((bf16[576,1152]{1,0:T(8,128)(2,1)S(1)}, bf16[576,1152]{1,0:T(8,128)(2,1)S(1)}, u32[]{:S(2)}, u32[]{:S(2)}) %collective-permute-start) | collective-permute-done | bytes 1327136 | tf_op jit(solution)/shard_map/ppermute | solution.py:25
  37.3 1.0 shard_map.114
  38.9 0.7 broadcast_in_dim.7
  39.7 16.5 %all-to-all-start.1 = ((bf16[4,32,1152]{2,1,0:T(8,128)(2,1)}), bf16[4,32,1152]{2,1,0:T(8,128)(2,1)S(1)}, u32[]{:S(2)}, u32[]{:S(2)}) async-start(bf16[4,32,1152]{2,1,0:T(8,128)(2,1)} %broadcast_in_dim.7), calls=%async_computation.1 | async-start | bytes 589824 | tf_op jit(solution)/shard_map/all_to_all | solution.py:363
  56.4 1.7 copy-done
  58.1 1.0 shard_map.115
  59.7 15.5 %all-to-all-done.1 = bf16[4,32,1152]{2,1,0:T(8,128)(2,1)S(1)} async-done(((bf16[4,32,1152]{2,1,0:T(8,128)(2,1)}), bf16[4,32,1152]{2,1,0:T(8,128)(2,1)S(1)}, u32[]{:S(2)}, u32[]{:S(2)}) %all-to-all-start.1) | async-done | bytes 294944 | tf_op jit(solution)/shard_map/all_to_all | solution.py:363
  75.3 1.2 broadcast_in_dim.8
  76.5 7.2 %all-to-all-start.2 = ((bf16[16,32,1280]{2,1,0:T(8,128)(2,1)}), bf16[16,32,1280]{2,1,0:T(8,128)(2,1)}, u32[]{:S(2)}, u32[]{:S(2)}) async-start(bf16[16,32,1280]{2,1,0:T(8,128)(2,1)} %broadcast_in_dim.8), calls=%async_computation.2 | async-start | bytes 2621440 | tf_op jit(solution)/shard_map/all_to_all | solution.py:363
  83.6 6.4 %collective-permute-start.1 = (bf16[128,1152]{1,0:T(8,128)(2,1)S(1)}, bf16[128,1152]{1,0:T(8,128)(2,1)S(1)}, u32[]{:S(2)}, u32[]{:S(2)}) collective-permute-start(bf16[128,1152]{1,0:T(8,128)(2,1)S(1)} %bitcast.20), channel_id=1, source_target_pairs={{32,0},{64,32},{96,64},{128,96},{160,128},{192,160},{224,192},{256... | collective-permute-start | bytes 884744 | tf_op jit(solution)/shard_map/ppermute | solution.py:21
  90.0 1.9 collective-permute-start.2
  92.0 4.2 %collective-permute-start.3 = (bf16[64,1152]{1,0:T(8,128)(2,1)S(1)}, bf16[64,1152]{1,0:T(8,128)(2,1)S(1)}, u32[]{:S(2)}, u32[]{:S(2)}) collective-permute-start(bf16[64,1152]{1,0:T(8,128)(2,1)S(1)} %get-tuple-element.63), channel_id=1, source_target_pairs={{64,0},{96,32},{128,64},{160,96},{192,128},{224,160},{256,192},{28... | collective-permute-start | bytes 442376 | tf_op jit(solution)/shard_map/ppermute | solution.py:21
  96.2 2.5 %collective-permute-start.4 = (bf16[64,1152]{1,0:T(8,128)(2,1)S(1)}, bf16[64,1152]{1,0:T(8,128)(2,1)S(1)}, u32[]{:S(2)}, u32[]{:S(2)}) collective-permute-start(bf16[64,1152]{1,0:T(8,128)(2,1)S(1)} %get-tuple-element.62), channel_id=1, source_target_pairs={{448,0},{480,32},{0,64},{32,96},{64,128},{96,160},{128,192},{160,2... | collective-permute-start | bytes 442376 | tf_op jit(solution)/shard_map/ppermute | solution.py:21
  98.7 4.0 %collective-permute-done.3.refs_3_ = bf16[64,1152]{1,0:T(8,128)(2,1)S(1)} collective-permute-done((bf16[64,1152]{1,0:T(8,128)(2,1)S(1)}, bf16[64,1152]{1,0:T(8,128)(2,1)S(1)}, u32[]{:S(2)}, u32[]{:S(2)}) %collective-permute-start.3) | collective-permute-done | bytes 147488 | tf_op jit(solution)/shard_map/ppermute | solution.py:21
  103.9 3.5 %collective-permute-done.4.refs_4_ = bf16[64,1152]{1,0:T(8,128)(2,1)S(1)} collective-permute-done((bf16[64,1152]{1,0:T(8,128)(2,1)S(1)}, bf16[64,1152]{1,0:T(8,128)(2,1)S(1)}, u32[]{:S(2)}, u32[]{:S(2)}) %collective-permute-start.4) | collective-permute-done | bytes 147488 | tf_op jit(solution)/shard_map/ppermute | solution.py:21
  109.8 0.7 copy-done.16
  113.1 1.9 collective-permute-start.5
  115.0 1.0 copy-done.17
  116.0 0.9 copy-done.21
  116.9 0.9 copy-done.23
  117.8 4.8 %shard_map.116 = (bf16[512,1152]{1,0:T(8,128)(2,1)S(1)}, f32[512,1152]{1,0:T(8,128)S(1)}, f32[512,1152]{1,0:T(8,128)S(1)}) custom-call(f32[3]{0:T(128)S(1)} %broadcast_add_fusion.scalar_ref, bf16[128,1152]{1,0:T(8,128)(2,1)S(1)} %bitcast.23, bf16[128,1152]{1,0:T(8,128)(2,1)S(1)} %collective-permute-done.1.refs_1_, bf16[128,1152]{1,0:T(8,128)(2,1)S(1)} %copy-done.17, ...), custom_call_target="tpu_custom_call" | custom-call | flops 1811939328 | bytes 3538944 | tf_op jit(solution)/shard_map/pallas_call | solution.py:249
  122.6 2.7 %shard_map.117 = (bf16[512,512]{1,0:T(8,128)(2,1)S(1)}, f32[128,1152]{1,0:T(8,128)S(1)}, bf16[128,1152]{1,0:T(8,128)(2,1)S(1)}, bf16[128,1152]{1,0:T(8,128)(2,1)...) custom-call(f32[3]{0:T(128)S(1)} %pad_maximum_fusion.scalar_ref, ...), custom_call_target="tpu_custom_call" | custom-call | flops 1207959552 | bytes 3538944 | tf_op jit(solution)/shard_map/pallas_call | solution.py:290
  125.4 0.8 shard_map.118
  126.3 2.4 %collective-permute-start.6 = (bf16[512,1152]{1,0:T(8,128)(2,1)S(1)}, bf16[512,1152]{1,0:T(8,128)(2,1)S(1)}, u32[]{:S(2)}, u32[]{:S(2)}) collective-permute-start(bf16[512,1152]{1,0:T(8,128)(2,1)S(1)} %shard_map.118), channel_id=1, source_target_pairs={{0,1},{1,0},{2,3},{3,2},{4,5},{5,4},{6,7},{7,6},{8,9},{9,8},{10,11... | collective-permute-start | bytes 3538952 | tf_op jit(solution)/shard_map/ppermute | solution.py:25
  128.7 2.5 %collective-permute-done.6.refs_0_ = bf16[512,1152]{1,0:T(8,128)(2,1)S(1)} collective-permute-done((bf16[512,1152]{1,0:T(8,128)(2,1)S(1)}, bf16[512,1152]{1,0:T(8,128)(2,1)S(1)}, u32[]{:S(2)}, u32[]{:S(2)}) %collective-permute-start.6) | collective-permute-done | bytes 1179680 | tf_op jit(solution)/shard_map/ppermute | solution.py:25
  131.3 1.0 copy-done.4
  132.3 7.2 %all-to-all-start.3 = ((bf16[16,32,1152]{2,1,0:T(8,128)(2,1)}), bf16[16,32,1152]{2,1,0:T(8,128)(2,1)}, u32[]{:S(2)}, u32[]{:S(2)}) async-start(bf16[16,32,1152]{2,1,0:T(8,128)(2,1)} %bitcast.19), calls=%async_computation.3 | async-start | bytes 2359296 | tf_op jit(solution)/shard_map/all_to_all | solution.py:437
  139.6 3.7 %collective-permute-start.7 = (bf16[128,1152]{1,0:T(8,128)(2,1)}, bf16[128,1152]{1,0:T(8,128)(2,1)S(1)}, u32[]{:S(2)}, u32[]{:S(2)}) collective-permute-start(bf16[128,1152]{1,0:T(8,128)(2,1)} %copy-done.19), channel_id=1, source_target_pairs={{480,0},{0,32},{32,64},{64,96},{96,128},{128,160},{160,192},{192,2... | collective-permute-start | bytes 884744 | tf_op jit(solution)/shard_map/ppermute | solution.py:21
  143.3 3.3 %collective-permute-start.8 = (bf16[128,1152]{1,0:T(8,128)(2,1)}, bf16[128,1152]{1,0:T(8,128)(2,1)S(1)}, u32[]{:S(2)}, u32[]{:S(2)}) collective-permute-start(bf16[128,1152]{1,0:T(8,128)(2,1)} %copy-done.18), channel_id=1, source_target_pairs={{32,0},{64,32},{96,64},{128,96},{160,128},{192,160},{224,192},{256... | collective-permute-start | bytes 884744 | tf_op jit(solution)/shard_map/ppermute | solution.py:21
  146.6 2.0 %collective-permute-start.9 = (bf16[64,1152]{1,0:T(8,128)(2,1)}, bf16[64,1152]{1,0:T(8,128)(2,1)S(1)}, u32[]{:S(2)}, u32[]{:S(2)}) collective-permute-start(bf16[64,1152]{1,0:T(8,128)(2,1)} %copy-done.25), channel_id=1, source_target_pairs={{448,0},{480,32},{0,64},{32,96},{64,128},{96,160},{128,192},{160,2... | collective-permute-start | bytes 442376 | tf_op jit(solution)/shard_map/ppermute | solution.py:21
  148.6 6.0 %collective-permute-start.10 = (bf16[64,1152]{1,0:T(8,128)(2,1)}, bf16[64,1152]{1,0:T(8,128)(2,1)S(1)}, u32[]{:S(2)}, u32[]{:S(2)}) collective-permute-start(bf16[64,1152]{1,0:T(8,128)(2,1)} %copy-done.24), channel_id=1, source_target_pairs={{64,0},{96,32},{128,64},{160,96},{192,128},{224,160},{256,192},{28... | collective-permute-start | bytes 442376 | tf_op jit(solution)/shard_map/ppermute | solution.py:21
  154.6 3.9 %collective-permute-done.9.refs_2_ = bf16[64,1152]{1,0:T(8,128)(2,1)S(1)} collective-permute-done((bf16[64,1152]{1,0:T(8,128)(2,1)}, bf16[64,1152]{1,0:T(8,128)(2,1)S(1)}, u32[]{:S(2)}, u32[]{:S(2)}) %collective-permute-start.9) | collective-permute-done | bytes 147488 | tf_op jit(solution)/shard_map/ppermute | solution.py:21
  158.5 2.4 %collective-permute-done.10.refs_3_ = bf16[64,1152]{1,0:T(8,128)(2,1)S(1)} collective-permute-done((bf16[64,1152]{1,0:T(8,128)(2,1)}, bf16[64,1152]{1,0:T(8,128)(2,1)S(1)}, u32[]{:S(2)}, u32[]{:S(2)}) %collective-permute-start.10) | collective-permute-done | bytes 147488 | tf_op jit(solution)/shard_map/ppermute | solution.py:21
  160.9 0.9 shard_map.120
  161.8 3.7 %all-to-all-start.4 = ((bf16[4,32,1152]{2,1,0:T(8,128)(2,1)}), bf16[4,32,1152]{2,1,0:T(8,128)(2,1)S(1)}, u32[]{:S(2)}, u32[]{:S(2)}) async-start(bf16[4,32,1152]{2,1,0:T(8,128)(2,1)} %bitcast.13), calls=%async_computation.4 | async-start | bytes 589824 | tf_op jit(solution)/shard_map/all_to_all | solution.py:440
  165.4 1.7 copy-done.1
  167.2 0.9 copy-done.10
  168.1 2.2 %shard_map.121.dpooled_ref = f32[32,1152]{1,0:T(8,128)S(1)} custom-call(s32[1]{0:T(128)} %bitcast.core_ref, f32[32,1152]{1,0:T(8,128)S(1)} %copy-done.10, bf16[16,32,1152]{2,1,0:T(8,128)(2,1)} %all-to-all-done.3.parts_ref, bf16[1152,1152]{1,0:T(8,128)(2,1)S(1)} %copy-done.1), custom_call_target="tpu_custom_call" | custom-call | flops 84934656 | bytes 2654208 | tf_op jit(solution)/shard_map/pallas_call | solution.py:199
  170.3 4.2 %shard_map.122 = bf16[1024,1152]{1,0:T(8,128)(2,1)} custom-call(bf16[1024,1152]{1,0:T(8,128)(2,1)S(1)} %bitcast.18, f32[1024,16]{1,0:T(8,128)S(1)} %copy-done.6, f32[32,1152]{1,0:T(8,128)S(1)} %shard_map.121.dpooled_ref, bf16[16,1152]{1,0:T(8,128)(2,1)S(1)} %bitcast.24, bf16[16,1152]{1,0:T(8,128)(2,1)S(1)} %copy-done.8, bf16[1152,16]{1,0:T(8,128)(2,1)S(1)} %fusion.gather_ref), custom_call_target="tpu_custom_call" | custom-call | flops 1207959552 | bytes 4718592 | tf_op jit(solution)/shard_map/pallas_call | solution.py:117
  174.5 9.7 %all-to-all-done.4.parts_ref = bf16[4,32,1152]{2,1,0:T(8,128)(2,1)S(1)} async-done(((bf16[4,32,1152]{2,1,0:T(8,128)(2,1)}), bf16[4,32,1152]{2,1,0:T(8,128)(2,1)S(1)}, u32[]{:S(2)}, u32[]{:S(2)}) %all-to-all-start.4) | async-done | bytes 294944 | tf_op jit(solution)/shard_map/all_to_all | solution.py:440
  184.2 1.4 shard_map.123
  (74 shorter events, 6.9 us)
Async XLA Ops:
  7.2 49.2 %all-gather.2.cloned.1.call-start = ((), (), s32[]{:S(2)}) async-start(), calls=%async_computation.5 | async-start | bytes 2820096 | tf_op jit(solution)/shard_map/all_gather | solution.py:387
  10.0 9.5 %copy-start.13 = (bf16[1152,16]{0,1:T(8,128)(2,1)S(1)}, bf16[1152,16]{0,1:T(8,128)(2,1)}, u32[]{:S(2)}) copy-start(bf16[1152,16]{0,1:T(8,128)(2,1)} %param.11) | copy-start | bytes 110596
  10.0 9.7 %copy-start.27 = (s32[4]{0:T(128)S(1)}, s32[4]{0:T(128)}, u32[]{:S(2)}) copy-start(s32[4]{0:T(128)} %constant.53.clone) | copy-start | bytes 52
  10.0 22.3 %all-to-all-start = ((bf16[8,72,1152]{2,1,0:T(8,128)(2,1)}), bf16[8,72,1152]{2,1,0:T(8,128)(2,1)S(1)}, u32[]{:S(2)}, u32[]{:S(2)}) async-start(bf16[8,72,1152]{2,1,0:T(8,128)(2,1)} %broadcast_in_dim.6), calls=%async_computation | async-start | bytes 2654208 | tf_op jit(solution)/shard_map/all_to_all | solution.py:363
  22.1 4.3 %copy-start.7 = (bf16[16,1152]{1,0:T(8,128)(2,1)}, bf16[16,1152]{1,0:T(8,128)(2,1)S(1)}, u32[]{:S(2)}) copy-start(bf16[16,1152]{1,0:T(8,128)(2,1)S(1)} %fusion.1.spread_ref) | copy-start | bytes 110596
  22.1 1.7 copy-start.2
  23.7 13.5 %copy-start.15 = (bf16[32,1152]{1,0:T(8,128)(2,1)S(1)}, bf16[32,1152]{1,0:T(8,128)(2,1)}, u32[]{:S(2)}) copy-start(bf16[32,1152]{1,0:T(8,128)(2,1)} %rows_ref.1) | copy-start | bytes 221188
  26.3 0.8 copy-start.5
  32.3 4.9 %collective-permute-start = (bf16[576,1152]{1,0:T(8,128)(2,1)S(1)}, bf16[576,1152]{1,0:T(8,128)(2,1)S(1)}, u32[]{:S(2)}, u32[]{:S(2)}) collective-permute-start(bf16[576,1152]{1,0:T(8,128)(2,1)S(1)} %bitcast.14), channel_id=1, source_target_pairs={{0,1},{1,0},{2,3},{3,2},{4,5},{5,4},{6,7},{7,6},{8,9},{9,8},{10,11... | collective-permute-start | bytes 3981320 | tf_op jit(solution)/shard_map/ppermute | solution.py:25
  37.3 18.9 %copy-start.26 = (s32[32]{0:T(128)S(1)}, s32[32]{0:T(128)}, u32[]{:S(2)}) copy-start(s32[32]{0:T(128)} %param.15) | copy-start | bytes 388
  38.3 0.7 copy-start.11
  39.7 35.6 %all-to-all-start.1 = ((bf16[4,32,1152]{2,1,0:T(8,128)(2,1)}), bf16[4,32,1152]{2,1,0:T(8,128)(2,1)S(1)}, u32[]{:S(2)}, u32[]{:S(2)}) async-start(bf16[4,32,1152]{2,1,0:T(8,128)(2,1)} %broadcast_in_dim.7), calls=%async_computation.1 | async-start | bytes 589824 | tf_op jit(solution)/shard_map/all_to_all | solution.py:363
  56.4 1.7 copy-start
  59.1 0.6 copy-start.9
  76.5 36.6 %all-to-all-start.2 = ((bf16[16,32,1280]{2,1,0:T(8,128)(2,1)}), bf16[16,32,1280]{2,1,0:T(8,128)(2,1)}, u32[]{:S(2)}, u32[]{:S(2)}) async-start(bf16[16,32,1280]{2,1,0:T(8,128)(2,1)} %broadcast_in_dim.8), calls=%async_computation.2 | async-start | bytes 2621440 | tf_op jit(solution)/shard_map/all_to_all | solution.py:363
  83.6 25.1 %collective-permute-start.1 = (bf16[128,1152]{1,0:T(8,128)(2,1)S(1)}, bf16[128,1152]{1,0:T(8,128)(2,1)S(1)}, u32[]{:S(2)}, u32[]{:S(2)}) collective-permute-start(bf16[128,1152]{1,0:T(8,128)(2,1)S(1)} %bitcast.20), channel_id=1, source_target_pairs={{32,0},{64,32},{96,64},{128,96},{160,128},{192,160},{224,192},{256... | collective-permute-start | bytes 884744 | tf_op jit(solution)/shard_map/ppermute | solution.py:21
  90.0 19.3 %collective-permute-start.2 = (bf16[128,1152]{1,0:T(8,128)(2,1)S(1)}, bf16[128,1152]{1,0:T(8,128)(2,1)S(1)}, u32[]{:S(2)}, u32[]{:S(2)}) collective-permute-start(bf16[128,1152]{1,0:T(8,128)(2,1)S(1)} %bitcast.21), channel_id=1, source_target_pairs={{480,0},{0,32},{32,64},{64,96},{96,128},{128,160},{160,192},{192,2... | collective-permute-start | bytes 884744 | tf_op jit(solution)/shard_map/ppermute | solution.py:21
  92.0 10.8 %collective-permute-start.3 = (bf16[64,1152]{1,0:T(8,128)(2,1)S(1)}, bf16[64,1152]{1,0:T(8,128)(2,1)S(1)}, u32[]{:S(2)}, u32[]{:S(2)}) collective-permute-start(bf16[64,1152]{1,0:T(8,128)(2,1)S(1)} %get-tuple-element.63), channel_id=1, source_target_pairs={{64,0},{96,32},{128,64},{160,96},{192,128},{224,160},{256,192},{28... | collective-permute-start | bytes 442376 | tf_op jit(solution)/shard_map/ppermute | solution.py:21
  96.2 11.3 %collective-permute-start.4 = (bf16[64,1152]{1,0:T(8,128)(2,1)S(1)}, bf16[64,1152]{1,0:T(8,128)(2,1)S(1)}, u32[]{:S(2)}, u32[]{:S(2)}) collective-permute-start(bf16[64,1152]{1,0:T(8,128)(2,1)S(1)} %get-tuple-element.62), channel_id=1, source_target_pairs={{448,0},{480,32},{0,64},{32,96},{64,128},{96,160},{128,192},{160,2... | collective-permute-start | bytes 442376 | tf_op jit(solution)/shard_map/ppermute | solution.py:21
  103.3 0.7 copy-start.20
  108.0 0.7 copy-start.22
  109.8 0.7 copy-start.16
  113.1 9.5 %collective-permute-start.5 = (bf16[512,1280]{1,0:T(8,128)(2,1)}, bf16[512,1280]{1,0:T(8,128)(2,1)S(1)}, u32[]{:S(2)}, u32[]{:S(2)}) collective-permute-start(bf16[512,1280]{1,0:T(8,128)(2,1)} %bitcast.7.refs_6_), channel_id=1, source_target_pairs={{0,1},{1,0},{2,3},{3,2},{4,5},{5,4},{6,7},{7,6},{8,9},{9,8},{10,11... | collective-permute-start | bytes 3932168 | tf_op jit(solution)/shard_map/ppermute | solution.py:25
  115.0 1.0 copy-start.17
  116.0 0.9 copy-start.21
  116.9 0.9 copy-start.23
  125.3 0.9 copy-start.18
  125.3 0.9 copy-start.19
  125.3 0.9 copy-start.24
  125.4 0.9 copy-start.25
  126.3 4.9 %collective-permute-start.6 = (bf16[512,1152]{1,0:T(8,128)(2,1)S(1)}, bf16[512,1152]{1,0:T(8,128)(2,1)S(1)}, u32[]{:S(2)}, u32[]{:S(2)}) collective-permute-start(bf16[512,1152]{1,0:T(8,128)(2,1)S(1)} %shard_map.118), channel_id=1, source_target_pairs={{0,1},{1,0},{2,3},{3,2},{4,5},{5,4},{6,7},{7,6},{8,9},{9,8},{10,11... | collective-permute-start | bytes 3538952 | tf_op jit(solution)/shard_map/ppermute | solution.py:25
  131.3 1.0 copy-start.4
  132.3 29.4 %all-to-all-start.3 = ((bf16[16,32,1152]{2,1,0:T(8,128)(2,1)}), bf16[16,32,1152]{2,1,0:T(8,128)(2,1)}, u32[]{:S(2)}, u32[]{:S(2)}) async-start(bf16[16,32,1152]{2,1,0:T(8,128)(2,1)} %bitcast.19), calls=%async_computation.3 | async-start | bytes 2359296 | tf_op jit(solution)/shard_map/all_to_all | solution.py:437
  139.6 21.3 %collective-permute-start.7 = (bf16[128,1152]{1,0:T(8,128)(2,1)}, bf16[128,1152]{1,0:T(8,128)(2,1)S(1)}, u32[]{:S(2)}, u32[]{:S(2)}) collective-permute-start(bf16[128,1152]{1,0:T(8,128)(2,1)} %copy-done.19), channel_id=1, source_target_pairs={{480,0},{0,32},{32,64},{64,96},{96,128},{128,160},{160,192},{192,2... | collective-permute-start | bytes 884744 | tf_op jit(solution)/shard_map/ppermute | solution.py:21
  143.3 17.6 %collective-permute-start.8 = (bf16[128,1152]{1,0:T(8,128)(2,1)}, bf16[128,1152]{1,0:T(8,128)(2,1)S(1)}, u32[]{:S(2)}, u32[]{:S(2)}) collective-permute-start(bf16[128,1152]{1,0:T(8,128)(2,1)} %copy-done.18), channel_id=1, source_target_pairs={{32,0},{64,32},{96,64},{128,96},{160,128},{192,160},{224,192},{256... | collective-permute-start | bytes 884744 | tf_op jit(solution)/shard_map/ppermute | solution.py:21
  146.6 11.9 %collective-permute-start.9 = (bf16[64,1152]{1,0:T(8,128)(2,1)}, bf16[64,1152]{1,0:T(8,128)(2,1)S(1)}, u32[]{:S(2)}, u32[]{:S(2)}) collective-permute-start(bf16[64,1152]{1,0:T(8,128)(2,1)} %copy-done.25), channel_id=1, source_target_pairs={{448,0},{480,32},{0,64},{32,96},{64,128},{96,160},{128,192},{160,2... | collective-permute-start | bytes 442376 | tf_op jit(solution)/shard_map/ppermute | solution.py:21
  148.6 12.3 %collective-permute-start.10 = (bf16[64,1152]{1,0:T(8,128)(2,1)}, bf16[64,1152]{1,0:T(8,128)(2,1)S(1)}, u32[]{:S(2)}, u32[]{:S(2)}) collective-permute-start(bf16[64,1152]{1,0:T(8,128)(2,1)} %copy-done.24), channel_id=1, source_target_pairs={{64,0},{96,32},{128,64},{160,96},{192,128},{224,160},{256,192},{28... | collective-permute-start | bytes 442376 | tf_op jit(solution)/shard_map/ppermute | solution.py:21
  161.8 22.4 %all-to-all-start.4 = ((bf16[4,32,1152]{2,1,0:T(8,128)(2,1)}), bf16[4,32,1152]{2,1,0:T(8,128)(2,1)S(1)}, u32[]{:S(2)}, u32[]{:S(2)}) async-start(bf16[4,32,1152]{2,1,0:T(8,128)(2,1)} %bitcast.13), calls=%async_computation.4 | async-start | bytes 589824 | tf_op jit(solution)/shard_map/all_to_all | solution.py:440
  165.4 1.7 copy-start.1
  167.2 0.9 copy-start.10
  168.1 2.2 %copy-start.3 = (bf16[32,32,1152]{2,1,0:T(8,128)(2,1)S(1)}, bf16[32,32,1152]{2,1,0:T(8,128)(2,1)}, u32[]{:S(2)}) copy-start(bf16[32,32,1152]{2,1,0:T(8,128)(2,1)} %param.10) | copy-start | bytes 7077892
  168.1 2.2 %copy-start.6 = (f32[1024,16]{1,0:T(8,128)S(1)}, f32[1024,16]{1,0:T(8,128)}, u32[]{:S(2)}) copy-start(f32[1024,16]{1,0:T(8,128)} %copy-done.5) | copy-start | bytes 196612
  168.1 2.2 %copy-start.8 = (bf16[16,1152]{1,0:T(8,128)(2,1)S(1)}, bf16[16,1152]{1,0:T(8,128)(2,1)}, u32[]{:S(2)}) copy-start(bf16[16,1152]{1,0:T(8,128)(2,1)} %copy-done.7) | copy-start | bytes 110596
  168.1 2.2 %copy-start.14 = (bf16[1152,16]{0,1:T(8,128)(2,1)S(1)}, bf16[1152,16]{0,1:T(8,128)(2,1)}, u32[]{:S(2)}) copy-start(bf16[1152,16]{0,1:T(8,128)(2,1)} %param.11) | copy-start | bytes 110596
  170.3 13.8 %copy-start.12 = (f32[32,1152]{1,0:T(8,128)S(1)}, f32[32,1152]{1,0:T(8,128)}, u32[]{:S(2)}) copy-start(f32[32,1152]{1,0:T(8,128)} %copy-done.11) | copy-start | bytes 442372
Sparse Core Ops, SparseCore 0:
  10.2 46.1 all-gather.1
